TPU v7x, 32 devices: a whole 2x2x4 slice. The times are simulated.
32 devices in a mesh: slab: 2 (over y), brick: 16 (over z, x, core).
Axes of the slice: x: 2, y: 2, z: 4, core: 2. Of those that a mesh axis runs over, the one named last changes fastest.
Arguments:
- inputs: bfloat16 [64, 8, 32, 128], P('brick', None, 'slab'), may hold values from -6 to 6
- pre_first: bfloat16 [64, 8, 32, 128], P('brick', None, 'slab'), may hold values from -8 to 8
- occupancy: int32 [64, 8, 32], P('brick', None, 'slab'), may hold values 0 or 1
- grad_out: bfloat16 [64, 8, 32, 128], P('brick', None, 'slab'), may hold values from -6 to 6
- w_first: bfloat16 [27, 128, 128], replicated, may hold values from -0.109375 to 0.109375
- w_second: bfloat16 [27, 128, 128], replicated, may hold values from -0.109375 to 0.109375
Outputs:
- grad_in: bfloat16 [64, 8, 32, 128], P('brick', None, 'slab')
- grad_first: bfloat16 [27, 128, 128], replicated
- grad_second: bfloat16 [27, 128, 128], replicated
All inputs are finite; a program needn't handle non-finite values. No bound on the sum of `occupancy` on one device may be relied on, other than what follows from the above.
Results may differ from a plain program's by a relative error of at most 0.0053.
Values may be sent and summed in bfloat16 or wider, within the bound.
No kernel may reach another device: no remote copies, remote signals or barrier semaphores. Data moves between devices by JAX's collectives and lax.ppermute only.
A program may use at most 64 MiB of HBM per device.

v0:
```python
import jax
import jax.numpy as jnp
from jax import lax
from jax.sharding import PartitionSpec as P


def with_halo(shard, sides, width):
    for axis, dim in sides:
        size, length = (lax.axis_size(axis), shard.shape[dim])
        up = [(i, (i + 1) % size) for i in range(size)]
        down = [(j, i) for i, j in up]
        last = lax.slice_in_dim(shard, length - width, length, axis=dim)
        initial = lax.slice_in_dim(shard, 0, width, axis=dim)
        before = lax.ppermute(last, axis, up)
        after = lax.ppermute(initial, axis, down)
        shard = jnp.concatenate([before, shard, after], axis=dim)
    return shard


def extend(field):
    padded = with_halo(field, (("slab", 2), ("brick", 0)), 1)
    return jnp.concatenate([padded[:, -1:], padded, padded[:, :1]], axis=1)


def columns(field):
    size_x, size_y, size_z, chans = field.shape
    padded = extend(field)
    pieces = []
    for a in (-1, 0, 1):
        for b in (-1, 0, 1):
            for c in (-1, 0, 1):
                pieces.append(
                    padded[1 - a : 1 - a + size_x, 1 - b : 1 - b + size_y, 1 - c : 1 - c + size_z]
                )
    stacked = jnp.concatenate(pieces, axis=-1)
    return stacked.reshape(size_x * size_y * size_z, 27 * chans)


def stacked_kernel(kernel):
    chans = kernel.shape[1]
    return jnp.transpose(kernel, (0, 2, 1)).reshape(27 * chans, chans)


def local_term(left, cols, scale):
    chans = left.shape[-1]
    flat_left = left.reshape(-1, chans)
    term = lax.dot_general(
        flat_left, cols, (((0,), (0,)), ((), ())), preferred_element_type=jnp.float32
    )
    term = term.reshape(chans, 27, chans).transpose(1, 0, 2)
    return term * scale


def reduce_kernel(term):
    return lax.psum(term, ("slab", "brick")).astype(jnp.bfloat16)


def per_device(inputs, pre_first, occupancy, grad_out, w_first, w_second):
    size_x, size_y, size_z, chans = inputs.shape
    cells_all = size_x * lax.axis_size("brick") * size_y * size_z * lax.axis_size("slab")
    scale = 10.0 / jnp.sqrt(jnp.float32(cells_all))
    occ = occupancy.astype(jnp.float32)[..., None]
    pre = pre_first.astype(jnp.float32)
    sig = jax.nn.sigmoid(pre)
    act = (pre * sig * occ).astype(jnp.bfloat16)
    grad_second_pre = (grad_out.astype(jnp.float32) * occ).astype(jnp.bfloat16)
    cols_second = columns(grad_second_pre)
    grad_act = jnp.dot(cols_second, stacked_kernel(w_second), preferred_element_type=jnp.float32)
    grad_act = grad_act.reshape(inputs.shape)
    second_term = local_term(act, cols_second, scale)
    grad_second = reduce_kernel(second_term)
    grad_first_pre = (grad_act * occ * sig * (1.0 + pre * (1.0 - sig))).astype(jnp.bfloat16)
    cols_first = columns(grad_first_pre)
    back = jnp.dot(cols_first, stacked_kernel(w_first), preferred_element_type=jnp.float32)
    grad_in = (grad_out.astype(jnp.float32) + back.reshape(inputs.shape)).astype(jnp.bfloat16)
    first_term = local_term(inputs, cols_first, scale)
    grad_first = reduce_kernel(first_term)
    return (grad_in, grad_first, grad_second)


def solution(mesh):
    in_specs = (
        P("brick", None, "slab", None),
        P("brick", None, "slab", None),
        P("brick", None, "slab"),
        P("brick", None, "slab", None),
        P(),
        P(),
    )
    out_specs = (P("brick", None, "slab", None), P(), P())
    return jax.shard_map(
        per_device, mesh=mesh, in_specs=in_specs, out_specs=out_specs, check_vma=False
    )
```

profile of v0, /device:TPU:0, one launch (start us, length us, event | category | flops | bytes accessed | tf_op | source)
XLA Modules:
  0.0 129.4 jit_solution(15316858743661446116)
XLA Ops:
  0.6 0.8 convert_element_type.29
  1.4 1.1 fusion.15
  2.6 3.0 %collective-permute-start = (bf16[4,8,1,128]{3,2,1,0:T(2,128)(2,1)S(1)}, bf16[4,8,1,128]{3,2,1,0:T(2,128)(2,1)S(1)}, u32[]{:S(2)}, u32[]{:S(2)}) collective-permute-start(bf16[4,8,1,128]{3,2,1,0:T(2,128)(2,1)S(1)} %get-tuple-element.15), channel_id=1, source_target_pairs={{0,16},{16,0},{1,17},{17,1},{2,18},{18,2},{3,19},{19,3},{4,20},{20... | collective-permute-start | bytes 24584 | tf_op jit(solution)/shard_map/ppermute | solution.py:14
  5.7 1.6 %collective-permute-done = bf16[4,8,1,128]{3,2,1,0:T(2,128)(2,1)S(1)} collective-permute-done((bf16[4,8,1,128]{3,2,1,0:T(2,128)(2,1)S(1)}, bf16[4,8,1,128]{3,2,1,0:T(2,128)(2,1)S(1)}, u32[]{:S(2)}, u32[]{:S(2)}) %collective-permute-start) | collective-permute-done | bytes 8224 | tf_op jit(solution)/shard_map/ppermute | solution.py:14
  7.3 2.0 %collective-permute-done.1 = bf16[4,8,1,128]{3,2,1,0:T(2,128)(2,1)S(1)} collective-permute-done((bf16[4,8,1,128]{3,2,1,0:T(2,128)(2,1)S(1)}, bf16[4,8,1,128]{3,2,1,0:T(2,128)(2,1)S(1)}, u32[]{:S(2)}, u32[]{:S(2)}) %collective-permute-start.1) | collective-permute-done | bytes 8224 | tf_op jit(solution)/shard_map/ppermute | solution.py:15
  9.4 4.4 %collective-permute-start.3 = (bf16[1,8,18,128]{3,2,1,0:T(8,128)(2,1)S(1)}, bf16[1,8,18,128]{3,2,1,0:T(8,128)(2,1)S(1)}, u32[]{:S(2)}, u32[]{:S(2)}) collective-permute-start(bf16[1,8,18,128]{3,2,1,0:T(8,128)(2,1)S(1)} %get-tuple-element.12), channel_id=1, source_target_pairs={{1,0},{2,1},{3,2},{4,3},{5,4},{6,5},{7,6},{8,7},{9,8},{10,9},{11,1... | collective-permute-start | bytes 110600 | tf_op jit(solution)/shard_map/ppermute | solution.py:15
  13.9 1.9 %copy.12 = bf16[27,128,128]{1,2,0:T(8,128)(2,1)S(1)} copy(bf16[27,128,128]{2,1,0:T(8,128)(2,1)} %param.11) | data formatting | bytes 1769472 | tf_op args[5]
  15.8 0.1 fusion.8
  16.1 0.2 maximum_maximum_fusion
  16.4 0.1 fusion.7
  17.9 1.8 %copy-done.1 = bf16[4,8,16,3456]{3,2,1,0:T(8,128)(2,1)} copy-done((bf16[4,8,16,3456]{3,2,1,0:T(8,128)(2,1)}, bf16[4,8,16,3456]{3,2,1,0:T(8,128)(2,1)S(1)}, u32[]{:S(2)}) %copy-start.1) | copy-done | bytes 3538968
  19.7 1.1 fusion.3
  20.8 0.2 collective-permute-start.4
  21.1 1.9 %collective-permute-start.5 = (bf16[4,8,1,128]{3,2,1,0:T(2,128)(2,1)S(1)}, bf16[4,8,1,128]{3,2,1,0:T(2,128)(2,1)S(1)}, u32[]{:S(2)}, u32[]{:S(2)}) collective-permute-start(bf16[4,8,1,128]{3,2,1,0:T(2,128)(2,1)S(1)} %get-tuple-element.14), channel_id=1, source_target_pairs={{16,0},{0,16},{17,1},{1,17},{18,2},{2,18},{19,3},{3,19},{20,4},{4,... | collective-permute-start | bytes 24584 | tf_op jit(solution)/shard_map/ppermute | solution.py:15
  22.9 1.3 %copy.13 = bf16[27,128,128]{1,2,0:T(8,128)(2,1)S(1)} copy(bf16[27,128,128]{2,1,0:T(8,128)(2,1)S(1)} %copy-done.2) | data formatting | bytes 1769472 | tf_op args[4]
  24.2 5.8 %copy.15 = bf16[3456,512]{1,0:T(8,128)(2,1)} copy(bf16[3456,512]{0,1:T(8,128)(2,1)} %bitcast.43) | data formatting | bytes 7077888 | tf_op jit(solution)/shard_map/dot_general | solution.py:47
  30.1 4.4 %collective-permute-start.7 = (bf16[1,8,18,128]{3,2,1,0:T(8,128)(2,1)S(1)}, bf16[1,8,18,128]{3,2,1,0:T(8,128)(2,1)S(1)}, u32[]{:S(2)}, u32[]{:S(2)}) collective-permute-start(bf16[1,8,18,128]{3,2,1,0:T(8,128)(2,1)S(1)} %get-tuple-element.8), channel_id=1, source_target_pairs={{1,0},{2,1},{3,2},{4,3},{5,4},{6,5},{7,6},{8,7},{9,8},{10,9},{11,1... | collective-permute-start | bytes 110600 | tf_op jit(solution)/shard_map/ppermute | solution.py:15
  34.5 4.3 %multiply_bitcast_fusion = f32[27,128,128]{2,1,0:T(8,128)} fusion(bf16[512,128,1]{1,0,2:T(8,128)(2,1)S(1)} %bitcast.47, bf16[27,128,512]{2,1,0:T(8,128)(2,1)} %bitcast.41), kind=kOutput, calls=%fused_computation.2 | convolution fusion | flops 453427200 | bytes 5439488 | tf_op jit(solution)/shard_map/dot_general | solution.py:47
  39.2 0.2 maximum_maximum_fusion.1
  39.5 0.1 fusion.5
  41.0 1.8 %fusion.4 = bf16[4,8,16,128]{3,2,1,0:T(8,128)(2,1)} fusion(bf16[4,8,16,3456]{3,2,1,0:T(8,128)(2,1)S(1)} %slice_dynamic-update-slice_fusion, bf16[3456,128,1,1]{1,0,3,2:T(8,128)(2,1)S(1)} %bitcast.45, bf16[4,8,16,128]{3,2,1,0:T(8,128)(2,1)S(1)} %copy-done.4), kind=kOutput, calls=%fused_computation.8 | convolution fusion | flops 453181440 | bytes 4685824 | tf_op jit(solution)/shard_map/dot_general | solution.py:74
  42.7 2.4 %fusion = f32[3456,128]{1,0:T(8,128)} fusion(bf16[4,8,16,3456]{3,2,1,0:T(8,128)(2,1)S(1)} %slice_dynamic-update-slice_fusion, bf16[4,8,16,128]{3,2,1,0:T(8,128)(2,1)S(1)} %copy-done), kind=kOutput, calls=%fused_computation.1 | convolution fusion | flops 453427200 | bytes 5439488 | tf_op jit(solution)/shard_map/dot_general | solution.py:47
  45.1 2.2 %copy.14 = f32[128,27,128]{2,0,1:T(8,128)S(1)} copy(f32[128,27,128]{0,2,1:T(8,128)} %bitcast.44) | data formatting | bytes 3538944 | tf_op jit(solution)/shard_map/mul | solution.py:51
  47.3 82.1 %all-reduce.2 = (bf16[27,128,128]{2,1,0:T(8,128)(2,1)}, bf16[27,128,128]{2,1,0:T(8,128)(2,1)}) all-reduce(f32[27,128,128]{2,1,0:T(8,128)S(1)} %bitcast.42, f32[27,128,128]{2,1,0:T(8,128)} %multiply_bitcast_fusion), channel_id=1, replica_groups=mesh['slab'=2,'brick'=16] {'slab','brick'}, use_global_device_ids=true, to_apply=%region_0.0 | all-reduce | flops 884736 | bytes 5308416 | tf_op jit(solution)/shard_map/psum | solution.py:55
  (77 shorter events, 3.4 us)
Async XLA Ops:
  0.6 42.1 %copy-start = (bf16[4,8,16,128]{3,2,1,0:T(8,128)(2,1)S(1)}, bf16[4,8,16,128]{3,2,1,0:T(8,128)(2,1)}, u32[]{:S(2)}) copy-start(bf16[4,8,16,128]{3,2,1,0:T(8,128)(2,1)} %param.6) | copy-start | bytes 393220
  2.6 4.8 %collective-permute-start = (bf16[4,8,1,128]{3,2,1,0:T(2,128)(2,1)S(1)}, bf16[4,8,1,128]{3,2,1,0:T(2,128)(2,1)S(1)}, u32[]{:S(2)}, u32[]{:S(2)}) collective-permute-start(bf16[4,8,1,128]{3,2,1,0:T(2,128)(2,1)S(1)} %get-tuple-element.15), channel_id=1, source_target_pairs={{0,16},{16,0},{1,17},{17,1},{2,18},{18,2},{3,19},{19,3},{4,20},{20... | collective-permute-start | bytes 24584 | tf_op jit(solution)/shard_map/ppermute | solution.py:14
  5.6 3.7 %collective-permute-start.1 = (bf16[4,8,1,128]{3,2,1,0:T(2,128)(2,1)S(1)}, bf16[4,8,1,128]{3,2,1,0:T(2,128)(2,1)S(1)}, u32[]{:S(2)}, u32[]{:S(2)}) collective-permute-start(bf16[4,8,1,128]{3,2,1,0:T(2,128)(2,1)S(1)} %get-tuple-element.16), channel_id=1, source_target_pairs={{16,0},{0,16},{17,1},{1,17},{18,2},{2,18},{19,3},{3,19},{20,4},{4,... | collective-permute-start | bytes 24584 | tf_op jit(solution)/shard_map/ppermute | solution.py:15
  9.4 6.4 %collective-permute-start.2 = (bf16[1,8,18,128]{3,2,1,0:T(8,128)(2,1)S(1)}, bf16[1,8,18,128]{3,2,1,0:T(8,128)(2,1)S(1)}, u32[]{:S(2)}, u32[]{:S(2)}) collective-permute-start(bf16[1,8,18,128]{3,2,1,0:T(8,128)(2,1)S(1)} %get-tuple-element.11), channel_id=1, source_target_pairs={{0,1},{1,2},{2,3},{3,4},{4,5},{5,6},{6,7},{7,8},{8,9},{9,10},{10,1... | collective-permute-start | bytes 110600 | tf_op jit(solution)/shard_map/ppermute | solution.py:14
  9.4 6.3 %collective-permute-start.3 = (bf16[1,8,18,128]{3,2,1,0:T(8,128)(2,1)S(1)}, bf16[1,8,18,128]{3,2,1,0:T(8,128)(2,1)S(1)}, u32[]{:S(2)}, u32[]{:S(2)}) collective-permute-start(bf16[1,8,18,128]{3,2,1,0:T(8,128)(2,1)S(1)} %get-tuple-element.12), channel_id=1, source_target_pairs={{1,0},{2,1},{3,2},{4,3},{5,4},{6,5},{7,6},{8,7},{9,8},{10,9},{11,1... | collective-permute-start | bytes 110600 | tf_op jit(solution)/shard_map/ppermute | solution.py:15
  16.3 3.4 %copy-start.3 = (bf16[4,8,16,128]{3,2,1,0:T(8,128)(2,1)S(1)}, bf16[4,8,16,128]{3,2,1,0:T(8,128)(2,1)}, u32[]{:S(2)}) copy-start(bf16[4,8,16,128]{3,2,1,0:T(8,128)(2,1)} %param.7) | copy-start | bytes 393220
  17.7 5.2 %copy-start.2 = (bf16[27,128,128]{2,1,0:T(8,128)(2,1)S(1)}, bf16[27,128,128]{2,1,0:T(8,128)(2,1)}, u32[]{:S(2)}) copy-start(bf16[27,128,128]{2,1,0:T(8,128)(2,1)} %param.10) | copy-start | bytes 2654212
  17.9 1.8 %copy-start.1 = (bf16[4,8,16,3456]{3,2,1,0:T(8,128)(2,1)}, bf16[4,8,16,3456]{3,2,1,0:T(8,128)(2,1)S(1)}, u32[]{:S(2)}) copy-start(bf16[4,8,16,3456]{3,2,1,0:T(8,128)(2,1)S(1)} %slice_dynamic-update-slice_fusion.24) | copy-start | bytes 10616836
  20.8 9.2 %collective-permute-start.4 = (bf16[4,8,1,128]{3,2,1,0:T(2,128)(2,1)S(1)}, bf16[4,8,1,128]{3,2,1,0:T(2,128)(2,1)S(1)}, u32[]{:S(2)}, u32[]{:S(2)}) collective-permute-start(bf16[4,8,1,128]{3,2,1,0:T(2,128)(2,1)S(1)} %get-tuple-element.13), channel_id=1, source_target_pairs={{0,16},{16,0},{1,17},{17,1},{2,18},{18,2},{3,19},{19,3},{4,20},{20... | collective-permute-start | bytes 24584 | tf_op jit(solution)/shard_map/ppermute | solution.py:14
  21.1 8.9 %collective-permute-start.5 = (bf16[4,8,1,128]{3,2,1,0:T(2,128)(2,1)S(1)}, bf16[4,8,1,128]{3,2,1,0:T(2,128)(2,1)S(1)}, u32[]{:S(2)}, u32[]{:S(2)}) collective-permute-start(bf16[4,8,1,128]{3,2,1,0:T(2,128)(2,1)S(1)} %get-tuple-element.14), channel_id=1, source_target_pairs={{16,0},{0,16},{17,1},{1,17},{18,2},{2,18},{19,3},{3,19},{20,4},{4,... | collective-permute-start | bytes 24584 | tf_op jit(solution)/shard_map/ppermute | solution.py:15
  30.0 8.8 %collective-permute-start.6 = (bf16[1,8,18,128]{3,2,1,0:T(8,128)(2,1)S(1)}, bf16[1,8,18,128]{3,2,1,0:T(8,128)(2,1)S(1)}, u32[]{:S(2)}, u32[]{:S(2)}) collective-permute-start(bf16[1,8,18,128]{3,2,1,0:T(8,128)(2,1)S(1)} %get-tuple-element.7), channel_id=1, source_target_pairs={{0,1},{1,2},{2,3},{3,4},{4,5},{5,6},{6,7},{7,8},{8,9},{9,10},{10,1... | collective-permute-start | bytes 110600 | tf_op jit(solution)/shard_map/ppermute | solution.py:14
  30.1 8.8 %collective-permute-start.7 = (bf16[1,8,18,128]{3,2,1,0:T(8,128)(2,1)S(1)}, bf16[1,8,18,128]{3,2,1,0:T(8,128)(2,1)S(1)}, u32[]{:S(2)}, u32[]{:S(2)}) collective-permute-start(bf16[1,8,18,128]{3,2,1,0:T(8,128)(2,1)S(1)} %get-tuple-element.8), channel_id=1, source_target_pairs={{1,0},{2,1},{3,2},{4,3},{5,4},{6,5},{7,6},{8,7},{9,8},{10,9},{11,1... | collective-permute-start | bytes 110600 | tf_op jit(solution)/shard_map/ppermute | solution.py:15
  39.4 1.6 %copy-start.4 = (bf16[4,8,16,128]{3,2,1,0:T(8,128)(2,1)S(1)}, bf16[4,8,16,128]{3,2,1,0:T(8,128)(2,1)}, u32[]{:S(2)}) copy-start(bf16[4,8,16,128]{3,2,1,0:T(8,128)(2,1)} %param.9) | copy-start | bytes 393220
where the time goes:
time: 130 us; the launch traced here: 129 us
  blocking collectives  82.1 us (63%)
  local copies, waits for them, and re-layouts  15.6 us (12%)
  starting transfers between devices  14.2 us (11%)
  matrix products  9.57 us (7%)
  waiting for transfers between devices  3.68 us (3%)
  other arithmetic  3.13 us (2%)
    psum x1, blocking collectives, reduce_kernel(): return lax.psum(term, ('slab', 'brick')).astype(jnp.bfloat16)  82.1 us
    ppermute x4, starting transfers between devices, with_halo(): after = lax.ppermute(initial, axis, down)  10.8 us
    unnamed x60, local copies, waits for them, and re-layouts  7.54 us
    dot_general x2, matrix products, local_term(): lax.dot_general(flat_left, cols, (((0,), (0,)), ((), ())), preferred_elem...  6.73 us
    dot_general x1, local copies, waits for them, and re-layouts, local_term(): lax.dot_general(flat_left, cols, (((0,), (0,)), ((), ())), preferred_elem...  5.77 us
    ppermute x4, starting transfers between devices, with_halo(): before = lax.ppermute(last, axis, up)  3.39 us
  transfers between devices with their start and end apart: 8, of which 2 were waited for; matrix products, arithmetic and copies ran while one was open for 10% of the time, Pallas kernels for 0%

commit v1 on v0

v1 whole, which is shorter than its diff:
```python
import functools

import jax
import jax.numpy as jnp
from jax import lax
from jax.experimental import pallas as pl
from jax.experimental.pallas import tpu as pltpu
from jax.sharding import PartitionSpec as P

AXES = ("slab", "brick")
F32 = jnp.float32
BF16 = jnp.bfloat16
OFFSETS = [(a, b, c) for a in (-1, 0, 1) for b in (-1, 0, 1) for c in (-1, 0, 1)]
EMPTY = -9984.0
VMEM_BYTES = 48 * 1024 * 1024


def send(value, slab_from, brick_from):
    slabs, bricks = lax.axis_size("slab"), lax.axis_size("brick")
    pairs = [
        (slab_from(s) * bricks + brick_from(b), s * bricks + b)
        for s in range(slabs)
        for b in range(bricks)
    ]
    return lax.ppermute(value, AXES, pairs)


def same(index):
    return index


def over_slabs(value, brick_from=same):
    slabs = lax.axis_size("slab")
    pieces = []
    for r in range(slabs):
        if r == 0 and brick_from is same:
            pieces.append(value)
        else:
            pieces.append(send(value, lambda s, r=r: (s + r) % slabs, brick_from))
    return pieces


def partner(value, bit):
    return send(value, same, lambda b: b ^ bit)


def shifted(field_ref, a, b, c, start, planes, nz):
    ny = field_ref.shape[2] - 2
    block = field_ref[c + 1, pl.ds(start - a, planes), pl.ds(1 - b, ny), pl.ds(0, nz), :]
    return block.reshape(planes * ny * nz, block.shape[-1])


def put_planes(field_ref, start, planes):
    n, ny, nz, chans = planes.shape
    flat = planes.reshape(n * ny, nz, chans)
    for c in (-1, 0, 1):
        rolled = flat if c == 0 else pltpu.roll(flat, c % nz, 1)
        rolled = rolled.astype(BF16).reshape(n, ny, nz, chans)
        field_ref[c + 1, pl.ds(start, n), pl.ds(1, ny)] = rolled
        field_ref[c + 1, pl.ds(start, n), pl.ds(0, 1)] = rolled[:, ny - 1 :]
        field_ref[c + 1, pl.ds(start, n), pl.ds(ny + 1, 1)] = rolled[:, :1]


def joined(refs, start, count):
    return jnp.concatenate([r[start : start + count].astype(F32) for r in refs], axis=2)


def fill_second(field_ref, own, other, rim_own, rim_other, me):
    width = own[0].shape[0] // 2
    for i in range(width):
        put_planes(field_ref, 2 + width * me + i, joined(own, i, 1))
        put_planes(field_ref, 2 + width * (1 - me) + i, joined(other, i, 1))
    for i in range(2):
        put_planes(field_ref, (2 + 2 * width) * me + i, joined(rim_own, i, 1))
        put_planes(field_ref, (2 + 2 * width) * (1 - me) + i, joined(rim_other, i, 1))


def sigmoid(v):
    return 1.0 / (1.0 + jnp.exp(-v))


def kernel_terms(left_ref, field_ref, start, planes, nz, scratch_ref, index_ref, per, scale):
    chans = left_ref.shape[-1]
    for j in range(per):
        k = jnp.minimum(index_ref[1] * per + j, 26)
        a, b, c = k // 9 - 1, (k // 3) % 3 - 1, k % 3 - 1
        cols = shifted(field_ref, a, b, c, start, planes, nz)
        term = lax.dot_general(
            left_ref[...], cols, (((0,), (0,)), ((), ())), preferred_element_type=F32
        )
        scratch_ref[pl.ds(j * chans, chans), :] = term * scale


def put_chunks(scratch_ref, keep_ref, sent_ref, me, rows):
    for r in range(2 * keep_ref.shape[0]):
        chunk = scratch_ref[pl.ds(pl.multiple_of((me ^ r) * rows, 8), rows), :]
        if r % 2 == 0:
            keep_ref[r // 2] = chunk
        else:
            sent_ref[r // 2] = chunk.astype(BF16)


def split_refs(refs, counts):
    out, at = [], 0
    for n in counts:
        out.append(list(refs[at : at + n]))
        at += n
    return out + [list(refs[at:])]


def second_kernel(slabs, per, scale, index_ref, *refs):
    own, other, rim_own, rim_other, rest = split_refs(refs, [slabs] * 4)
    keep_ref, sent_ref, field_ref, act_ref, scratch_ref = rest
    me = index_ref[0]
    width, (ny, zs, chans) = own[0].shape[0] // 2, own[0].shape[1:]
    nz = zs * slabs
    fill_second(field_ref, own, other, rim_own, rim_other, me)
    for i in range(width):
        for refs_of, who in ((own, me), (other, 1 - me)):
            pre = joined(refs_of, width + i, 1)
            act = (pre * sigmoid(pre)).astype(BF16).reshape(ny * nz, chans)
            at = pl.multiple_of((who * width + i) * ny * nz, ny * nz)
            act_ref[pl.ds(at, ny * nz), :] = act
    kernel_terms(act_ref, field_ref, 2, 2 * width, nz, scratch_ref, index_ref, per, scale)
    put_chunks(scratch_ref, keep_ref, sent_ref, index_ref[2], keep_ref.shape[1])


def first_kernel(slabs, per, scale, index_ref, *refs):
    own, other, rim_own, rim_other, in_own, in_other, rest = split_refs(refs, [slabs] * 6)
    (grad_out_ref, w_second_ref, w_first_ref, grad_in_ref, keep_ref, sent_ref) = rest[:6]
    field_ref, first_ref, left_ref, scratch_ref = rest[6:]
    me = index_ref[0]
    width, (ny, zs, chans) = own[0].shape[0] // 2, own[0].shape[1:]
    nz = zs * slabs
    fill_second(field_ref, own, other, rim_own, rim_other, me)

    def conv(ref, start, planes, depth, w_ref):
        cols = jnp.concatenate(
            [shifted(ref, a, b, c, start, planes, depth) for a, b, c in OFFSETS], axis=1
        )
        out = jnp.dot(cols, w_ref[...], preferred_element_type=F32)
        return out.reshape(planes, ny, depth, chans)

    def put_first(at, pre):
        grad_act = conv(field_ref, at + 1, pre.shape[0], nz, w_second_ref)
        sig = sigmoid(pre)
        put_planes(first_ref, at, grad_act * (sig * (1.0 + pre * (1.0 - sig))))

    for i in range(0, width, 2):
        put_first(1 + width * me + i, joined(own, width + i, 2))
        put_first(1 + width * (1 - me) + i, joined(other, width + i, 2))
    put_first((1 + 2 * width) * me, joined(rim_own, 2, 1))
    put_first((1 + 2 * width) * (1 - me), joined(rim_other, 2, 1))

    back = conv(first_ref, 1 + width * me, width, zs, w_first_ref)
    grad_in_ref[...] = (grad_out_ref[...].astype(F32) + back).astype(BF16)

    for i in range(width):
        for refs_of, who in ((in_own, me), (in_other, 1 - me)):
            rows = joined(refs_of, i, 1).astype(BF16).reshape(ny * nz, chans)
            at = pl.multiple_of((who * width + i) * ny * nz, ny * nz)
            left_ref[pl.ds(at, ny * nz), :] = rows
    kernel_terms(left_ref, first_ref, 1, 2 * width, nz, scratch_ref, index_ref, per, scale)
    put_chunks(scratch_ref, keep_ref, sent_ref, index_ref[2], keep_ref.shape[1])


def vmem(shape, dtype):
    return pltpu.VMEM(shape, dtype)


def call(body, index, operands, out_shape, scratch, flops, name):
    return pl.pallas_call(
        body,
        out_shape=out_shape,
        in_specs=[pl.BlockSpec(memory_space=pltpu.SMEM)]
        + [pl.BlockSpec(memory_space=pltpu.VMEM)] * len(operands),
        out_specs=[pl.BlockSpec(memory_space=pltpu.VMEM)] * len(out_shape),
        scratch_shapes=scratch,
        compiler_params=pltpu.CompilerParams(vmem_limit_bytes=VMEM_BYTES),
        cost_estimate=pl.CostEstimate(flops=flops, bytes_accessed=4 << 20, transcendentals=0),
        name=name,
    )(index, *operands)


def reduce_pairs(keep, sent, pairs):
    held = list(range(0, pairs, 2))
    gone = list(range(1, pairs, 2))
    bits = []
    bit = 1
    while bit < pairs:
        bits.append(bit)
        got = partner(sent, 2 * bit).astype(F32)
        total = keep + got
        nxt = 2 * bit
        if nxt < pairs // 2:
            pick = [i for i, r in enumerate(held) if not r & nxt]
            drop = [i for i, r in enumerate(held) if r & nxt]
            keep = total[pick[0] :: pick[1] - pick[0]] if len(pick) > 1 else total[pick[0]][None]
            sent = total[drop[0] :: drop[1] - drop[0]] if len(drop) > 1 else total[drop[0]][None]
            sent = sent.astype(BF16)
            held = [held[i] for i in pick]
            bit = nxt
        else:
            break
    last = pairs // 2
    mine = total.astype(BF16)
    got = partner(mine, 2 * last)
    whole = (mine.astype(F32) + got[::-1].astype(F32)).astype(BF16)
    pieces = [(whole, held)]
    for bit in reversed(bits):
        array = jnp.concatenate([p for p, _ in pieces], axis=0)
        names = [r for _, n in pieces for r in n]
        got = partner(array, 2 * bit)
        pieces = [(array, names), (got, [r ^ bit for r in names])]
    array = jnp.concatenate([p for p, _ in pieces], axis=0)
    return array, [r for _, n in pieces for r in n]


def place_kernel(slabs, names, index_ref, *refs):
    pieces, (out_ref, scratch_ref) = refs[:-2], refs[-2:]
    rows = pieces[0].shape[1]
    pairs = len(names)
    me, pair, slab = index_ref[0], index_ref[2], index_ref[3]
    for n, piece in enumerate(pieces):
        r, core = n // 2, n % 2
        share = lax.rem(slab + r, slabs) * 2 + (me ^ core)
        for i, distance in enumerate(names):
            at = pl.multiple_of((share * pairs + (pair ^ distance)) * rows, 16)
            scratch_ref[pl.ds(at, rows), :] = piece[i]
    out_ref[...] = scratch_ref[pl.ds(0, out_ref.shape[0]), :]


def per_device(inputs, pre_first, occupancy, grad_out, w_first, w_second):
    width, ny, zs, chans = inputs.shape
    slabs, bricks = lax.axis_size("slab"), lax.axis_size("brick")
    pairs, nz = bricks // 2, zs * slabs
    cells_all = width * bricks * ny * nz
    scale = 10.0 / cells_all**0.5
    per = -(-27 // (2 * slabs))
    while per * chans % (16 * pairs):
        per += 1
    rows = per * chans // pairs
    slab, brick = lax.axis_index("slab"), lax.axis_index("brick")
    me = lax.rem(brick, 2)
    index = jnp.stack([me, slab * 2 + me, brick // 2, slab]).astype(jnp.int32)

    occ = occupancy[..., None] != 0
    masked = jnp.where(occ, grad_out, jnp.zeros_like(grad_out))
    pre = jnp.where(occ, pre_first, jnp.full_like(pre_first, EMPTY))
    both = jnp.concatenate([masked, pre], axis=0)
    odd = me == 1
    rim = jnp.concatenate(
        [
            jnp.where(odd, masked[width - 2 :], masked[:2]),
            jnp.where(odd, pre[width - 1 :], pre[:1]),
        ],
        axis=0,
    )

    def swap(b):
        return (b + 1) % bricks if b % 2 else (b - 1) % bricks

    own = over_slabs(both)
    rim_own = over_slabs(rim, swap)
    other = [partner(v, 1) for v in own]
    rim_other = [partner(v, 1) for v in rim_own]
    in_own = over_slabs(inputs)
    in_other = [partner(v, 1) for v in in_own]

    def stacked(kernel):
        return jnp.transpose(kernel, (0, 2, 1)).reshape(27 * chans, chans)

    shares = [
        jax.ShapeDtypeStruct((pairs // 2, rows, chans), F32),
        jax.ShapeDtypeStruct((pairs // 2, rows, chans), BF16),
    ]
    field = vmem((3, 2 * width + 4, ny + 2, nz, chans), BF16)
    group = 2 * width * ny * nz
    terms = vmem((per * chans, chans), F32)
    around = [*own, *other, *rim_own, *rim_other]
    keep, sent = call(
        functools.partial(second_kernel, slabs, per, scale),
        index,
        around,
        shares,
        [field, vmem((group, chans), BF16), terms],
        2 * group * per * chans * chans,
        "second_kernel_gradient",
    )
    grad_in, keep_first, sent_first = call(
        functools.partial(first_kernel, slabs, per, scale),
        index,
        [*around, *in_own, *in_other, grad_out, stacked(w_second), stacked(w_first)],
        [jax.ShapeDtypeStruct(inputs.shape, BF16), *shares],
        [
            field,
            vmem((3, 2 * width + 2, ny + 2, nz, chans), BF16),
            vmem((group, chans), BF16),
            terms,
        ],
        2 * group * (28 + per) * chans * chans,
        "first_kernel_gradient",
    )

    def finish(keep, sent):
        array, names = reduce_pairs(keep, sent, pairs)
        pieces = []
        for v in over_slabs(array):
            pieces += [v, partner(v, 1)]
        (out,) = call(
            functools.partial(place_kernel, slabs, names),
            index,
            pieces,
            [jax.ShapeDtypeStruct((27 * chans, chans), BF16)],
            [vmem((2 * slabs * per * chans, chans), BF16)],
            0,
            "place",
        )
        return out.reshape(27, chans, chans)

    return (grad_in, finish(keep_first, sent_first), finish(keep, sent))


def solution(mesh):
    in_specs = (
        P("brick", None, "slab", None),
        P("brick", None, "slab", None),
        P("brick", None, "slab"),
        P("brick", None, "slab", None),
        P(),
        P(),
    )
    out_specs = (P("brick", None, "slab", None), P(), P())
    return jax.shard_map(
        per_device, mesh=mesh, in_specs=in_specs, out_specs=out_specs, check_vma=False
    )
```

time: 130 us -> 72 us (0.55)
  blocking collectives: 82.1 us -> 0 us
  waiting for transfers between devices: 3.68 us -> 20.3 us
  Pallas kernels: 0 us -> 14.8 us
  starting transfers between devices: 14.2 us -> 28.6 us
  local copies, waits for them, and re-layouts: 15.6 us -> 4.16 us
  matrix products: 9.57 us -> 0 us
    psum x1 -> x0, blocking collectives: 82.1 us -> none  [reduce_kernel(): return lax.psum(term, ('slab', 'brick')).astype(jnp.bfloat16)]
    ppermute x8 -> x26, waiting for transfers between devices: 3.68 us -> 20.3 us  [send(): return lax.ppermute(value, AXES, pairs)]
    pallas_call x0 -> x4, Pallas kernels: none -> 14.8 us  [call(): pl.pallas_call(body, out_shape=out_shape, in_specs=[pl.BlockSpec(memory_s...]
    ppermute x8 -> x26, starting transfers between devices: 14.2 us -> 28.6 us  [send(): return lax.ppermute(value, AXES, pairs)]
    dot_general x4 -> x0, matrix products: 9.57 us -> none  [the longest x2 6.73 us: local_term(): lax.dot_general(flat_left, cols, (((0,), (0,)), ((), ())), preferred_elem...]
    unnamed x60 -> x12, local copies, waits for them, and re-layouts: 7.54 us -> 0.91 us
    dot_general x1 -> x0, local copies, waits for them, and re-layouts: 5.77 us -> none  [local_term(): lax.dot_general(flat_left, cols, (((0,), (0,)), ((), ())), preferred_elem...]
    transpose x0 -> x2, local copies, waits for them, and re-layouts: none -> 3.24 us  [stacked(): return jnp.transpose(kernel, (0, 2, 1)).reshape(27 * chans, chans)]
  transfers between devices with their start and end apart: 8 -> 26, of which waited for: 2 -> 14; matrix products, arithmetic and copies ran while one was open for 10% -> 6% of each run, Pallas kernels for 0% -> 6%
where the time goes in v1:
time: 72 us; the launch traced here: 71.7 us
  starting transfers between devices  28.6 us (40%)
  waiting for transfers between devices  20.3 us (28%)
  Pallas kernels  14.8 us (21%)
  local copies, waits for them, and re-layouts  4.16 us (6%)
  other arithmetic  2.89 us (4%)
  between operations  0.87 us (1%)
    ppermute x26, starting transfers between devices, send(): return lax.ppermute(value, AXES, pairs)  28.6 us
    ppermute x26, waiting for transfers between devices, send(): return lax.ppermute(value, AXES, pairs)  20.3 us
    pallas_call x4, Pallas kernels, call(): pl.pallas_call(body, out_shape=out_shape, in_specs=[pl.BlockSpec(memory_s...  14.8 us
    transpose x2, local copies, waits for them, and re-layouts, stacked(): return jnp.transpose(kernel, (0, 2, 1)).reshape(27 * chans, chans)  3.24 us
  transfers between devices with their start and end apart: 26, of which 14 were waited for; matrix products, arithmetic and copies ran while one was open for 6% of the time, Pallas kernels for 6%

profile of v1, /device:TPU:0, one launch (start us, length us, event | category | flops | bytes accessed | tf_op | source)
XLA Modules:
  0.0 71.7 jit_solution(15868965091718972489)
XLA Ops:
  2.6 3.0 %collective-permute-start = (bf16[8,8,16,128]{3,2,1,0:T(8,128)(2,1)S(1)}, bf16[8,8,16,128]{3,2,1,0:T(8,128)(2,1)S(1)}, u32[]{:S(2)}, u32[]{:S(2)}) collective-permute-start(bf16[8,8,16,128]{3,2,1,0:T(8,128)(2,1)S(1)} %pad_maximum_fusion.refs_0_), channel_id=1, source_target_pairs={{16,0},{17,1},{18,2},{19,3},{20,4},{21,5},{22,6},{23,7},{24,8},{25... | collective-permute-start | bytes 786440 | tf_op jit(solution)/shard_map/ppermute | solution.py:25
  6.3 3.7 %collective-permute-start.3 = (bf16[3,8,16,128]{3,2,1,0:T(8,128)(2,1)}, bf16[3,8,16,128]{3,2,1,0:T(8,128)(2,1)S(1)}, u32[]{:S(2)}, u32[]{:S(2)}) collective-permute-start(bf16[3,8,16,128]{3,2,1,0:T(8,128)(2,1)} %pad_maximum_fusion.5), channel_id=1, source_target_pairs={{15,0},{2,1},{1,2},{4,3},{3,4},{6,5},{5,6},{8,7},{7,8},{10,9},{9,1... | collective-permute-start | bytes 294920 | tf_op jit(solution)/shard_map/ppermute | solution.py:25
  10.5 2.2 %collective-permute-done.refs_1_ = bf16[8,8,16,128]{3,2,1,0:T(8,128)(2,1)S(1)} collective-permute-done((bf16[8,8,16,128]{3,2,1,0:T(8,128)(2,1)S(1)}, bf16[8,8,16,128]{3,2,1,0:T(8,128)(2,1)S(1)}, u32[]{:S(2)}, u32[]{:S(2)}) %collective-permute-start) | collective-permute-done | bytes 262176 | tf_op jit(solution)/shard_map/ppermute | solution.py:25
  13.3 5.7 %collective-permute-start.4 = (bf16[3,8,16,128]{3,2,1,0:T(8,128)(2,1)}, bf16[3,8,16,128]{3,2,1,0:T(8,128)(2,1)}, u32[]{:S(2)}, u32[]{:S(2)}) collective-permute-start(bf16[3,8,16,128]{3,2,1,0:T(8,128)(2,1)} %pad_maximum_fusion.5), channel_id=1, source_target_pairs={{31,0},{18,1},{17,2},{20,3},{19,4},{22,5},{21,6},{24,7},{23,8},{26... | collective-permute-start | bytes 294920 | tf_op jit(solution)/shard_map/ppermute | solution.py:25
  19.0 1.3 %copy.9 = bf16[27,128,128]{2,1,0:T(8,128)(2,1)S(1)} copy(bf16[27,128,128]{1,2,0:T(8,128)(2,1)S(1)} %bitcast.12) | data formatting | bytes 1769472 | tf_op jit(solution)/shard_map/transpose | solution.py:271
  20.3 1.9 %copy.10 = bf16[27,128,128]{2,1,0:T(8,128)(2,1)S(1)} copy(bf16[27,128,128]{1,2,0:T(8,128)(2,1)} %bitcast.13) | data formatting | bytes 1769472 | tf_op jit(solution)/shard_map/transpose | solution.py:271
  25.3 8.8 %first_kernel_gradient.1 = (bf16[4,8,16,128]{3,2,1,0:T(8,128)(2,1)}, f32[4,112,128]{2,1,0:T(8,128)S(1)}, bf16[4,112,128]{2,1,0:T(8,128)(2,1)S(1)}) custom-call(s32[4]{0:T(128)S(1)} %pad_add_fusion.index_ref, bf16[8,8,16,128]{3,2,1,0:T(8,128)(2,1)S(1)} %pad_maximum_fusion.refs_0_, bf16[8,8,16,128]{3,2,1,0:T(8,128)(2,1)S(1)} %collective-permute-done.refs_1_, ...), custom_call_target="tpu_custom_call" | custom-call | flops 2348810240 | bytes 4194304 | tf_op jit(solution)/shard_map/first_kernel_gradient/pallas_call | solution.py:172
  34.1 2.8 %second_kernel_gradient.1 = (f32[4,112,128]{2,1,0:T(8,128)S(1)}, bf16[4,112,128]{2,1,0:T(8,128)(2,1)S(1)}) custom-call(s32[4]{0:T(128)S(1)} %pad_add_fusion.index_ref, bf16[8,8,16,128]{3,2,1,0:T(8,128)(2,1)S(1)} %pad_maximum_fusion.refs_0_, bf16[8,8,16,128]{3,2,1,0:T(8,128)(2,1)S(1)} %collective-permute-done.refs_1_, ...), custom_call_target="tpu_custom_call" | custom-call | flops 469762048 | bytes 4194304 | tf_op jit(solution)/shard_map/second_kernel_gradient/pallas_call | solution.py:172
  36.9 2.1 %collective-permute-start.18 = (bf16[4,112,128]{2,1,0:T(8,128)(2,1)S(1)}, bf16[4,112,128]{2,1,0:T(8,128)(2,1)S(1)}, u32[]{:S(2)}, u32[]{:S(2)}) collective-permute-start(bf16[4,112,128]{2,1,0:T(8,128)(2,1)S(1)} %get-tuple-element.12), channel_id=1, source_target_pairs={{2,0},{3,1},{0,2},{1,3},{6,4},{7,5},{4,6},{5,7},{10,8},{11,9},{8,1... | collective-permute-start | bytes 344072 | tf_op jit(solution)/shard_map/ppermute | solution.py:25
  39.4 2.8 %collective-permute-done.18 = bf16[4,112,128]{2,1,0:T(8,128)(2,1)S(1)} collective-permute-done((bf16[4,112,128]{2,1,0:T(8,128)(2,1)S(1)}, bf16[4,112,128]{2,1,0:T(8,128)(2,1)S(1)}, u32[]{:S(2)}, u32[]{:S(2)}) %collective-permute-start.18) | collective-permute-done | bytes 114720 | tf_op jit(solution)/shard_map/ppermute | solution.py:25
  42.4 1.2 %collective-permute-done.11 = bf16[2,112,128]{2,1,0:T(8,128)(2,1)S(1)} collective-permute-done((bf16[2,112,128]{2,1,0:T(8,128)(2,1)S(1)}, bf16[2,112,128]{2,1,0:T(8,128)(2,1)S(1)}, u32[]{:S(2)}, u32[]{:S(2)}) %collective-permute-start.11) | collective-permute-done | bytes 57376 | tf_op jit(solution)/shard_map/ppermute | solution.py:25
  43.6 3.2 %collective-permute-start.12 = (bf16[2,112,128]{2,1,0:T(8,128)(2,1)S(1)}, bf16[2,112,128]{2,1,0:T(8,128)(2,1)S(1)}, u32[]{:S(2)}, u32[]{:S(2)}) collective-permute-start(bf16[2,112,128]{2,1,0:T(8,128)(2,1)S(1)} %add_convert_fusion.3), channel_id=1, source_target_pairs={{8,0},{9,1},{10,2},{11,3},{12,4},{13,5},{14,6},{15,7},{0,8},{1,9},... | collective-permute-start | bytes 172040 | tf_op jit(solution)/shard_map/ppermute | solution.py:25
  46.8 2.1 %collective-permute-start.20 = (bf16[2,112,128]{2,1,0:T(8,128)(2,1)S(1)}, bf16[2,112,128]{2,1,0:T(8,128)(2,1)S(1)}, u32[]{:S(2)}, u32[]{:S(2)}) collective-permute-start(bf16[2,112,128]{2,1,0:T(8,128)(2,1)S(1)} %add_convert_fusion.1), channel_id=1, source_target_pairs={{8,0},{9,1},{10,2},{11,3},{12,4},{13,5},{14,6},{15,7},{0,8},{1,9},... | collective-permute-start | bytes 172040 | tf_op jit(solution)/shard_map/ppermute | solution.py:25
  48.9 1.9 %collective-permute-done.12 = bf16[2,112,128]{2,1,0:T(8,128)(2,1)S(1)} collective-permute-done((bf16[2,112,128]{2,1,0:T(8,128)(2,1)S(1)}, bf16[2,112,128]{2,1,0:T(8,128)(2,1)S(1)}, u32[]{:S(2)}, u32[]{:S(2)}) %collective-permute-start.12) | collective-permute-done | bytes 57376 | tf_op jit(solution)/shard_map/ppermute | solution.py:25
  52.0 1.4 %collective-permute-start.21 = (bf16[2,112,128]{2,1,0:T(8,128)(2,1)S(1)}, bf16[2,112,128]{2,1,0:T(8,128)(2,1)S(1)}, u32[]{:S(2)}, u32[]{:S(2)}) collective-permute-start(bf16[2,112,128]{2,1,0:T(8,128)(2,1)S(1)} %add_convert_fusion), channel_id=1, source_target_pairs={{4,0},{5,1},{6,2},{7,3},{0,4},{1,5},{2,6},{3,7},{12,8},{13,9},{14,... | collective-permute-start | bytes 172040 | tf_op jit(solution)/shard_map/ppermute | solution.py:25
  53.4 1.6 %collective-permute-done.13 = bf16[2,112,128]{2,1,0:T(8,128)(2,1)S(1)} collective-permute-done((bf16[2,112,128]{2,1,0:T(8,128)(2,1)S(1)}, bf16[2,112,128]{2,1,0:T(8,128)(2,1)S(1)}, u32[]{:S(2)}, u32[]{:S(2)}) %collective-permute-start.13) | collective-permute-done | bytes 57376 | tf_op jit(solution)/shard_map/ppermute | solution.py:25
  56.3 2.0 %collective-permute-start.22 = (bf16[4,112,128]{2,1,0:T(8,128)(2,1)S(1)}, bf16[4,112,128]{2,1,0:T(8,128)(2,1)S(1)}, u32[]{:S(2)}, u32[]{:S(2)}) collective-permute-start(bf16[4,112,128]{2,1,0:T(8,128)(2,1)S(1)} %pad_maximum_fusion.4), channel_id=1, source_target_pairs={{2,0},{3,1},{0,2},{1,3},{6,4},{7,5},{4,6},{5,7},{10,8},{11,9},{8,1... | collective-permute-start | bytes 344072 | tf_op jit(solution)/shard_map/ppermute | solution.py:25
  58.3 1.6 %collective-permute-done.14 = bf16[4,112,128]{2,1,0:T(8,128)(2,1)S(1)} collective-permute-done((bf16[4,112,128]{2,1,0:T(8,128)(2,1)S(1)}, bf16[4,112,128]{2,1,0:T(8,128)(2,1)S(1)}, u32[]{:S(2)}, u32[]{:S(2)}) %collective-permute-start.14) | collective-permute-done | bytes 114720 | tf_op jit(solution)/shard_map/ppermute | solution.py:25
  60.0 1.5 %collective-permute-start.16 = (bf16[8,112,128]{2,1,0:T(8,128)(2,1)S(1)}, bf16[8,112,128]{2,1,0:T(8,128)(2,1)S(1)}, u32[]{:S(2)}, u32[]{:S(2)}) collective-permute-start(bf16[8,112,128]{2,1,0:T(8,128)(2,1)S(1)} %pad_maximum_fusion.1.refs_0_), channel_id=1, source_target_pairs={{16,0},{17,1},{18,2},{19,3},{20,4},{21,5},{22,6},{23,7},{24,8},{25... | collective-permute-start | bytes 688136 | tf_op jit(solution)/shard_map/ppermute | solution.py:25
  61.5 1.2 %collective-permute-start.24 = (bf16[8,112,128]{2,1,0:T(8,128)(2,1)S(1)}, bf16[8,112,128]{2,1,0:T(8,128)(2,1)S(1)}, u32[]{:S(2)}, u32[]{:S(2)}) collective-permute-start(bf16[8,112,128]{2,1,0:T(8,128)(2,1)S(1)} %pad_maximum_fusion.2.refs_0_), channel_id=1, source_target_pairs={{16,0},{17,1},{18,2},{19,3},{20,4},{21,5},{22,6},{23,7},{24,8},{25... | collective-permute-start | bytes 688136 | tf_op jit(solution)/shard_map/ppermute | solution.py:25
  62.7 3.3 %collective-permute-done.16.refs_2_ = bf16[8,112,128]{2,1,0:T(8,128)(2,1)S(1)} collective-permute-done((bf16[8,112,128]{2,1,0:T(8,128)(2,1)S(1)}, bf16[8,112,128]{2,1,0:T(8,128)(2,1)S(1)}, u32[]{:S(2)}, u32[]{:S(2)}) %collective-permute-start.16) | collective-permute-done | bytes 229408 | tf_op jit(solution)/shard_map/ppermute | solution.py:25
  66.6 1.9 %collective-permute-done.24.refs_2_ = bf16[8,112,128]{2,1,0:T(8,128)(2,1)S(1)} collective-permute-done((bf16[8,112,128]{2,1,0:T(8,128)(2,1)S(1)}, bf16[8,112,128]{2,1,0:T(8,128)(2,1)S(1)}, u32[]{:S(2)}, u32[]{:S(2)}) %collective-permute-start.24) | collective-permute-done | bytes 229408 | tf_op jit(solution)/shard_map/ppermute | solution.py:25
  68.5 1.6 %place.2 = bf16[3456,128]{1,0:T(8,128)(2,1)} custom-call(s32[4]{0:T(128)S(1)} %pad_add_fusion.index_ref, bf16[8,112,128]{2,1,0:T(8,128)(2,1)S(1)} %pad_maximum_fusion.1.refs_0_, bf16[8,112,128]{2,1,0:T(8,128)(2,1)S(1)} %collective-permute-done.15.refs_1_, bf16[8,112,128]{2,1,0:T(8,128)(2,1)S(1)} %collective-permute-done.16.refs_2_, ...), custom_call_target="tpu_custom_call" | custom-call | bytes 4194304 | tf_op jit(solution)/shard_map/place/pallas_call | solution.py:172
  70.1 1.6 %place.3 = bf16[3456,128]{1,0:T(8,128)(2,1)} custom-call(s32[4]{0:T(128)S(1)} %pad_add_fusion.index_ref, bf16[8,112,128]{2,1,0:T(8,128)(2,1)S(1)} %pad_maximum_fusion.2.refs_0_, bf16[8,112,128]{2,1,0:T(8,128)(2,1)S(1)} %collective-permute-done.23.refs_1_, bf16[8,112,128]{2,1,0:T(8,128)(2,1)S(1)} %collective-permute-done.24.refs_2_, ...), custom_call_target="tpu_custom_call" | custom-call | bytes 4194304 | tf_op jit(solution)/shard_map/place/pallas_call | solution.py:172
  (65 shorter events, 10.3 us)
Async XLA Ops:
  2.6 10.2 %collective-permute-start = (bf16[8,8,16,128]{3,2,1,0:T(8,128)(2,1)S(1)}, bf16[8,8,16,128]{3,2,1,0:T(8,128)(2,1)S(1)}, u32[]{:S(2)}, u32[]{:S(2)}) collective-permute-start(bf16[8,8,16,128]{3,2,1,0:T(8,128)(2,1)S(1)} %pad_maximum_fusion.refs_0_), channel_id=1, source_target_pairs={{16,0},{17,1},{18,2},{19,3},{20,4},{21,5},{22,6},{23,7},{24,8},{25... | collective-permute-start | bytes 786440 | tf_op jit(solution)/shard_map/ppermute | solution.py:25
  6.3 7.0 %collective-permute-start.3 = (bf16[3,8,16,128]{3,2,1,0:T(8,128)(2,1)}, bf16[3,8,16,128]{3,2,1,0:T(8,128)(2,1)S(1)}, u32[]{:S(2)}, u32[]{:S(2)}) collective-permute-start(bf16[3,8,16,128]{3,2,1,0:T(8,128)(2,1)} %pad_maximum_fusion.5), channel_id=1, source_target_pairs={{15,0},{2,1},{1,2},{4,3},{3,4},{6,5},{5,6},{8,7},{7,8},{10,9},{9,1... | collective-permute-start | bytes 294920 | tf_op jit(solution)/shard_map/ppermute | solution.py:25
  10.0 9.0 %collective-permute-start.7 = (bf16[4,8,16,128]{3,2,1,0:T(8,128)(2,1)S(1)}, bf16[4,8,16,128]{3,2,1,0:T(8,128)(2,1)S(1)}, u32[]{:S(2)}, u32[]{:S(2)}) collective-permute-start(bf16[4,8,16,128]{3,2,1,0:T(8,128)(2,1)S(1)} %copy-done.1), channel_id=1, source_target_pairs={{16,0},{17,1},{18,2},{19,3},{20,4},{21,5},{22,6},{23,7},{24,8},{25... | collective-permute-start | bytes 393224 | tf_op jit(solution)/shard_map/ppermute | solution.py:25
  10.5 13.8 %collective-permute-start.1 = (bf16[8,8,16,128]{3,2,1,0:T(8,128)(2,1)S(1)}, bf16[8,8,16,128]{3,2,1,0:T(8,128)(2,1)S(1)}, u32[]{:S(2)}, u32[]{:S(2)}) collective-permute-start(bf16[8,8,16,128]{3,2,1,0:T(8,128)(2,1)S(1)} %pad_maximum_fusion.refs_0_), channel_id=1, source_target_pairs={{1,0},{0,1},{3,2},{2,3},{5,4},{4,5},{7,6},{6,7},{9,8},{8,9},{11,10... | collective-permute-start | bytes 786440 | tf_op jit(solution)/shard_map/ppermute | solution.py:25
  12.8 11.6 %collective-permute-start.2 = (bf16[8,8,16,128]{3,2,1,0:T(8,128)(2,1)S(1)}, bf16[8,8,16,128]{3,2,1,0:T(8,128)(2,1)S(1)}, u32[]{:S(2)}, u32[]{:S(2)}) collective-permute-start(bf16[8,8,16,128]{3,2,1,0:T(8,128)(2,1)S(1)} %collective-permute-done.refs_1_), channel_id=1, source_target_pairs={{1,0},{0,1},{3,2},{2,3},{5,4},{4,5},{7,6},{6,7},{9,8},{8,9},{11,10... | collective-permute-start | bytes 786440 | tf_op jit(solution)/shard_map/ppermute | solution.py:25
  12.8 10.1 %collective-permute-start.8 = (bf16[4,8,16,128]{3,2,1,0:T(8,128)(2,1)S(1)}, bf16[4,8,16,128]{3,2,1,0:T(8,128)(2,1)S(1)}, u32[]{:S(2)}, u32[]{:S(2)}) collective-permute-start(bf16[4,8,16,128]{3,2,1,0:T(8,128)(2,1)S(1)} %copy-done.1), channel_id=1, source_target_pairs={{1,0},{0,1},{3,2},{2,3},{5,4},{4,5},{7,6},{6,7},{9,8},{8,9},{11,10... | collective-permute-start | bytes 393224 | tf_op jit(solution)/shard_map/ppermute | solution.py:25
  13.3 9.0 %collective-permute-start.4 = (bf16[3,8,16,128]{3,2,1,0:T(8,128)(2,1)}, bf16[3,8,16,128]{3,2,1,0:T(8,128)(2,1)}, u32[]{:S(2)}, u32[]{:S(2)}) collective-permute-start(bf16[3,8,16,128]{3,2,1,0:T(8,128)(2,1)} %pad_maximum_fusion.5), channel_id=1, source_target_pairs={{31,0},{18,1},{17,2},{20,3},{19,4},{22,5},{21,6},{24,7},{23,8},{26... | collective-permute-start | bytes 294920 | tf_op jit(solution)/shard_map/ppermute | solution.py:25
  19.0 5.4 %collective-permute-start.9 = (bf16[4,8,16,128]{3,2,1,0:T(8,128)(2,1)S(1)}, bf16[4,8,16,128]{3,2,1,0:T(8,128)(2,1)S(1)}, u32[]{:S(2)}, u32[]{:S(2)}) collective-permute-start(bf16[4,8,16,128]{3,2,1,0:T(8,128)(2,1)S(1)} %collective-permute-done.7.refs_9_), channel_id=1, source_target_pairs={{1,0},{0,1},{3,2},{2,3},{5,4},{4,5},{7,6},{6,7},{9,8},{8,9},{11,10... | collective-permute-start | bytes 393224 | tf_op jit(solution)/shard_map/ppermute | solution.py:25
  22.3 1.7 %collective-permute-start.5 = (bf16[3,8,16,128]{3,2,1,0:T(8,128)(2,1)}, bf16[3,8,16,128]{3,2,1,0:T(8,128)(2,1)S(1)}, u32[]{:S(2)}, u32[]{:S(2)}) collective-permute-start(bf16[3,8,16,128]{3,2,1,0:T(8,128)(2,1)} %copy-done.2), channel_id=1, source_target_pairs={{1,0},{0,1},{3,2},{2,3},{5,4},{4,5},{7,6},{6,7},{9,8},{8,9},{11,10... | collective-permute-start | bytes 294920 | tf_op jit(solution)/shard_map/ppermute | solution.py:25
  34.1 5.2 %collective-permute-start.10 = (bf16[4,112,128]{2,1,0:T(8,128)(2,1)S(1)}, bf16[4,112,128]{2,1,0:T(8,128)(2,1)S(1)}, u32[]{:S(2)}, u32[]{:S(2)}) collective-permute-start(bf16[4,112,128]{2,1,0:T(8,128)(2,1)S(1)} %get-tuple-element.10), channel_id=1, source_target_pairs={{2,0},{3,1},{0,2},{1,3},{6,4},{7,5},{4,6},{5,7},{10,8},{11,9},{8,1... | collective-permute-start | bytes 344072 | tf_op jit(solution)/shard_map/ppermute | solution.py:25
  36.9 5.3 %collective-permute-start.18 = (bf16[4,112,128]{2,1,0:T(8,128)(2,1)S(1)}, bf16[4,112,128]{2,1,0:T(8,128)(2,1)S(1)}, u32[]{:S(2)}, u32[]{:S(2)}) collective-permute-start(bf16[4,112,128]{2,1,0:T(8,128)(2,1)S(1)} %get-tuple-element.12), channel_id=1, source_target_pairs={{2,0},{3,1},{0,2},{1,3},{6,4},{7,5},{4,6},{5,7},{10,8},{11,9},{8,1... | collective-permute-start | bytes 344072 | tf_op jit(solution)/shard_map/ppermute | solution.py:25
  39.3 4.2 %collective-permute-start.11 = (bf16[2,112,128]{2,1,0:T(8,128)(2,1)S(1)}, bf16[2,112,128]{2,1,0:T(8,128)(2,1)S(1)}, u32[]{:S(2)}, u32[]{:S(2)}) collective-permute-start(bf16[2,112,128]{2,1,0:T(8,128)(2,1)S(1)} %slice.31), channel_id=1, source_target_pairs={{4,0},{5,1},{6,2},{7,3},{0,4},{1,5},{2,6},{3,7},{12,8},{13,9},{14,... | collective-permute-start | bytes 172040 | tf_op jit(solution)/shard_map/ppermute | solution.py:25
  42.2 4.6 %collective-permute-start.19 = (bf16[2,112,128]{2,1,0:T(8,128)(2,1)S(1)}, bf16[2,112,128]{2,1,0:T(8,128)(2,1)S(1)}, u32[]{:S(2)}, u32[]{:S(2)}) collective-permute-start(bf16[2,112,128]{2,1,0:T(8,128)(2,1)S(1)} %slice.33), channel_id=1, source_target_pairs={{4,0},{5,1},{6,2},{7,3},{0,4},{1,5},{2,6},{3,7},{12,8},{13,9},{14,... | collective-permute-start | bytes 172040 | tf_op jit(solution)/shard_map/ppermute | solution.py:25
  43.6 7.2 %collective-permute-start.12 = (bf16[2,112,128]{2,1,0:T(8,128)(2,1)S(1)}, bf16[2,112,128]{2,1,0:T(8,128)(2,1)S(1)}, u32[]{:S(2)}, u32[]{:S(2)}) collective-permute-start(bf16[2,112,128]{2,1,0:T(8,128)(2,1)S(1)} %add_convert_fusion.3), channel_id=1, source_target_pairs={{8,0},{9,1},{10,2},{11,3},{12,4},{13,5},{14,6},{15,7},{0,8},{1,9},... | collective-permute-start | bytes 172040 | tf_op jit(solution)/shard_map/ppermute | solution.py:25
  46.8 5.2 %collective-permute-start.20 = (bf16[2,112,128]{2,1,0:T(8,128)(2,1)S(1)}, bf16[2,112,128]{2,1,0:T(8,128)(2,1)S(1)}, u32[]{:S(2)}, u32[]{:S(2)}) collective-permute-start(bf16[2,112,128]{2,1,0:T(8,128)(2,1)S(1)} %add_convert_fusion.1), channel_id=1, source_target_pairs={{8,0},{9,1},{10,2},{11,3},{12,4},{13,5},{14,6},{15,7},{0,8},{1,9},... | collective-permute-start | bytes 172040 | tf_op jit(solution)/shard_map/ppermute | solution.py:25
  50.8 4.2 %collective-permute-start.13 = (bf16[2,112,128]{2,1,0:T(8,128)(2,1)S(1)}, bf16[2,112,128]{2,1,0:T(8,128)(2,1)S(1)}, u32[]{:S(2)}, u32[]{:S(2)}) collective-permute-start(bf16[2,112,128]{2,1,0:T(8,128)(2,1)S(1)} %add_convert_fusion.2), channel_id=1, source_target_pairs={{4,0},{5,1},{6,2},{7,3},{0,4},{1,5},{2,6},{3,7},{12,8},{13,9},{14,... | collective-permute-start | bytes 172040 | tf_op jit(solution)/shard_map/ppermute | solution.py:25
  52.0 4.2 %collective-permute-start.21 = (bf16[2,112,128]{2,1,0:T(8,128)(2,1)S(1)}, bf16[2,112,128]{2,1,0:T(8,128)(2,1)S(1)}, u32[]{:S(2)}, u32[]{:S(2)}) collective-permute-start(bf16[2,112,128]{2,1,0:T(8,128)(2,1)S(1)} %add_convert_fusion), channel_id=1, source_target_pairs={{4,0},{5,1},{6,2},{7,3},{0,4},{1,5},{2,6},{3,7},{12,8},{13,9},{14,... | collective-permute-start | bytes 172040 | tf_op jit(solution)/shard_map/ppermute | solution.py:25
  55.1 4.9 %collective-permute-start.14 = (bf16[4,112,128]{2,1,0:T(8,128)(2,1)S(1)}, bf16[4,112,128]{2,1,0:T(8,128)(2,1)S(1)}, u32[]{:S(2)}, u32[]{:S(2)}) collective-permute-start(bf16[4,112,128]{2,1,0:T(8,128)(2,1)S(1)} %pad_maximum_fusion.3), channel_id=1, source_target_pairs={{2,0},{3,1},{0,2},{1,3},{6,4},{7,5},{4,6},{5,7},{10,8},{11,9},{8,1... | collective-permute-start | bytes 344072 | tf_op jit(solution)/shard_map/ppermute | solution.py:25
  56.3 5.2 %collective-permute-start.22 = (bf16[4,112,128]{2,1,0:T(8,128)(2,1)S(1)}, bf16[4,112,128]{2,1,0:T(8,128)(2,1)S(1)}, u32[]{:S(2)}, u32[]{:S(2)}) collective-permute-start(bf16[4,112,128]{2,1,0:T(8,128)(2,1)S(1)} %pad_maximum_fusion.4), channel_id=1, source_target_pairs={{2,0},{3,1},{0,2},{1,3},{6,4},{7,5},{4,6},{5,7},{10,8},{11,9},{8,1... | collective-permute-start | bytes 344072 | tf_op jit(solution)/shard_map/ppermute | solution.py:25
  60.0 6.1 %collective-permute-start.16 = (bf16[8,112,128]{2,1,0:T(8,128)(2,1)S(1)}, bf16[8,112,128]{2,1,0:T(8,128)(2,1)S(1)}, u32[]{:S(2)}, u32[]{:S(2)}) collective-permute-start(bf16[8,112,128]{2,1,0:T(8,128)(2,1)S(1)} %pad_maximum_fusion.1.refs_0_), channel_id=1, source_target_pairs={{16,0},{17,1},{18,2},{19,3},{20,4},{21,5},{22,6},{23,7},{24,8},{25... | collective-permute-start | bytes 688136 | tf_op jit(solution)/shard_map/ppermute | solution.py:25
  61.5 7.0 %collective-permute-start.24 = (bf16[8,112,128]{2,1,0:T(8,128)(2,1)S(1)}, bf16[8,112,128]{2,1,0:T(8,128)(2,1)S(1)}, u32[]{:S(2)}, u32[]{:S(2)}) collective-permute-start(bf16[8,112,128]{2,1,0:T(8,128)(2,1)S(1)} %pad_maximum_fusion.2.refs_0_), channel_id=1, source_target_pairs={{16,0},{17,1},{18,2},{19,3},{20,4},{21,5},{22,6},{23,7},{24,8},{25... | collective-permute-start | bytes 688136 | tf_op jit(solution)/shard_map/ppermute | solution.py:25
  62.7 5.8 %collective-permute-start.15 = (bf16[8,112,128]{2,1,0:T(8,128)(2,1)S(1)}, bf16[8,112,128]{2,1,0:T(8,128)(2,1)S(1)}, u32[]{:S(2)}, u32[]{:S(2)}) collective-permute-start(bf16[8,112,128]{2,1,0:T(8,128)(2,1)S(1)} %pad_maximum_fusion.1.refs_0_), channel_id=1, source_target_pairs={{1,0},{0,1},{3,2},{2,3},{5,4},{4,5},{7,6},{6,7},{9,8},{8,9},{11,10... | collective-permute-start | bytes 688136 | tf_op jit(solution)/shard_map/ppermute | solution.py:25
  66.1 2.5 %collective-permute-start.17 = (bf16[8,112,128]{2,1,0:T(8,128)(2,1)S(1)}, bf16[8,112,128]{2,1,0:T(8,128)(2,1)S(1)}, u32[]{:S(2)}, u32[]{:S(2)}) collective-permute-start(bf16[8,112,128]{2,1,0:T(8,128)(2,1)S(1)} %collective-permute-done.16.refs_2_), channel_id=1, source_target_pairs={{1,0},{0,1},{3,2},{2,3},{5,4},{4,5},{7,6},{6,7},{9,8},{8,9},{11,10... | collective-permute-start | bytes 688136 | tf_op jit(solution)/shard_map/ppermute | solution.py:25
  66.1 4.1 %collective-permute-start.23 = (bf16[8,112,128]{2,1,0:T(8,128)(2,1)S(1)}, bf16[8,112,128]{2,1,0:T(8,128)(2,1)S(1)}, u32[]{:S(2)}, u32[]{:S(2)}) collective-permute-start(bf16[8,112,128]{2,1,0:T(8,128)(2,1)S(1)} %pad_maximum_fusion.2.refs_0_), channel_id=1, source_target_pairs={{1,0},{0,1},{3,2},{2,3},{5,4},{4,5},{7,6},{6,7},{9,8},{8,9},{11,10... | collective-permute-start | bytes 688136 | tf_op jit(solution)/shard_map/ppermute | solution.py:25
  (8 other events, 45.3 us)

commit v2 on v1

v2 whole, which is shorter than its diff:
```python
import functools
import math

import jax
import jax.numpy as jnp
from jax import lax
from jax.experimental import pallas as pl
from jax.experimental.pallas import tpu as pltpu
from jax.sharding import PartitionSpec as P

AXES = ("slab", "brick")
F32 = jnp.float32
BF16 = jnp.bfloat16
OFFSETS = [(a, b, c) for a in (-1, 0, 1) for b in (-1, 0, 1) for c in (-1, 0, 1)]
EMPTY = -9984.0


def send(value, slab_from, brick_from):
    slabs, bricks = lax.axis_size("slab"), lax.axis_size("brick")
    pairs = [
        (slab_from(s) * bricks + brick_from(b), s * bricks + b)
        for s in range(slabs)
        for b in range(bricks)
    ]
    return lax.ppermute(value, AXES, pairs)


def same(index):
    return index


def over_slabs(value, brick_from=same):
    slabs = lax.axis_size("slab")
    pieces = []
    for r in range(slabs):
        if r == 0 and brick_from is same:
            pieces.append(value)
        else:
            pieces.append(send(value, lambda s, r=r: (s + r) % slabs, brick_from))
    return pieces


def partner(value, bit):
    return send(value, same, lambda b: b ^ bit)


def shifted(field_ref, a, b, c, start, planes, nz):
    ny = field_ref.shape[2] - 2
    block = field_ref[c + 1, pl.ds(start - a, planes), pl.ds(1 - b, ny), pl.ds(0, nz), :]
    return block.reshape(planes * ny * nz, block.shape[-1])


def put_planes(field_ref, start, planes):
    n, ny, nz, chans = planes.shape
    flat = planes.reshape(n * ny, nz, chans)
    for c in (-1, 0, 1):
        rolled = flat if c == 0 else pltpu.roll(flat, c % nz, 1)
        rolled = rolled.astype(BF16).reshape(n, ny, nz, chans)
        field_ref[c + 1, pl.ds(start, n), pl.ds(1, ny)] = rolled
        field_ref[c + 1, pl.ds(start, n), pl.ds(0, 1)] = rolled[:, ny - 1 :]
        field_ref[c + 1, pl.ds(start, n), pl.ds(ny + 1, 1)] = rolled[:, :1]


def joined(refs, start, count):
    return jnp.concatenate([r[start : start + count].astype(F32) for r in refs], axis=2)


def fill_second(field_ref, own, other, rim_own, rim_other, me):
    width = own[0].shape[0] // 3
    for i in range(width):
        put_planes(field_ref, 2 + width * me + i, joined(own, i, 1))
        put_planes(field_ref, 2 + width * (1 - me) + i, joined(other, i, 1))
    for i in range(2):
        put_planes(field_ref, (2 + 2 * width) * me + i, joined(rim_own, i, 1))
        put_planes(field_ref, (2 + 2 * width) * (1 - me) + i, joined(rim_other, i, 1))


def sigmoid(v):
    return 1.0 / (1.0 + jnp.exp(-v))


def kernel_terms(left_ref, field_ref, start, planes, nz, scratch_ref, index_ref, per, scale):
    chans = left_ref.shape[-1]
    for j in range(per):
        k = jnp.minimum(index_ref[1] * per + j, 26)
        a, b, c = k // 9 - 1, (k // 3) % 3 - 1, k % 3 - 1
        cols = shifted(field_ref, a, b, c, start, planes, nz)
        term = lax.dot_general(
            left_ref[...], cols, (((0,), (0,)), ((), ())), preferred_element_type=F32
        )
        scratch_ref[pl.ds(j * chans, chans), :] = term * scale


def put_chunks(scratch_ref, keep_ref, sent_refs, me, tensor):
    count, rows = keep_ref.shape[0], keep_ref.shape[1] // 2
    for i in range(count):
        for rest, ref in enumerate((keep_ref, *sent_refs)):
            at = pl.multiple_of((me ^ (4 * i + rest)) * rows, 8)
            chunk = scratch_ref[pl.ds(at, rows), :].astype(ref.dtype)
            ref[i, pl.ds(tensor * rows, rows), :] = chunk


def group_kernel(slabs, per, scale, index_ref, *refs):
    own, other = refs[:slabs], refs[slabs : 2 * slabs]
    rim_own, rim_other = (
        [ref.at[pl.ds(3 * r, 3)] for r in range(slabs)] for ref in refs[2 * slabs : 2 * slabs + 2]
    )
    grad_out_ref, w_second_ref, w_first_ref, grad_in_ref, keep_ref, *refs = refs[2 * slabs + 2 :]
    *sent_refs, field_ref, first_ref, left_ref, scratch_ref = refs
    me, pair = index_ref[0], index_ref[2]
    width, (ny, zs, chans) = own[0].shape[0] // 3, own[0].shape[1:]
    nz = zs * slabs
    fill_second(field_ref, own, other, rim_own, rim_other, me)

    def fill_left(plane):
        for i in range(width):
            for refs_of, who in ((own, me), (other, 1 - me)):
                rows = plane(refs_of, i).astype(BF16).reshape(ny * nz, chans)
                at = pl.multiple_of((who * width + i) * ny * nz, ny * nz)
                left_ref[pl.ds(at, ny * nz), :] = rows

    def conv(ref, start, planes, depth, w_ref):
        cols = jnp.concatenate(
            [shifted(ref, a, b, c, start, planes, depth) for a, b, c in OFFSETS], axis=1
        )
        out = jnp.dot(cols, w_ref[...], preferred_element_type=F32)
        return out.reshape(planes, ny, depth, chans)

    def put_first(at, pre):
        grad_act = conv(field_ref, at + 1, pre.shape[0], nz, w_second_ref)
        sig = sigmoid(pre)
        put_planes(first_ref, at, grad_act * (sig * (1.0 + pre * (1.0 - sig))))

    for i in range(0, width, 2):
        put_first(1 + width * me + i, joined(own, width + i, 2))
        put_first(1 + width * (1 - me) + i, joined(other, width + i, 2))
    put_first((1 + 2 * width) * me, joined(rim_own, 2, 1))
    put_first((1 + 2 * width) * (1 - me), joined(rim_other, 2, 1))

    back = conv(first_ref, 1 + width * me, width, zs, w_first_ref)
    grad_in_ref[...] = (grad_out_ref[...].astype(F32) + back).astype(BF16)

    fill_left(lambda refs_of, i: joined(refs_of, 2 * width + i, 1))
    kernel_terms(left_ref, first_ref, 1, 2 * width, nz, scratch_ref, index_ref, per, scale)
    put_chunks(scratch_ref, keep_ref, sent_refs, pair, 0)

    def act(refs_of, i):
        pre = joined(refs_of, width + i, 1)
        return pre * sigmoid(pre)

    fill_left(act)
    kernel_terms(left_ref, field_ref, 2, 2 * width, nz, scratch_ref, index_ref, per, scale)
    put_chunks(scratch_ref, keep_ref, sent_refs, pair, 1)


def vmem(shape, dtype):
    return pltpu.VMEM(shape, dtype)


def vmem_bytes(scratch):
    held = sum(math.prod(v.shape) * v.dtype.itemsize for v in scratch)
    return (12 << 20) + held * 3 // 2


def call(body, index, operands, out_shape, scratch, flops, name):
    def space(shape):
        return pl.BlockSpec(memory_space=pltpu.SMEM if shape.dtype == jnp.int32 else pltpu.VMEM)

    return pl.pallas_call(
        body,
        out_shape=out_shape,
        in_specs=[space(v) for v in (index, *operands)],
        out_specs=[space(v) for v in out_shape],
        scratch_shapes=scratch,
        compiler_params=pltpu.CompilerParams(vmem_limit_bytes=vmem_bytes(scratch)),
        cost_estimate=pl.CostEstimate(flops=flops, bytes_accessed=4 << 20, transcendentals=0),
        name=name,
    )(index, *operands)


def combine(keep, sent, pairs, slabs):
    total = keep + sum(partner(v, 2 * d).astype(F32) for d, v in enumerate(sent, 1))
    held = list(range(0, pairs, 4))
    middle = [1 << i for i in range(2, pairs.bit_length() - 2)]
    for bit in middle:
        keep = jnp.stack([total[i] for i, r in enumerate(held) if not r & bit])
        sent = jnp.stack([total[i] for i, r in enumerate(held) if r & bit])
        total = keep + partner(sent.astype(BF16), 2 * bit).astype(F32)
        held = [r for r in held if not r & bit]
    mine = lax.reduce_precision(total, 8, 7).astype(BF16)
    got = partner(mine, pairs)
    array = (mine.astype(F32) + got[::-1].astype(F32)).astype(BF16)
    for bit in [*middle[::-1], 2]:
        array = jnp.concatenate([array, partner(array, 2 * bit)], axis=0)
        held = held + [r ^ bit for r in held]
    pieces = {(0, 0): array}
    for r in range(slabs):
        for odd in range(2):
            if r or odd:
                pieces[r, odd] = send(
                    array,
                    lambda s, r=r: (s + r) % slabs,
                    lambda b, odd=odd: b ^ (2 * odd),
                )
    return pieces, held


def place_kernel(slabs, pairs, held, index_ref, *refs):
    pieces, outs, scratch_ref, sems = refs[:-4], refs[-4:-2], refs[-2], refs[-1]
    me, pair, slab = index_ref[0], index_ref[2], index_ref[3]
    length = scratch_ref.shape[2]
    rows = length // pairs
    copies = []
    for core in range(2):
        for r in range(slabs):
            share = lax.rem(slab + r, slabs) * 2 + (me ^ core)
            for t, out_ref in enumerate(outs):
                slot = core * slabs + r
                for odd in range(2):
                    for i, d in enumerate(held):
                        at = pl.multiple_of((pair ^ d ^ odd) * rows, 16)
                        piece = pieces[2 * slot + odd]
                        scratch_ref[t, slot, pl.ds(at, rows), :] = piece[i, pl.ds(t * rows, rows), :]
                full, part = divmod(out_ref.shape[0], length)
                cases = [(share < full, length)] + ([(share == full, part)] if part else [])
                start = pl.multiple_of(share * length, 16)
                for case, size in cases:
                    copy = pltpu.make_async_copy(
                        scratch_ref.at[t, slot, pl.ds(0, size)],
                        out_ref.at[pl.ds(start, size)],
                        sems.at[t, slot],
                    )
                    copies.append((case, copy))
                    pl.when(case)(copy.start)
    for case, copy in copies:
        pl.when(case)(copy.wait)


def place(slabs, pairs, held, index, pieces, rows):
    chans = pieces[0].shape[-1]
    length = pieces[0].shape[1] // 2 * pairs
    shape = jax.ShapeDtypeStruct((rows, chans), BF16)
    scratch = [vmem((2, 2 * slabs, length, chans), BF16)]
    return pl.pallas_call(
        functools.partial(place_kernel, slabs, pairs, held),
        out_shape=[shape] * 2,
        in_specs=[pl.BlockSpec(memory_space=pltpu.SMEM)]
        + [pl.BlockSpec(memory_space=pltpu.VMEM)] * len(pieces),
        out_specs=[pl.BlockSpec(memory_space=pl.ANY)] * 2,
        scratch_shapes=[*scratch, pltpu.SemaphoreType.DMA((2, 2 * slabs))],
        compiler_params=pltpu.CompilerParams(vmem_limit_bytes=vmem_bytes(scratch)),
        name="place",
    )(index, *pieces)


def per_device(inputs, pre_first, occupancy, grad_out, w_first, w_second):
    width, ny, zs, chans = inputs.shape
    slabs, bricks = lax.axis_size("slab"), lax.axis_size("brick")
    pairs, nz = bricks // 2, zs * slabs
    cells_all = width * bricks * ny * nz
    scale = 10.0 / cells_all**0.5
    per = -(-27 // (2 * slabs))
    while per * chans % (16 * pairs):
        per += 1
    rows = per * chans // pairs
    slab, brick = lax.axis_index("slab"), lax.axis_index("brick")
    me = lax.rem(brick, 2)
    index = jnp.stack([me, slab * 2 + me, brick // 2, slab]).astype(jnp.int32)

    occ = occupancy[..., None] != 0
    masked = jnp.where(occ, grad_out, jnp.zeros_like(grad_out))
    pre = jnp.where(occ, pre_first, jnp.full_like(pre_first, EMPTY))
    both = jnp.concatenate([masked, pre, inputs], axis=0)
    odd = me == 1
    rim = jnp.concatenate(
        [
            jnp.where(odd, masked[width - 2 :], masked[:2]),
            jnp.where(odd, pre[width - 1 :], pre[:1]),
        ],
        axis=0,
    )

    def swap(b):
        return (b + 1) % bricks if b % 2 else (b - 1) % bricks

    own = over_slabs(both)
    rim_own = jnp.concatenate(over_slabs(rim, swap), axis=0)

    def stacked(kernel):
        return jnp.transpose(kernel, (0, 2, 1)).reshape(27 * chans, chans)

    w_second, w_first, rim_own, own[-1] = lax.optimization_barrier(
        (stacked(w_second), stacked(w_first), rim_own, own[-1])
    )
    other = [partner(v, 1) for v in own]
    rim_other = partner(rim_own, 1)

    shares = [
        jax.ShapeDtypeStruct((pairs // 4, 2 * rows, chans), dtype)
        for dtype in (F32, BF16, BF16, BF16)
    ]
    group = 2 * width * ny * nz
    grad_in, keep, *sent = call(
        functools.partial(group_kernel, slabs, per, scale),
        index,
        [*own, *other, rim_own, rim_other, grad_out, w_second, w_first],
        [jax.ShapeDtypeStruct(inputs.shape, BF16), *shares],
        [
            vmem((3, 2 * width + 4, ny + 2, nz, chans), BF16),
            vmem((3, 2 * width + 2, ny + 2, nz, chans), BF16),
            vmem((group, chans), BF16),
            vmem((per * chans, chans), F32),
        ],
        2 * group * (28 + 2 * per) * chans * chans,
        "group",
    )
    pieces, held = combine(keep, sent, pairs, slabs)
    pieces = [pieces[r, odd] for r in range(slabs) for odd in range(2)]
    pieces += [partner(v, 1) for v in pieces]
    outs = place(slabs, pairs, held, index, pieces, 27 * chans)
    grad_first, grad_second = (out.reshape(27, chans, chans) for out in outs)
    return (grad_in, grad_first, grad_second)


def solution(mesh):
    in_specs = (
        P("brick", None, "slab", None),
        P("brick", None, "slab", None),
        P("brick", None, "slab"),
        P("brick", None, "slab", None),
        P(),
        P(),
    )
    out_specs = (P("brick", None, "slab", None), P(), P())
    return jax.shard_map(
        per_device, mesh=mesh, in_specs=in_specs, out_specs=out_specs, check_vma=False
    )
```

time: 72 us -> 64.9 us (0.901)
  starting transfers between devices: 28.6 us -> 18.5 us
  waiting for transfers between devices: 20.3 us -> 27.8 us
  Pallas kernels: 14.8 us -> 12 us
  local copies, waits for them, and re-layouts: 4.16 us -> 3.2 us
    ppermute x26 -> x18, starting transfers between devices: 28.6 us -> 18.5 us  [send(): return lax.ppermute(value, AXES, pairs)]
    ppermute x26 -> x18, waiting for transfers between devices: 20.3 us -> 27.8 us  [send(): return lax.ppermute(value, AXES, pairs)]
    pallas_call x4 -> x2, Pallas kernels: 14.8 us -> 12 us  [the longest x1 10.2 us: call(): pl.pallas_call(body, out_shape=out_shape, in_specs=[space(v) for v in (in...]
    unnamed x12 -> x6, local copies, waits for them, and re-layouts: 0.91 us -> 0.01 us
  transfers between devices with their start and end apart: 26 -> 18, of which waited for: 14 -> 15; matrix products, arithmetic and copies ran while one was open for 6% -> 5% of each run, Pallas kernels for 6% -> 0%
where the time goes in v2:
time: 64.9 us; the launch traced here: 64.6 us
  waiting for transfers between devices  27.8 us (43%)
  starting transfers between devices  18.5 us (29%)
  Pallas kernels  12 us (18%)
  local copies, waits for them, and re-layouts  3.2 us (5%)
  other arithmetic  2.23 us (3%)
  between operations  0.74 us (1%)
    ppermute x18, waiting for transfers between devices, send(): return lax.ppermute(value, AXES, pairs)  27.8 us
    ppermute x18, starting transfers between devices, send(): return lax.ppermute(value, AXES, pairs)  18.5 us
    pallas_call x1, Pallas kernels, call(): pl.pallas_call(body, out_shape=out_shape, in_specs=[space(v) for v in (in...  10.2 us
    transpose x2, local copies, waits for them, and re-layouts, stacked(): return jnp.transpose(kernel, (0, 2, 1)).reshape(27 * chans, chans)  3.19 us
    pallas_call x1, Pallas kernels, place(): pl.pallas_call(functools.partial(place_kernel, slabs, pairs, held), out_s...  1.82 us
  transfers between devices with their start and end apart: 18, of which 15 were waited for; matrix products, arithmetic and copies ran while one was open for 5% of the time, Pallas kernels for 0%

profile of v2, /device:TPU:0, one launch (start us, length us, event | category | flops | bytes accessed | tf_op | source)
XLA Modules:
  0.0 64.6 jit_solution(1173507816489409647)
XLA Ops:
  0.6 0.8 %broadcast_compare_fusion = pred[4,8,16]{2,1,0:T(8,128)(4,1)S(1)} fusion(s32[4,8,16]{2,1,0:T(8,128)} %param.8), kind=kLoop, calls=%fused_computation.10 | loop fusion | flops 512 | bytes 2560 | tf_op jit(solution)/shard_map/ne | solution.py:270
  1.4 1.2 %broadcast_select_fusion.1 = (bf16[4,8,16,128]{3,2,1,0:T(8,128)(2,1)S(1)}, bf16[4,8,16,128]{3,2,1,0:T(8,128)(2,1)S(1)}) fusion(bf16[4,8,16,128]{3,2,1,0:T(8,128)(2,1)} %refs_6_.1, pred[4,8,16]{2,1,0:T(8,128)(4,1)S(1)} %broadcast_compare_fusion, bf16[4,8,16,128]{3,2,1,0:T(8,128)(2,1)} %param.7), kind=kLoop, calls=%fused_computation.6 | loop fusion | flops 131072 | bytes 524800 | tf_op jit(solution)/shard_map/jit(_where)/select_n | solution.py:271
  2.7 3.0 %collective-permute-start.2 = (bf16[12,8,16,128]{3,2,1,0:T(8,128)(2,1)S(1)}, bf16[12,8,16,128]{3,2,1,0:T(8,128)(2,1)S(1)}, u32[]{:S(2)}, u32[]{:S(2)}) collective-permute-start(bf16[12,8,16,128]{3,2,1,0:T(8,128)(2,1)S(1)} %pad_maximum_fusion.refs_0_), channel_id=1, source_target_pairs={{16,0},{17,1},{18,2},{19,3},{20,4},{21,5},{22,6},{23,7},{24,8},{25... | collective-permute-start | bytes 1179656 | tf_op jit(solution)/shard_map/ppermute | solution.py:25
  5.7 3.7 %collective-permute-start.1 = (bf16[3,8,16,128]{3,2,1,0:T(8,128)(2,1)S(1)}, bf16[3,8,16,128]{3,2,1,0:T(8,128)(2,1)S(1)}, u32[]{:S(2)}, u32[]{:S(2)}) collective-permute-start(bf16[3,8,16,128]{3,2,1,0:T(8,128)(2,1)S(1)} %pad_maximum_fusion.3), channel_id=1, source_target_pairs={{31,0},{18,1},{17,2},{20,3},{19,4},{22,5},{21,6},{24,7},{23,8},{26... | collective-permute-start | bytes 294920 | tf_op jit(solution)/shard_map/ppermute | solution.py:25
  9.7 1.3 %copy.10 = bf16[27,128,128]{2,1,0:T(8,128)(2,1)S(1)} copy(bf16[27,128,128]{1,2,0:T(8,128)(2,1)S(1)} %bitcast.12) | data formatting | bytes 1769472 | tf_op jit(solution)/shard_map/transpose | solution.py:290
  11.0 1.9 %copy.9 = bf16[27,128,128]{2,1,0:T(8,128)(2,1)S(1)} copy(bf16[27,128,128]{1,2,0:T(8,128)(2,1)} %bitcast.13) | data formatting | bytes 1769472 | tf_op jit(solution)/shard_map/transpose | solution.py:290
  13.6 2.6 %collective-permute-done = bf16[3,8,16,128]{3,2,1,0:T(8,128)(2,1)S(1)} collective-permute-done((bf16[3,8,16,128]{3,2,1,0:T(8,128)(2,1)S(1)}, bf16[3,8,16,128]{3,2,1,0:T(8,128)(2,1)S(1)}, u32[]{:S(2)}, u32[]{:S(2)}) %collective-permute-start) | collective-permute-done | bytes 98336 | tf_op jit(solution)/shard_map/ppermute | solution.py:25
  16.2 0.7 %collective-permute-done.2.refs_1_ = bf16[12,8,16,128]{3,2,1,0:T(8,128)(2,1)S(1)} collective-permute-done((bf16[12,8,16,128]{3,2,1,0:T(8,128)(2,1)S(1)}, bf16[12,8,16,128]{3,2,1,0:T(8,128)(2,1)S(1)}, u32[]{:S(2)}, u32[]{:S(2)}) %collective-permute-start.2) | collective-permute-done | bytes 393248 | tf_op jit(solution)/shard_map/ppermute | solution.py:25
  17.5 1.2 %collective-permute-done.5.refs_5_ = bf16[6,8,16,128]{3,2,1,0:T(8,128)(2,1)S(1)} collective-permute-done((bf16[6,8,16,128]{3,2,1,0:T(8,128)(2,1)S(1)}, bf16[6,8,16,128]{3,2,1,0:T(8,128)(2,1)S(1)}, u32[]{:S(2)}, u32[]{:S(2)}) %collective-permute-start.5) | collective-permute-done | bytes 196640 | tf_op jit(solution)/shard_map/ppermute | solution.py:25
  19.0 10.2 %group.1 = (bf16[4,8,16,128]{3,2,1,0:T(8,128)(2,1)}, f32[2,224,128]{2,1,0:T(8,128)S(1)}, bf16[2,224,128]{2,1,0:T(8,128)(2,1)S(1)}, bf16[2,224,128]{2,1,0:T(8,128)(2,1)S(1)}, bf16[2,224,128]{2,1,0:T(8,128)(2,1)S(1)}) custom-call(s32[4]{0:T(128)S(1)} %pad_add_fusion.index_ref, bf16[12,8,16,128]{3,2,1,0:T(8,128)(2,1)S(1)} %pad_maximum_fusion.refs_0_, ...), custom_call_target="tpu_custom_call" | custom-call | flops 2818572288 | bytes 4194304 | tf_op jit(solution)/shard_map/group/pallas_call | solution.py:169
  29.3 1.7 %collective-permute-start.6 = (bf16[2,224,128]{2,1,0:T(8,128)(2,1)S(1)}, bf16[2,224,128]{2,1,0:T(8,128)(2,1)S(1)}, u32[]{:S(2)}, u32[]{:S(2)}) collective-permute-start(bf16[2,224,128]{2,1,0:T(8,128)(2,1)S(1)} %get-tuple-element.20), channel_id=1, source_target_pairs={{2,0},{3,1},{0,2},{1,3},{6,4},{7,5},{4,6},{5,7},{10,8},{11,9},{8,1... | collective-permute-start | bytes 344072 | tf_op jit(solution)/shard_map/ppermute | solution.py:25
  31.0 1.6 %collective-permute-start.7 = (bf16[2,224,128]{2,1,0:T(8,128)(2,1)S(1)}, bf16[2,224,128]{2,1,0:T(8,128)(2,1)S(1)}, u32[]{:S(2)}, u32[]{:S(2)}) collective-permute-start(bf16[2,224,128]{2,1,0:T(8,128)(2,1)S(1)} %get-tuple-element.21), channel_id=1, source_target_pairs={{4,0},{5,1},{6,2},{7,3},{0,4},{1,5},{2,6},{3,7},{12,8},{13,9},{14,... | collective-permute-start | bytes 344072 | tf_op jit(solution)/shard_map/ppermute | solution.py:25
  32.8 1.7 %collective-permute-done.6 = bf16[2,224,128]{2,1,0:T(8,128)(2,1)S(1)} collective-permute-done((bf16[2,224,128]{2,1,0:T(8,128)(2,1)S(1)}, bf16[2,224,128]{2,1,0:T(8,128)(2,1)S(1)}, u32[]{:S(2)}, u32[]{:S(2)}) %collective-permute-start.6) | collective-permute-done | bytes 114720 | tf_op jit(solution)/shard_map/ppermute | solution.py:25
  34.4 2.5 %collective-permute-done.7 = bf16[2,224,128]{2,1,0:T(8,128)(2,1)S(1)} collective-permute-done((bf16[2,224,128]{2,1,0:T(8,128)(2,1)S(1)}, bf16[2,224,128]{2,1,0:T(8,128)(2,1)S(1)}, u32[]{:S(2)}, u32[]{:S(2)}) %collective-permute-start.7) | collective-permute-done | bytes 114720 | tf_op jit(solution)/shard_map/ppermute | solution.py:25
  37.0 1.2 %collective-permute-done.8 = bf16[2,224,128]{2,1,0:T(8,128)(2,1)S(1)} collective-permute-done((bf16[2,224,128]{2,1,0:T(8,128)(2,1)S(1)}, bf16[2,224,128]{2,1,0:T(8,128)(2,1)S(1)}, u32[]{:S(2)}, u32[]{:S(2)}) %collective-permute-start.8) | collective-permute-done | bytes 114720 | tf_op jit(solution)/shard_map/ppermute | solution.py:25
  38.3 2.7 %collective-permute-start.9 = (bf16[2,224,128]{2,1,0:T(8,128)(2,1)S(1)}, bf16[2,224,128]{2,1,0:T(8,128)(2,1)S(1)}, u32[]{:S(2)}, u32[]{:S(2)}) collective-permute-start(bf16[2,224,128]{2,1,0:T(8,128)(2,1)S(1)} %reduce-precision_convert_fusion), channel_id=1, source_target_pairs={{8,0},{9,1},{10,2},{11,3},{12,4},{13,5},{14,6},{15,7},{0,8},{1,9},... | collective-permute-start | bytes 344072 | tf_op jit(solution)/shard_map/ppermute | solution.py:25
  41.0 4.7 %collective-permute-done.9 = bf16[2,224,128]{2,1,0:T(8,128)(2,1)S(1)} collective-permute-done((bf16[2,224,128]{2,1,0:T(8,128)(2,1)S(1)}, bf16[2,224,128]{2,1,0:T(8,128)(2,1)S(1)}, u32[]{:S(2)}, u32[]{:S(2)}) %collective-permute-start.9) | collective-permute-done | bytes 114720 | tf_op jit(solution)/shard_map/ppermute | solution.py:25
  45.7 0.8 %collective-permute-start.10 = (bf16[2,224,128]{2,1,0:T(8,128)(2,1)S(1)}, bf16[2,224,128]{2,1,0:T(8,128)(2,1)S(1)}, u32[]{:S(2)}, u32[]{:S(2)}) collective-permute-start(bf16[2,224,128]{2,1,0:T(8,128)(2,1)S(1)} %add_convert_fusion), channel_id=1, source_target_pairs={{4,0},{5,1},{6,2},{7,3},{0,4},{1,5},{2,6},{3,7},{12,8},{13,9},{14,... | collective-permute-start | bytes 344072 | tf_op jit(solution)/shard_map/ppermute | solution.py:25
  46.5 4.1 %collective-permute-done.10 = bf16[2,224,128]{2,1,0:T(8,128)(2,1)S(1)} collective-permute-done((bf16[2,224,128]{2,1,0:T(8,128)(2,1)S(1)}, bf16[2,224,128]{2,1,0:T(8,128)(2,1)S(1)}, u32[]{:S(2)}, u32[]{:S(2)}) %collective-permute-start.10) | collective-permute-done | bytes 114720 | tf_op jit(solution)/shard_map/ppermute | solution.py:25
  50.6 2.7 %collective-permute-start.13 = (bf16[4,224,128]{2,1,0:T(8,128)(2,1)S(1)}, bf16[4,224,128]{2,1,0:T(8,128)(2,1)S(1)}, u32[]{:S(2)}, u32[]{:S(2)}) collective-permute-start(bf16[4,224,128]{2,1,0:T(8,128)(2,1)S(1)} %pad_maximum_fusion.1.refs_0_), channel_id=1, source_target_pairs={{18,0},{19,1},{16,2},{17,3},{22,4},{23,5},{20,6},{21,7},{26,8},{27... | collective-permute-start | bytes 688136 | tf_op jit(solution)/shard_map/ppermute | solution.py:25
  54.2 4.5 %collective-permute-done.13.refs_3_ = bf16[4,224,128]{2,1,0:T(8,128)(2,1)S(1)} collective-permute-done((bf16[4,224,128]{2,1,0:T(8,128)(2,1)S(1)}, bf16[4,224,128]{2,1,0:T(8,128)(2,1)S(1)}, u32[]{:S(2)}, u32[]{:S(2)}) %collective-permute-start.13) | collective-permute-done | bytes 229408 | tf_op jit(solution)/shard_map/ppermute | solution.py:25
  58.7 2.3 %collective-permute-done.12.refs_2_ = bf16[4,224,128]{2,1,0:T(8,128)(2,1)S(1)} collective-permute-done((bf16[4,224,128]{2,1,0:T(8,128)(2,1)S(1)}, bf16[4,224,128]{2,1,0:T(8,128)(2,1)S(1)}, u32[]{:S(2)}, u32[]{:S(2)}) %collective-permute-start.12) | collective-permute-done | bytes 229408 | tf_op jit(solution)/shard_map/ppermute | solution.py:25
  61.5 1.0 %collective-permute-done.16.refs_6_ = bf16[4,224,128]{2,1,0:T(8,128)(2,1)S(1)} collective-permute-done((bf16[4,224,128]{2,1,0:T(8,128)(2,1)S(1)}, bf16[4,224,128]{2,1,0:T(8,128)(2,1)S(1)}, u32[]{:S(2)}, u32[]{:S(2)}) %collective-permute-start.16) | collective-permute-done | bytes 229408 | tf_op jit(solution)/shard_map/ppermute | solution.py:25
  62.8 1.8 %place.1 = (bf16[3456,128]{1,0:T(8,128)(2,1)}, bf16[3456,128]{1,0:T(8,128)(2,1)}) custom-call(s32[4]{0:T(128)S(1)} %pad_add_fusion.index_ref, bf16[4,224,128]{2,1,0:T(8,128)(2,1)S(1)} %pad_maximum_fusion.1.refs_0_, bf16[4,224,128]{2,1,0:T(8,128)(2,1)S(1)} %collective-permute-done.11.refs_1_, bf16[4,224,128]{2,1,0:T(8,128)(2,1)S(1)} %collective-permute-done.12.refs_2_, ...), custom_call_target="tpu_custom_call" | custom-call | tf_op jit(solution)/shard_map/place/pallas_call | solution.py:244
  (33 shorter events, 4.1 us)
Async XLA Ops:
  0.6 2.0 %copy-start.2 = (bf16[4,8,16,128]{3,2,1,0:T(8,128)(2,1)S(1)}, bf16[4,8,16,128]{3,2,1,0:T(8,128)(2,1)}, u32[]{:S(2)}) copy-start(bf16[4,8,16,128]{3,2,1,0:T(8,128)(2,1)} %param.6) | copy-start | bytes 393220
  1.4 8.3 %copy-start.1 = (bf16[27,128,128]{2,1,0:T(8,128)(2,1)S(1)}, bf16[27,128,128]{2,1,0:T(8,128)(2,1)}, u32[]{:S(2)}) copy-start(bf16[27,128,128]{2,1,0:T(8,128)(2,1)} %param.10) | copy-start | bytes 2654212
  2.7 14.3 %collective-permute-start.2 = (bf16[12,8,16,128]{3,2,1,0:T(8,128)(2,1)S(1)}, bf16[12,8,16,128]{3,2,1,0:T(8,128)(2,1)S(1)}, u32[]{:S(2)}, u32[]{:S(2)}) collective-permute-start(bf16[12,8,16,128]{3,2,1,0:T(8,128)(2,1)S(1)} %pad_maximum_fusion.refs_0_), channel_id=1, source_target_pairs={{16,0},{17,1},{18,2},{19,3},{20,4},{21,5},{22,6},{23,7},{24,8},{25... | collective-permute-start | bytes 1179656 | tf_op jit(solution)/shard_map/ppermute | solution.py:25
  5.7 7.9 %collective-permute-start.1 = (bf16[3,8,16,128]{3,2,1,0:T(8,128)(2,1)S(1)}, bf16[3,8,16,128]{3,2,1,0:T(8,128)(2,1)S(1)}, u32[]{:S(2)}, u32[]{:S(2)}) collective-permute-start(bf16[3,8,16,128]{3,2,1,0:T(8,128)(2,1)S(1)} %pad_maximum_fusion.3), channel_id=1, source_target_pairs={{31,0},{18,1},{17,2},{20,3},{19,4},{22,5},{21,6},{24,7},{23,8},{26... | collective-permute-start | bytes 294920 | tf_op jit(solution)/shard_map/ppermute | solution.py:25
  9.4 6.7 %collective-permute-start = (bf16[3,8,16,128]{3,2,1,0:T(8,128)(2,1)S(1)}, bf16[3,8,16,128]{3,2,1,0:T(8,128)(2,1)S(1)}, u32[]{:S(2)}, u32[]{:S(2)}) collective-permute-start(bf16[3,8,16,128]{3,2,1,0:T(8,128)(2,1)S(1)} %pad_maximum_fusion.3), channel_id=1, source_target_pairs={{15,0},{2,1},{1,2},{4,3},{3,4},{6,5},{5,6},{8,7},{7,8},{10,9},{9,1... | collective-permute-start | bytes 294920 | tf_op jit(solution)/shard_map/ppermute | solution.py:25
  9.7 7.8 %collective-permute-start.3 = (bf16[12,8,16,128]{3,2,1,0:T(8,128)(2,1)S(1)}, bf16[12,8,16,128]{3,2,1,0:T(8,128)(2,1)S(1)}, u32[]{:S(2)}, u32[]{:S(2)}) collective-permute-start(bf16[12,8,16,128]{3,2,1,0:T(8,128)(2,1)S(1)} %pad_maximum_fusion.refs_0_), channel_id=1, source_target_pairs={{1,0},{0,1},{3,2},{2,3},{5,4},{4,5},{7,6},{6,7},{9,8},{8,9},{11,10... | collective-permute-start | bytes 1179656 | tf_op jit(solution)/shard_map/ppermute | solution.py:25
  12.9 6.1 %copy-start = (bf16[4,8,16,128]{3,2,1,0:T(8,128)(2,1)S(1)}, bf16[4,8,16,128]{3,2,1,0:T(8,128)(2,1)}, u32[]{:S(2)}) copy-start(bf16[4,8,16,128]{3,2,1,0:T(8,128)(2,1)} %refs_6_.1) | copy-start | bytes 393220
  16.9 2.1 %collective-permute-start.4 = (bf16[12,8,16,128]{3,2,1,0:T(8,128)(2,1)S(1)}, bf16[12,8,16,128]{3,2,1,0:T(8,128)(2,1)}, u32[]{:S(2)}, u32[]{:S(2)}) collective-permute-start(bf16[12,8,16,128]{3,2,1,0:T(8,128)(2,1)S(1)} %collective-permute-done.2.refs_1_), channel_id=1, source_target_pairs={{1,0},{0,1},{3,2},{2,3},{5,4},{4,5},{7,6},{6,7},{9,8},{8,9},{11,10... | collective-permute-start | bytes 1179656 | tf_op jit(solution)/shard_map/ppermute | solution.py:25
  16.9 1.8 %collective-permute-start.5 = (bf16[6,8,16,128]{3,2,1,0:T(8,128)(2,1)S(1)}, bf16[6,8,16,128]{3,2,1,0:T(8,128)(2,1)S(1)}, u32[]{:S(2)}, u32[]{:S(2)}) collective-permute-start(bf16[6,8,16,128]{3,2,1,0:T(8,128)(2,1)S(1)} %pad_maximum_fusion.2.refs_4_), channel_id=1, source_target_pairs={{1,0},{0,1},{3,2},{2,3},{5,4},{4,5},{7,6},{6,7},{9,8},{8,9},{11,10... | collective-permute-start | bytes 589832 | tf_op jit(solution)/shard_map/ppermute | solution.py:25
  29.3 5.2 %collective-permute-start.6 = (bf16[2,224,128]{2,1,0:T(8,128)(2,1)S(1)}, bf16[2,224,128]{2,1,0:T(8,128)(2,1)S(1)}, u32[]{:S(2)}, u32[]{:S(2)}) collective-permute-start(bf16[2,224,128]{2,1,0:T(8,128)(2,1)S(1)} %get-tuple-element.20), channel_id=1, source_target_pairs={{2,0},{3,1},{0,2},{1,3},{6,4},{7,5},{4,6},{5,7},{10,8},{11,9},{8,1... | collective-permute-start | bytes 344072 | tf_op jit(solution)/shard_map/ppermute | solution.py:25
  31.0 6.0 %collective-permute-start.7 = (bf16[2,224,128]{2,1,0:T(8,128)(2,1)S(1)}, bf16[2,224,128]{2,1,0:T(8,128)(2,1)S(1)}, u32[]{:S(2)}, u32[]{:S(2)}) collective-permute-start(bf16[2,224,128]{2,1,0:T(8,128)(2,1)S(1)} %get-tuple-element.21), channel_id=1, source_target_pairs={{4,0},{5,1},{6,2},{7,3},{0,4},{1,5},{2,6},{3,7},{12,8},{13,9},{14,... | collective-permute-start | bytes 344072 | tf_op jit(solution)/shard_map/ppermute | solution.py:25
  32.5 5.7 %collective-permute-start.8 = (bf16[2,224,128]{2,1,0:T(8,128)(2,1)S(1)}, bf16[2,224,128]{2,1,0:T(8,128)(2,1)S(1)}, u32[]{:S(2)}, u32[]{:S(2)}) collective-permute-start(bf16[2,224,128]{2,1,0:T(8,128)(2,1)S(1)} %get-tuple-element.22), channel_id=1, source_target_pairs={{6,0},{7,1},{4,2},{5,3},{2,4},{3,5},{0,6},{1,7},{14,8},{15,9},{12,... | collective-permute-start | bytes 344072 | tf_op jit(solution)/shard_map/ppermute | solution.py:25
  38.3 7.4 %collective-permute-start.9 = (bf16[2,224,128]{2,1,0:T(8,128)(2,1)S(1)}, bf16[2,224,128]{2,1,0:T(8,128)(2,1)S(1)}, u32[]{:S(2)}, u32[]{:S(2)}) collective-permute-start(bf16[2,224,128]{2,1,0:T(8,128)(2,1)S(1)} %reduce-precision_convert_fusion), channel_id=1, source_target_pairs={{8,0},{9,1},{10,2},{11,3},{12,4},{13,5},{14,6},{15,7},{0,8},{1,9},... | collective-permute-start | bytes 344072 | tf_op jit(solution)/shard_map/ppermute | solution.py:25
  45.7 4.9 %collective-permute-start.10 = (bf16[2,224,128]{2,1,0:T(8,128)(2,1)S(1)}, bf16[2,224,128]{2,1,0:T(8,128)(2,1)S(1)}, u32[]{:S(2)}, u32[]{:S(2)}) collective-permute-start(bf16[2,224,128]{2,1,0:T(8,128)(2,1)S(1)} %add_convert_fusion), channel_id=1, source_target_pairs={{4,0},{5,1},{6,2},{7,3},{0,4},{1,5},{2,6},{3,7},{12,8},{13,9},{14,... | collective-permute-start | bytes 344072 | tf_op jit(solution)/shard_map/ppermute | solution.py:25
  50.6 8.1 %collective-permute-start.13 = (bf16[4,224,128]{2,1,0:T(8,128)(2,1)S(1)}, bf16[4,224,128]{2,1,0:T(8,128)(2,1)S(1)}, u32[]{:S(2)}, u32[]{:S(2)}) collective-permute-start(bf16[4,224,128]{2,1,0:T(8,128)(2,1)S(1)} %pad_maximum_fusion.1.refs_0_), channel_id=1, source_target_pairs={{18,0},{19,1},{16,2},{17,3},{22,4},{23,5},{20,6},{21,7},{26,8},{27... | collective-permute-start | bytes 688136 | tf_op jit(solution)/shard_map/ppermute | solution.py:25
  53.3 7.7 %collective-permute-start.12 = (bf16[4,224,128]{2,1,0:T(8,128)(2,1)S(1)}, bf16[4,224,128]{2,1,0:T(8,128)(2,1)S(1)}, u32[]{:S(2)}, u32[]{:S(2)}) collective-permute-start(bf16[4,224,128]{2,1,0:T(8,128)(2,1)S(1)} %pad_maximum_fusion.1.refs_0_), channel_id=1, source_target_pairs={{16,0},{17,1},{18,2},{19,3},{20,4},{21,5},{22,6},{23,7},{24,8},{25... | collective-permute-start | bytes 688136 | tf_op jit(solution)/shard_map/ppermute | solution.py:25
  53.8 7.2 %collective-permute-start.11 = (bf16[4,224,128]{2,1,0:T(8,128)(2,1)S(1)}, bf16[4,224,128]{2,1,0:T(8,128)(2,1)S(1)}, u32[]{:S(2)}, u32[]{:S(2)}) collective-permute-start(bf16[4,224,128]{2,1,0:T(8,128)(2,1)S(1)} %pad_maximum_fusion.1.refs_0_), channel_id=1, source_target_pairs={{2,0},{3,1},{0,2},{1,3},{6,4},{7,5},{4,6},{5,7},{10,8},{11,9},{8,1... | collective-permute-start | bytes 688136 | tf_op jit(solution)/shard_map/ppermute | solution.py:25
  54.2 7.3 %collective-permute-start.14 = (bf16[4,224,128]{2,1,0:T(8,128)(2,1)S(1)}, bf16[4,224,128]{2,1,0:T(8,128)(2,1)S(1)}, u32[]{:S(2)}, u32[]{:S(2)}) collective-permute-start(bf16[4,224,128]{2,1,0:T(8,128)(2,1)S(1)} %pad_maximum_fusion.1.refs_0_), channel_id=1, source_target_pairs={{1,0},{0,1},{3,2},{2,3},{5,4},{4,5},{7,6},{6,7},{9,8},{8,9},{11,10... | collective-permute-start | bytes 688136 | tf_op jit(solution)/shard_map/ppermute | solution.py:25
  58.7 2.8 %collective-permute-start.17 = (bf16[4,224,128]{2,1,0:T(8,128)(2,1)S(1)}, bf16[4,224,128]{2,1,0:T(8,128)(2,1)S(1)}, u32[]{:S(2)}, u32[]{:S(2)}) collective-permute-start(bf16[4,224,128]{2,1,0:T(8,128)(2,1)S(1)} %collective-permute-done.13.refs_3_), channel_id=1, source_target_pairs={{1,0},{0,1},{3,2},{2,3},{5,4},{4,5},{7,6},{6,7},{9,8},{8,9},{11,10... | collective-permute-start | bytes 688136 | tf_op jit(solution)/shard_map/ppermute | solution.py:25
  60.9 1.5 %collective-permute-start.16 = (bf16[4,224,128]{2,1,0:T(8,128)(2,1)S(1)}, bf16[4,224,128]{2,1,0:T(8,128)(2,1)S(1)}, u32[]{:S(2)}, u32[]{:S(2)}) collective-permute-start(bf16[4,224,128]{2,1,0:T(8,128)(2,1)S(1)} %collective-permute-done.12.refs_2_), channel_id=1, source_target_pairs={{1,0},{0,1},{3,2},{2,3},{5,4},{4,5},{7,6},{6,7},{9,8},{8,9},{11,10... | collective-permute-start | bytes 688136 | tf_op jit(solution)/shard_map/ppermute | solution.py:25
  61.0 1.8 %collective-permute-start.15 = (bf16[4,224,128]{2,1,0:T(8,128)(2,1)S(1)}, bf16[4,224,128]{2,1,0:T(8,128)(2,1)S(1)}, u32[]{:S(2)}, u32[]{:S(2)}) collective-permute-start(bf16[4,224,128]{2,1,0:T(8,128)(2,1)S(1)} %collective-permute-done.11.refs_1_), channel_id=1, source_target_pairs={{1,0},{0,1},{3,2},{2,3},{5,4},{4,5},{7,6},{6,7},{9,8},{8,9},{11,10... | collective-permute-start | bytes 688136 | tf_op jit(solution)/shard_map/ppermute | solution.py:25

commit v3 on v2

--- a/solution.py
+++ b/solution.py
@@ -81,14 +81,21 @@
 
 def kernel_terms(left_ref, field_ref, start, planes, nz, scratch_ref, index_ref, per, scale):
     chans = left_ref.shape[-1]
-    for j in range(per):
+
+    def step(j):
         k = jnp.minimum(index_ref[1] * per + j, 26)
         a, b, c = k // 9 - 1, (k // 3) % 3 - 1, k % 3 - 1
         cols = shifted(field_ref, a, b, c, start, planes, nz)
         term = lax.dot_general(
             left_ref[...], cols, (((0,), (0,)), ((), ())), preferred_element_type=F32
         )
-        scratch_ref[pl.ds(j * chans, chans), :] = term * scale
+        scratch_ref[pl.ds(pl.multiple_of(j * chans, chans), chans), :] = term * scale
+
+    if left_ref.shape[0] <= 2048:
+        for j in range(per):
+            step(j)
+    else:
+        lax.fori_loop(0, per, lambda j, carry: (step(j), carry)[1], 0)
 
 
 def put_chunks(scratch_ref, keep_ref, sent_refs, me, tensor):
@@ -106,49 +113,84 @@
         [ref.at[pl.ds(3 * r, 3)] for r in range(slabs)] for ref in refs[2 * slabs : 2 * slabs + 2]
     )
     grad_out_ref, w_second_ref, w_first_ref, grad_in_ref, keep_ref, *refs = refs[2 * slabs + 2 :]
-    *sent_refs, field_ref, first_ref, left_ref, scratch_ref = refs
+    *sent_refs, field_ref, first_ref, pre_ref, left_ref, parts_ref, wide_ref, scratch_ref = refs
     me, pair = index_ref[0], index_ref[2]
     width, (ny, zs, chans) = own[0].shape[0] // 3, own[0].shape[1:]
     nz = zs * slabs
+    unrolled = ny * nz <= 256
     fill_second(field_ref, own, other, rim_own, rim_other, me)
 
-    def fill_left(plane):
-        for i in range(width):
-            for refs_of, who in ((own, me), (other, 1 - me)):
-                rows = plane(refs_of, i).astype(BF16).reshape(ny * nz, chans)
-                at = pl.multiple_of((who * width + i) * ny * nz, ny * nz)
-                left_ref[pl.ds(at, ny * nz), :] = rows
-
-    def conv(ref, start, planes, depth, w_ref):
+    def products(ref, start, depth, w_ref):
         cols = jnp.concatenate(
-            [shifted(ref, a, b, c, start, planes, depth) for a, b, c in OFFSETS], axis=1
+            [shifted(ref, 0, b, c, start, 1, depth) for _, b, c in OFFSETS[:9]], axis=1
         )
-        out = jnp.dot(cols, w_ref[...], preferred_element_type=F32)
-        return out.reshape(planes, ny, depth, chans)
-
-    def put_first(at, pre):
-        grad_act = conv(field_ref, at + 1, pre.shape[0], nz, w_second_ref)
+        return lax.dot_general(
+            cols, w_ref[...], (((1,), (1,)), ((), ())), preferred_element_type=F32
+        )
+
+    def conv(ref, start, planes, depth, w_ref, put):
+        def out(i, part):
+            total = sum(part(i - 1 - a)[:, (a + 1) * chans : (a + 2) * chans] for a in (-1, 0, 1))
+            put(i - 2, total.reshape(1, ny, depth, chans))
+
+        if unrolled:
+            parts = []
+            for i in range(planes + 2):
+                parts.append(products(ref, start - 1 + i, depth, w_ref))
+                if i >= 2:
+                    out(i, parts.__getitem__)
+            return
+
+        rows = pl.ds(0, ny * depth)
+
+        def step(i, carry):
+            parts_ref[i % 3, rows] = products(ref, start - 1 + i, depth, w_ref)
+            pl.when(i >= 2)(lambda: out(i, lambda j: parts_ref[(j + 3) % 3, rows]))
+            return carry
+
+        lax.fori_loop(0, planes + 2, step, 0)
+
+    def pre_of(i):
+        return pre_ref[pl.ds(i, 1)]
+
+    def put_pre(refs_of, i, at):
+        pre_ref[pl.ds(at, 1)] = joined(refs_of, i, 1)
+
+    for i in range(width):
+        put_pre(own, width + i, 1 + width * me + i)
+        put_pre(other, width + i, 1 + width * (1 - me) + i)
+    put_pre(rim_own, 2, (1 + 2 * width) * me)
+    put_pre(rim_other, 2, (1 + 2 * width) * (1 - me))
+
+    def put_first(i, grad_act):
+        pre = pre_of(i)
         sig = sigmoid(pre)
-        put_planes(first_ref, at, grad_act * (sig * (1.0 + pre * (1.0 - sig))))
-
-    for i in range(0, width, 2):
-        put_first(1 + width * me + i, joined(own, width + i, 2))
-        put_first(1 + width * (1 - me) + i, joined(other, width + i, 2))
-    put_first((1 + 2 * width) * me, joined(rim_own, 2, 1))
-    put_first((1 + 2 * width) * (1 - me), joined(rim_other, 2, 1))
-
-    back = conv(first_ref, 1 + width * me, width, zs, w_first_ref)
-    grad_in_ref[...] = (grad_out_ref[...].astype(F32) + back).astype(BF16)
-
-    fill_left(lambda refs_of, i: joined(refs_of, 2 * width + i, 1))
+        put_planes(first_ref, i, grad_act * (sig * (1.0 + pre * (1.0 - sig))))
+
+    def put_grad_in(i, back):
+        grad_in_ref[pl.ds(i, 1)] = (grad_out_ref[pl.ds(i, 1)].astype(F32) + back).astype(BF16)
+
+    def widened(w_ref):
+        for k in range(27):
+            a, bc = divmod(k, 9)
+            wide_ref[pl.ds(a * chans, chans), pl.ds(bc * chans, chans)] = w_ref[k]
+        return wide_ref
+
+    conv(field_ref, 1, 2 * width + 2, nz, widened(w_second_ref), put_first)
+    conv(first_ref, 1 + width * me, width, zs, widened(w_first_ref), put_grad_in)
+
+    for i in range(width):
+        for refs_of, who in ((own, me), (other, 1 - me)):
+            rows = joined(refs_of, 2 * width + i, 1).astype(BF16).reshape(ny * nz, chans)
+            at = pl.multiple_of((who * width + i) * ny * nz, ny * nz)
+            left_ref[pl.ds(at, ny * nz), :] = rows
     kernel_terms(left_ref, first_ref, 1, 2 * width, nz, scratch_ref, index_ref, per, scale)
     put_chunks(scratch_ref, keep_ref, sent_refs, pair, 0)
 
-    def act(refs_of, i):
-        pre = joined(refs_of, width + i, 1)
-        return pre * sigmoid(pre)
-
-    fill_left(act)
+    for i in range(2 * width):
+        pre = pre_of(1 + i)
+        act = (pre * sigmoid(pre)).astype(BF16)
+        left_ref[pl.ds(i * ny * nz, ny * nz), :] = act.reshape(ny * nz, chans)
     kernel_terms(left_ref, field_ref, 2, 2 * width, nz, scratch_ref, index_ref, per, scale)
     put_chunks(scratch_ref, keep_ref, sent_refs, pair, 1)
 
@@ -286,12 +328,7 @@
     own = over_slabs(both)
     rim_own = jnp.concatenate(over_slabs(rim, swap), axis=0)
 
-    def stacked(kernel):
-        return jnp.transpose(kernel, (0, 2, 1)).reshape(27 * chans, chans)
-
-    w_second, w_first, rim_own, own[-1] = lax.optimization_barrier(
-        (stacked(w_second), stacked(w_first), rim_own, own[-1])
-    )
+    rim_own, own[-1] = lax.optimization_barrier((rim_own, own[-1]))
     other = [partner(v, 1) for v in own]
     rim_other = partner(rim_own, 1)
 
@@ -308,7 +345,10 @@
         [
             vmem((3, 2 * width + 4, ny + 2, nz, chans), BF16),
             vmem((3, 2 * width + 2, ny + 2, nz, chans), BF16),
+            vmem((2 * width + 2, ny, nz, chans), F32),
             vmem((group, chans), BF16),
+            vmem((3, ny * nz, 3 * chans), F32),
+            vmem((3 * chans, 9 * chans), BF16),
             vmem((per * chans, chans), F32),
         ],
         2 * group * (28 + 2 * per) * chans * chans,

time: 64.9 us -> 63.6 us (0.980)
  waiting for transfers between devices: 27.8 us -> 31.4 us
  local copies, waits for them, and re-layouts: 3.2 us -> 0.02 us
  Pallas kernels: 12 us -> 10.8 us
    ppermute x18, waiting for transfers between devices: 27.8 us -> 31.4 us  [send(): return lax.ppermute(value, AXES, pairs)]
    transpose x2 -> x0, local copies, waits for them, and re-layouts: 3.19 us -> none  [stacked(): return jnp.transpose(kernel, (0, 2, 1)).reshape(27 * chans, chans)]
    pallas_call x1, Pallas kernels: 10.2 us -> 9 us  [call(): pl.pallas_call(body, out_shape=out_shape, in_specs=[space(v) for v in (in...]
  transfers between devices with their start and end apart: 18 -> 18, of which waited for: 15 -> 15; matrix products, arithmetic and copies ran while one was open for 5% -> 0% of each run, Pallas kernels for 0% -> 0%
where the time goes in v3:
time: 63.6 us; the launch traced here: 63.4 us
  waiting for transfers between devices  31.4 us (49%)
  starting transfers between devices  18.2 us (29%)
  Pallas kernels  10.8 us (17%)
  other arithmetic  2.23 us (4%)
  between operations  0.73 us (1%)
    ppermute x18, waiting for transfers between devices, send(): return lax.ppermute(value, AXES, pairs)  31.4 us
    ppermute x18, starting transfers between devices, send(): return lax.ppermute(value, AXES, pairs)  18.2 us
    pallas_call x1, Pallas kernels, call(): pl.pallas_call(body, out_shape=out_shape, in_specs=[space(v) for v in (in...  9 us
    pallas_call x1, Pallas kernels, place(): pl.pallas_call(functools.partial(place_kernel, slabs, pairs, held), out_s...  1.82 us
  transfers between devices with their start and end apart: 18, of which 15 were waited for; matrix products, arithmetic and copies ran while one was open for 0% of the time, Pallas kernels for 0%

profile of v3, /device:TPU:0, one launch (start us, length us, event | category | flops | bytes accessed | tf_op | source)
XLA Modules:
  0.0 63.4 jit_solution(2674888578354572058)
XLA Ops:
  0.6 0.8 %broadcast_compare_fusion = pred[4,8,16]{2,1,0:T(8,128)(4,1)S(1)} fusion(s32[4,8,16]{2,1,0:T(8,128)} %param.8), kind=kLoop, calls=%fused_computation.10 | loop fusion | flops 512 | bytes 2560 | tf_op jit(solution)/shard_map/ne | solution.py:312
  1.4 1.2 %broadcast_select_fusion.1 = (bf16[4,8,16,128]{3,2,1,0:T(8,128)(2,1)S(1)}, bf16[4,8,16,128]{3,2,1,0:T(8,128)(2,1)S(1)}) fusion(bf16[4,8,16,128]{3,2,1,0:T(8,128)(2,1)} %refs_6_.1, pred[4,8,16]{2,1,0:T(8,128)(4,1)S(1)} %broadcast_compare_fusion, bf16[4,8,16,128]{3,2,1,0:T(8,128)(2,1)} %param.7), kind=kLoop, calls=%fused_computation.6 | loop fusion | flops 131072 | bytes 524800 | tf_op jit(solution)/shard_map/jit(_where)/select_n | solution.py:313
  2.7 3.0 %collective-permute-start.2 = (bf16[12,8,16,128]{3,2,1,0:T(8,128)(2,1)S(1)}, bf16[12,8,16,128]{3,2,1,0:T(8,128)(2,1)S(1)}, u32[]{:S(2)}, u32[]{:S(2)}) collective-permute-start(bf16[12,8,16,128]{3,2,1,0:T(8,128)(2,1)S(1)} %pad_maximum_fusion.refs_0_), channel_id=1, source_target_pairs={{16,0},{17,1},{18,2},{19,3},{20,4},{21,5},{22,6},{23,7},{24,8},{25... | collective-permute-start | bytes 1179656 | tf_op jit(solution)/shard_map/ppermute | solution.py:25
  5.8 3.7 %collective-permute-start.1 = (bf16[3,8,16,128]{3,2,1,0:T(8,128)(2,1)S(1)}, bf16[3,8,16,128]{3,2,1,0:T(8,128)(2,1)S(1)}, u32[]{:S(2)}, u32[]{:S(2)}) collective-permute-start(bf16[3,8,16,128]{3,2,1,0:T(8,128)(2,1)S(1)} %pad_maximum_fusion.3), channel_id=1, source_target_pairs={{31,0},{18,1},{17,2},{20,3},{19,4},{22,5},{21,6},{24,7},{23,8},{26... | collective-permute-start | bytes 294920 | tf_op jit(solution)/shard_map/ppermute | solution.py:25
  9.7 3.9 %collective-permute-done.1 = bf16[3,8,16,128]{3,2,1,0:T(8,128)(2,1)S(1)} collective-permute-done((bf16[3,8,16,128]{3,2,1,0:T(8,128)(2,1)S(1)}, bf16[3,8,16,128]{3,2,1,0:T(8,128)(2,1)S(1)}, u32[]{:S(2)}, u32[]{:S(2)}) %collective-permute-start.1) | collective-permute-done | bytes 98336 | tf_op jit(solution)/shard_map/ppermute | solution.py:25
  13.6 2.6 %collective-permute-done = bf16[3,8,16,128]{3,2,1,0:T(8,128)(2,1)S(1)} collective-permute-done((bf16[3,8,16,128]{3,2,1,0:T(8,128)(2,1)S(1)}, bf16[3,8,16,128]{3,2,1,0:T(8,128)(2,1)S(1)}, u32[]{:S(2)}, u32[]{:S(2)}) %collective-permute-start) | collective-permute-done | bytes 98336 | tf_op jit(solution)/shard_map/ppermute | solution.py:25
  16.2 0.7 %collective-permute-done.2.refs_1_ = bf16[12,8,16,128]{3,2,1,0:T(8,128)(2,1)S(1)} collective-permute-done((bf16[12,8,16,128]{3,2,1,0:T(8,128)(2,1)S(1)}, bf16[12,8,16,128]{3,2,1,0:T(8,128)(2,1)S(1)}, u32[]{:S(2)}, u32[]{:S(2)}) %collective-permute-start.2) | collective-permute-done | bytes 393248 | tf_op jit(solution)/shard_map/ppermute | solution.py:25
  16.9 0.5 collective-permute-start.5
  17.5 1.2 %collective-permute-done.5.refs_5_ = bf16[6,8,16,128]{3,2,1,0:T(8,128)(2,1)S(1)} collective-permute-done((bf16[6,8,16,128]{3,2,1,0:T(8,128)(2,1)S(1)}, bf16[6,8,16,128]{3,2,1,0:T(8,128)(2,1)S(1)}, u32[]{:S(2)}, u32[]{:S(2)}) %collective-permute-start.5) | collective-permute-done | bytes 196640 | tf_op jit(solution)/shard_map/ppermute | solution.py:25
  19.1 9.0 %group.1 = (bf16[4,8,16,128]{3,2,1,0:T(8,128)(2,1)}, f32[2,224,128]{2,1,0:T(8,128)S(1)}, bf16[2,224,128]{2,1,0:T(8,128)(2,1)S(1)}, bf16[2,224,128]{2,1,0:T(8,128)(2,1)S(1)}, bf16[2,224,128]{2,1,0:T(8,128)(2,1)S(1)}) custom-call(s32[4]{0:T(128)S(1)} %pad_add_fusion.index_ref, bf16[12,8,16,128]{3,2,1,0:T(8,128)(2,1)S(1)} %pad_maximum_fusion.refs_0_, ...), custom_call_target="tpu_custom_call" | custom-call | flops 2818572288 | bytes 4194304 | tf_op jit(solution)/shard_map/group/pallas_call | solution.py:211
  28.1 1.7 %collective-permute-start.6 = (bf16[2,224,128]{2,1,0:T(8,128)(2,1)S(1)}, bf16[2,224,128]{2,1,0:T(8,128)(2,1)S(1)}, u32[]{:S(2)}, u32[]{:S(2)}) collective-permute-start(bf16[2,224,128]{2,1,0:T(8,128)(2,1)S(1)} %get-tuple-element.16), channel_id=1, source_target_pairs={{2,0},{3,1},{0,2},{1,3},{6,4},{7,5},{4,6},{5,7},{10,8},{11,9},{8,1... | collective-permute-start | bytes 344072 | tf_op jit(solution)/shard_map/ppermute | solution.py:25
  29.8 1.6 %collective-permute-start.7 = (bf16[2,224,128]{2,1,0:T(8,128)(2,1)S(1)}, bf16[2,224,128]{2,1,0:T(8,128)(2,1)S(1)}, u32[]{:S(2)}, u32[]{:S(2)}) collective-permute-start(bf16[2,224,128]{2,1,0:T(8,128)(2,1)S(1)} %get-tuple-element.17), channel_id=1, source_target_pairs={{4,0},{5,1},{6,2},{7,3},{0,4},{1,5},{2,6},{3,7},{12,8},{13,9},{14,... | collective-permute-start | bytes 344072 | tf_op jit(solution)/shard_map/ppermute | solution.py:25
  31.6 1.7 %collective-permute-done.6 = bf16[2,224,128]{2,1,0:T(8,128)(2,1)S(1)} collective-permute-done((bf16[2,224,128]{2,1,0:T(8,128)(2,1)S(1)}, bf16[2,224,128]{2,1,0:T(8,128)(2,1)S(1)}, u32[]{:S(2)}, u32[]{:S(2)}) %collective-permute-start.6) | collective-permute-done | bytes 114720 | tf_op jit(solution)/shard_map/ppermute | solution.py:25
  33.2 2.6 %collective-permute-done.7 = bf16[2,224,128]{2,1,0:T(8,128)(2,1)S(1)} collective-permute-done((bf16[2,224,128]{2,1,0:T(8,128)(2,1)S(1)}, bf16[2,224,128]{2,1,0:T(8,128)(2,1)S(1)}, u32[]{:S(2)}, u32[]{:S(2)}) %collective-permute-start.7) | collective-permute-done | bytes 114720 | tf_op jit(solution)/shard_map/ppermute | solution.py:25
  35.8 1.2 %collective-permute-done.8 = bf16[2,224,128]{2,1,0:T(8,128)(2,1)S(1)} collective-permute-done((bf16[2,224,128]{2,1,0:T(8,128)(2,1)S(1)}, bf16[2,224,128]{2,1,0:T(8,128)(2,1)S(1)}, u32[]{:S(2)}, u32[]{:S(2)}) %collective-permute-start.8) | collective-permute-done | bytes 114720 | tf_op jit(solution)/shard_map/ppermute | solution.py:25
  37.1 2.7 %collective-permute-start.9 = (bf16[2,224,128]{2,1,0:T(8,128)(2,1)S(1)}, bf16[2,224,128]{2,1,0:T(8,128)(2,1)S(1)}, u32[]{:S(2)}, u32[]{:S(2)}) collective-permute-start(bf16[2,224,128]{2,1,0:T(8,128)(2,1)S(1)} %reduce-precision_convert_fusion), channel_id=1, source_target_pairs={{8,0},{9,1},{10,2},{11,3},{12,4},{13,5},{14,6},{15,7},{0,8},{1,9},... | collective-permute-start | bytes 344072 | tf_op jit(solution)/shard_map/ppermute | solution.py:25
  39.8 4.7 %collective-permute-done.9 = bf16[2,224,128]{2,1,0:T(8,128)(2,1)S(1)} collective-permute-done((bf16[2,224,128]{2,1,0:T(8,128)(2,1)S(1)}, bf16[2,224,128]{2,1,0:T(8,128)(2,1)S(1)}, u32[]{:S(2)}, u32[]{:S(2)}) %collective-permute-start.9) | collective-permute-done | bytes 114720 | tf_op jit(solution)/shard_map/ppermute | solution.py:25
  44.5 0.5 collective-permute-start.10
  45.0 4.4 %collective-permute-done.10 = bf16[2,224,128]{2,1,0:T(8,128)(2,1)S(1)} collective-permute-done((bf16[2,224,128]{2,1,0:T(8,128)(2,1)S(1)}, bf16[2,224,128]{2,1,0:T(8,128)(2,1)S(1)}, u32[]{:S(2)}, u32[]{:S(2)}) %collective-permute-start.10) | collective-permute-done | bytes 114720 | tf_op jit(solution)/shard_map/ppermute | solution.py:25
  49.4 2.7 %collective-permute-start.13 = (bf16[4,224,128]{2,1,0:T(8,128)(2,1)S(1)}, bf16[4,224,128]{2,1,0:T(8,128)(2,1)S(1)}, u32[]{:S(2)}, u32[]{:S(2)}) collective-permute-start(bf16[4,224,128]{2,1,0:T(8,128)(2,1)S(1)} %pad_maximum_fusion.1.refs_0_), channel_id=1, source_target_pairs={{18,0},{19,1},{16,2},{17,3},{22,4},{23,5},{20,6},{21,7},{26,8},{27... | collective-permute-start | bytes 688136 | tf_op jit(solution)/shard_map/ppermute | solution.py:25
  52.9 4.6 %collective-permute-done.13.refs_3_ = bf16[4,224,128]{2,1,0:T(8,128)(2,1)S(1)} collective-permute-done((bf16[4,224,128]{2,1,0:T(8,128)(2,1)S(1)}, bf16[4,224,128]{2,1,0:T(8,128)(2,1)S(1)}, u32[]{:S(2)}, u32[]{:S(2)}) %collective-permute-start.13) | collective-permute-done | bytes 229408 | tf_op jit(solution)/shard_map/ppermute | solution.py:25
  57.5 2.2 %collective-permute-done.12.refs_2_ = bf16[4,224,128]{2,1,0:T(8,128)(2,1)S(1)} collective-permute-done((bf16[4,224,128]{2,1,0:T(8,128)(2,1)S(1)}, bf16[4,224,128]{2,1,0:T(8,128)(2,1)S(1)}, u32[]{:S(2)}, u32[]{:S(2)}) %collective-permute-start.12) | collective-permute-done | bytes 229408 | tf_op jit(solution)/shard_map/ppermute | solution.py:25
  60.2 1.0 %collective-permute-done.16.refs_6_ = bf16[4,224,128]{2,1,0:T(8,128)(2,1)S(1)} collective-permute-done((bf16[4,224,128]{2,1,0:T(8,128)(2,1)S(1)}, bf16[4,224,128]{2,1,0:T(8,128)(2,1)S(1)}, u32[]{:S(2)}, u32[]{:S(2)}) %collective-permute-start.16) | collective-permute-done | bytes 229408 | tf_op jit(solution)/shard_map/ppermute | solution.py:25
  61.5 1.8 %place.1 = (bf16[3456,128]{1,0:T(8,128)(2,1)}, bf16[3456,128]{1,0:T(8,128)(2,1)}) custom-call(s32[4]{0:T(128)S(1)} %pad_add_fusion.index_ref, bf16[4,224,128]{2,1,0:T(8,128)(2,1)S(1)} %pad_maximum_fusion.1.refs_0_, bf16[4,224,128]{2,1,0:T(8,128)(2,1)S(1)} %collective-permute-done.11.refs_1_, bf16[4,224,128]{2,1,0:T(8,128)(2,1)S(1)} %collective-permute-done.12.refs_2_, ...), custom_call_target="tpu_custom_call" | custom-call | tf_op jit(solution)/shard_map/place/pallas_call | solution.py:286
  (33 shorter events, 2.9 us)
Async XLA Ops:
  0.6 2.0 %copy-start.3 = (bf16[4,8,16,128]{3,2,1,0:T(8,128)(2,1)S(1)}, bf16[4,8,16,128]{3,2,1,0:T(8,128)(2,1)}, u32[]{:S(2)}) copy-start(bf16[4,8,16,128]{3,2,1,0:T(8,128)(2,1)} %param.6) | copy-start | bytes 393220
  1.4 17.7 %copy-start.2 = (bf16[27,128,128]{2,1,0:T(8,128)(2,1)S(1)}, bf16[27,128,128]{2,1,0:T(8,128)(2,1)}, u32[]{:S(2)}) copy-start(bf16[27,128,128]{2,1,0:T(8,128)(2,1)} %refs_8_.1) | copy-start | bytes 2654212
  2.6 16.5 %copy-start.1 = (bf16[27,128,128]{2,1,0:T(8,128)(2,1)S(1)}, bf16[27,128,128]{2,1,0:T(8,128)(2,1)}, u32[]{:S(2)}) copy-start(bf16[27,128,128]{2,1,0:T(8,128)(2,1)} %refs_7_.1) | copy-start | bytes 2654212
  2.7 14.3 %collective-permute-start.2 = (bf16[12,8,16,128]{3,2,1,0:T(8,128)(2,1)S(1)}, bf16[12,8,16,128]{3,2,1,0:T(8,128)(2,1)S(1)}, u32[]{:S(2)}, u32[]{:S(2)}) collective-permute-start(bf16[12,8,16,128]{3,2,1,0:T(8,128)(2,1)S(1)} %pad_maximum_fusion.refs_0_), channel_id=1, source_target_pairs={{16,0},{17,1},{18,2},{19,3},{20,4},{21,5},{22,6},{23,7},{24,8},{25... | collective-permute-start | bytes 1179656 | tf_op jit(solution)/shard_map/ppermute | solution.py:25
  5.7 13.3 %copy-start = (bf16[4,8,16,128]{3,2,1,0:T(8,128)(2,1)S(1)}, bf16[4,8,16,128]{3,2,1,0:T(8,128)(2,1)}, u32[]{:S(2)}) copy-start(bf16[4,8,16,128]{3,2,1,0:T(8,128)(2,1)} %refs_6_.1) | copy-start | bytes 393220
  5.8 7.9 %collective-permute-start.1 = (bf16[3,8,16,128]{3,2,1,0:T(8,128)(2,1)S(1)}, bf16[3,8,16,128]{3,2,1,0:T(8,128)(2,1)S(1)}, u32[]{:S(2)}, u32[]{:S(2)}) collective-permute-start(bf16[3,8,16,128]{3,2,1,0:T(8,128)(2,1)S(1)} %pad_maximum_fusion.3), channel_id=1, source_target_pairs={{31,0},{18,1},{17,2},{20,3},{19,4},{22,5},{21,6},{24,7},{23,8},{26... | collective-permute-start | bytes 294920 | tf_op jit(solution)/shard_map/ppermute | solution.py:25
  9.5 6.7 %collective-permute-start = (bf16[3,8,16,128]{3,2,1,0:T(8,128)(2,1)S(1)}, bf16[3,8,16,128]{3,2,1,0:T(8,128)(2,1)S(1)}, u32[]{:S(2)}, u32[]{:S(2)}) collective-permute-start(bf16[3,8,16,128]{3,2,1,0:T(8,128)(2,1)S(1)} %pad_maximum_fusion.3), channel_id=1, source_target_pairs={{15,0},{2,1},{1,2},{4,3},{3,4},{6,5},{5,6},{8,7},{7,8},{10,9},{9,1... | collective-permute-start | bytes 294920 | tf_op jit(solution)/shard_map/ppermute | solution.py:25
  9.7 7.8 %collective-permute-start.3 = (bf16[12,8,16,128]{3,2,1,0:T(8,128)(2,1)S(1)}, bf16[12,8,16,128]{3,2,1,0:T(8,128)(2,1)S(1)}, u32[]{:S(2)}, u32[]{:S(2)}) collective-permute-start(bf16[12,8,16,128]{3,2,1,0:T(8,128)(2,1)S(1)} %pad_maximum_fusion.refs_0_), channel_id=1, source_target_pairs={{1,0},{0,1},{3,2},{2,3},{5,4},{4,5},{7,6},{6,7},{9,8},{8,9},{11,10... | collective-permute-start | bytes 1179656 | tf_op jit(solution)/shard_map/ppermute | solution.py:25
  16.9 2.1 %collective-permute-start.4 = (bf16[12,8,16,128]{3,2,1,0:T(8,128)(2,1)S(1)}, bf16[12,8,16,128]{3,2,1,0:T(8,128)(2,1)}, u32[]{:S(2)}, u32[]{:S(2)}) collective-permute-start(bf16[12,8,16,128]{3,2,1,0:T(8,128)(2,1)S(1)} %collective-permute-done.2.refs_1_), channel_id=1, source_target_pairs={{1,0},{0,1},{3,2},{2,3},{5,4},{4,5},{7,6},{6,7},{9,8},{8,9},{11,10... | collective-permute-start | bytes 1179656 | tf_op jit(solution)/shard_map/ppermute | solution.py:25
  16.9 1.8 %collective-permute-start.5 = (bf16[6,8,16,128]{3,2,1,0:T(8,128)(2,1)S(1)}, bf16[6,8,16,128]{3,2,1,0:T(8,128)(2,1)S(1)}, u32[]{:S(2)}, u32[]{:S(2)}) collective-permute-start(bf16[6,8,16,128]{3,2,1,0:T(8,128)(2,1)S(1)} %pad_maximum_fusion.2.refs_4_), channel_id=1, source_target_pairs={{1,0},{0,1},{3,2},{2,3},{5,4},{4,5},{7,6},{6,7},{9,8},{8,9},{11,10... | collective-permute-start | bytes 589832 | tf_op jit(solution)/shard_map/ppermute | solution.py:25
  28.1 5.1 %collective-permute-start.6 = (bf16[2,224,128]{2,1,0:T(8,128)(2,1)S(1)}, bf16[2,224,128]{2,1,0:T(8,128)(2,1)S(1)}, u32[]{:S(2)}, u32[]{:S(2)}) collective-permute-start(bf16[2,224,128]{2,1,0:T(8,128)(2,1)S(1)} %get-tuple-element.16), channel_id=1, source_target_pairs={{2,0},{3,1},{0,2},{1,3},{6,4},{7,5},{4,6},{5,7},{10,8},{11,9},{8,1... | collective-permute-start | bytes 344072 | tf_op jit(solution)/shard_map/ppermute | solution.py:25
  29.8 6.0 %collective-permute-start.7 = (bf16[2,224,128]{2,1,0:T(8,128)(2,1)S(1)}, bf16[2,224,128]{2,1,0:T(8,128)(2,1)S(1)}, u32[]{:S(2)}, u32[]{:S(2)}) collective-permute-start(bf16[2,224,128]{2,1,0:T(8,128)(2,1)S(1)} %get-tuple-element.17), channel_id=1, source_target_pairs={{4,0},{5,1},{6,2},{7,3},{0,4},{1,5},{2,6},{3,7},{12,8},{13,9},{14,... | collective-permute-start | bytes 344072 | tf_op jit(solution)/shard_map/ppermute | solution.py:25
  31.4 5.7 %collective-permute-start.8 = (bf16[2,224,128]{2,1,0:T(8,128)(2,1)S(1)}, bf16[2,224,128]{2,1,0:T(8,128)(2,1)S(1)}, u32[]{:S(2)}, u32[]{:S(2)}) collective-permute-start(bf16[2,224,128]{2,1,0:T(8,128)(2,1)S(1)} %get-tuple-element.18), channel_id=1, source_target_pairs={{6,0},{7,1},{4,2},{5,3},{2,4},{3,5},{0,6},{1,7},{14,8},{15,9},{12,... | collective-permute-start | bytes 344072 | tf_op jit(solution)/shard_map/ppermute | solution.py:25
  37.1 7.3 %collective-permute-start.9 = (bf16[2,224,128]{2,1,0:T(8,128)(2,1)S(1)}, bf16[2,224,128]{2,1,0:T(8,128)(2,1)S(1)}, u32[]{:S(2)}, u32[]{:S(2)}) collective-permute-start(bf16[2,224,128]{2,1,0:T(8,128)(2,1)S(1)} %reduce-precision_convert_fusion), channel_id=1, source_target_pairs={{8,0},{9,1},{10,2},{11,3},{12,4},{13,5},{14,6},{15,7},{0,8},{1,9},... | collective-permute-start | bytes 344072 | tf_op jit(solution)/shard_map/ppermute | solution.py:25
  44.5 4.9 %collective-permute-start.10 = (bf16[2,224,128]{2,1,0:T(8,128)(2,1)S(1)}, bf16[2,224,128]{2,1,0:T(8,128)(2,1)S(1)}, u32[]{:S(2)}, u32[]{:S(2)}) collective-permute-start(bf16[2,224,128]{2,1,0:T(8,128)(2,1)S(1)} %add_convert_fusion), channel_id=1, source_target_pairs={{4,0},{5,1},{6,2},{7,3},{0,4},{1,5},{2,6},{3,7},{12,8},{13,9},{14,... | collective-permute-start | bytes 344072 | tf_op jit(solution)/shard_map/ppermute | solution.py:25
  49.4 8.1 %collective-permute-start.13 = (bf16[4,224,128]{2,1,0:T(8,128)(2,1)S(1)}, bf16[4,224,128]{2,1,0:T(8,128)(2,1)S(1)}, u32[]{:S(2)}, u32[]{:S(2)}) collective-permute-start(bf16[4,224,128]{2,1,0:T(8,128)(2,1)S(1)} %pad_maximum_fusion.1.refs_0_), channel_id=1, source_target_pairs={{18,0},{19,1},{16,2},{17,3},{22,4},{23,5},{20,6},{21,7},{26,8},{27... | collective-permute-start | bytes 688136 | tf_op jit(solution)/shard_map/ppermute | solution.py:25
  52.1 7.6 %collective-permute-start.12 = (bf16[4,224,128]{2,1,0:T(8,128)(2,1)S(1)}, bf16[4,224,128]{2,1,0:T(8,128)(2,1)S(1)}, u32[]{:S(2)}, u32[]{:S(2)}) collective-permute-start(bf16[4,224,128]{2,1,0:T(8,128)(2,1)S(1)} %pad_maximum_fusion.1.refs_0_), channel_id=1, source_target_pairs={{16,0},{17,1},{18,2},{19,3},{20,4},{21,5},{22,6},{23,7},{24,8},{25... | collective-permute-start | bytes 688136 | tf_op jit(solution)/shard_map/ppermute | solution.py:25
  52.5 7.3 %collective-permute-start.11 = (bf16[4,224,128]{2,1,0:T(8,128)(2,1)S(1)}, bf16[4,224,128]{2,1,0:T(8,128)(2,1)S(1)}, u32[]{:S(2)}, u32[]{:S(2)}) collective-permute-start(bf16[4,224,128]{2,1,0:T(8,128)(2,1)S(1)} %pad_maximum_fusion.1.refs_0_), channel_id=1, source_target_pairs={{2,0},{3,1},{0,2},{1,3},{6,4},{7,5},{4,6},{5,7},{10,8},{11,9},{8,1... | collective-permute-start | bytes 688136 | tf_op jit(solution)/shard_map/ppermute | solution.py:25
  52.9 7.3 %collective-permute-start.14 = (bf16[4,224,128]{2,1,0:T(8,128)(2,1)S(1)}, bf16[4,224,128]{2,1,0:T(8,128)(2,1)S(1)}, u32[]{:S(2)}, u32[]{:S(2)}) collective-permute-start(bf16[4,224,128]{2,1,0:T(8,128)(2,1)S(1)} %pad_maximum_fusion.1.refs_0_), channel_id=1, source_target_pairs={{1,0},{0,1},{3,2},{2,3},{5,4},{4,5},{7,6},{6,7},{9,8},{8,9},{11,10... | collective-permute-start | bytes 688136 | tf_op jit(solution)/shard_map/ppermute | solution.py:25
  57.5 2.8 %collective-permute-start.17 = (bf16[4,224,128]{2,1,0:T(8,128)(2,1)S(1)}, bf16[4,224,128]{2,1,0:T(8,128)(2,1)S(1)}, u32[]{:S(2)}, u32[]{:S(2)}) collective-permute-start(bf16[4,224,128]{2,1,0:T(8,128)(2,1)S(1)} %collective-permute-done.13.refs_3_), channel_id=1, source_target_pairs={{1,0},{0,1},{3,2},{2,3},{5,4},{4,5},{7,6},{6,7},{9,8},{8,9},{11,10... | collective-permute-start | bytes 688136 | tf_op jit(solution)/shard_map/ppermute | solution.py:25
  59.7 1.5 %collective-permute-start.16 = (bf16[4,224,128]{2,1,0:T(8,128)(2,1)S(1)}, bf16[4,224,128]{2,1,0:T(8,128)(2,1)S(1)}, u32[]{:S(2)}, u32[]{:S(2)}) collective-permute-start(bf16[4,224,128]{2,1,0:T(8,128)(2,1)S(1)} %collective-permute-done.12.refs_2_), channel_id=1, source_target_pairs={{1,0},{0,1},{3,2},{2,3},{5,4},{4,5},{7,6},{6,7},{9,8},{8,9},{11,10... | collective-permute-start | bytes 688136 | tf_op jit(solution)/shard_map/ppermute | solution.py:25
  59.8 1.7 %collective-permute-start.15 = (bf16[4,224,128]{2,1,0:T(8,128)(2,1)S(1)}, bf16[4,224,128]{2,1,0:T(8,128)(2,1)S(1)}, u32[]{:S(2)}, u32[]{:S(2)}) collective-permute-start(bf16[4,224,128]{2,1,0:T(8,128)(2,1)S(1)} %collective-permute-done.11.refs_1_), channel_id=1, source_target_pairs={{1,0},{0,1},{3,2},{2,3},{5,4},{4,5},{7,6},{6,7},{9,8},{8,9},{11,10... | collective-permute-start | bytes 688136 | tf_op jit(solution)/shard_map/ppermute | solution.py:25

commit v4 on v3

--- a/solution.py
+++ b/solution.py
@@ -66,7 +66,7 @@
 
 
 def fill_second(field_ref, own, other, rim_own, rim_other, me):
-    width = own[0].shape[0] // 3
+    width = own[0].shape[0] // 2
     for i in range(width):
         put_planes(field_ref, 2 + width * me + i, joined(own, i, 1))
         put_planes(field_ref, 2 + width * (1 - me) + i, joined(other, i, 1))
@@ -107,48 +107,71 @@
             ref[i, pl.ds(tensor * rows, rows), :] = chunk
 
 
+def convolve(ref, start, planes, depth, w_ref, parts_ref, put):
+    ny, chans = ref.shape[2] - 2, ref.shape[4]
+
+    def products(at):
+        cols = jnp.concatenate(
+            [shifted(ref, 0, b, c, at, 1, depth) for _, b, c in OFFSETS[:9]], axis=1
+        )
+        return jnp.dot(cols, w_ref[...], preferred_element_type=F32)
+
+    def out(i, part):
+        total = sum(part(i - 1 - a)[:, (a + 1) * chans : (a + 2) * chans] for a in (-1, 0, 1))
+        put(i - 2, total.reshape(1, ny, depth, chans))
+
+    if ny * depth <= 256:
+        parts = []
+        for i in range(planes + 2):
+            parts.append(products(start - 1 + i))
+            if i >= 2:
+                out(i, parts.__getitem__)
+        return
+
+    rows = pl.ds(0, ny * depth)
+
+    def step(i, carry):
+        parts_ref[i % 3, rows] = products(start - 1 + i)
+        pl.when(i >= 2)(lambda: out(i, lambda j: parts_ref[(j + 3) % 3, rows]))
+        return carry
+
+    lax.fori_loop(0, planes + 2, step, 0)
+
+
+def widen_kernel(*refs):
+    half = len(refs) // 2
+    for w_ref, wide_ref in zip(refs[1 : half + 1], refs[half + 1 :], strict=True):
+        chans = w_ref.shape[1]
+        for k in range(27):
+            a, bc = divmod(k, 9)
+            block = jnp.transpose(w_ref[k].astype(F32)).astype(BF16)
+            wide_ref[pl.ds(bc * chans, chans), pl.ds(a * chans, chans)] = block
+
+
+def grad_in_kernel(index_ref, near_ref, grad_out_ref, w_ref, grad_in_ref, field_ref, parts_ref):
+    planes, padded, nz, chans = near_ref.shape
+    width, ny, zs, _ = grad_out_ref.shape
+    for i in range(planes):
+        put_planes(field_ref, i, near_ref[pl.ds(i, 1), pl.ds(1, ny)].astype(F32))
+
+    def put(i, back):
+        grad_in_ref[pl.ds(i, 1)] = (grad_out_ref[pl.ds(i, 1)].astype(F32) + back).astype(BF16)
+
+    convolve(field_ref, 1, width, zs, w_ref, parts_ref, put)
+
+
 def group_kernel(slabs, per, scale, index_ref, *refs):
-    own, other = refs[:slabs], refs[slabs : 2 * slabs]
+    own, other, in_own, in_other = (refs[i * slabs : (i + 1) * slabs] for i in range(4))
+    refs = refs[2 * slabs :]
     rim_own, rim_other = (
         [ref.at[pl.ds(3 * r, 3)] for r in range(slabs)] for ref in refs[2 * slabs : 2 * slabs + 2]
     )
-    grad_out_ref, w_second_ref, w_first_ref, grad_in_ref, keep_ref, *refs = refs[2 * slabs + 2 :]
-    *sent_refs, field_ref, first_ref, pre_ref, left_ref, parts_ref, wide_ref, scratch_ref = refs
+    w_second_ref, near_ref, keep_ref, *refs = refs[2 * slabs + 2 :]
+    *sent_refs, field_ref, first_ref, pre_ref, left_ref, parts_ref, scratch_ref = refs
     me, pair = index_ref[0], index_ref[2]
-    width, (ny, zs, chans) = own[0].shape[0] // 3, own[0].shape[1:]
+    width, ny, zs, chans = in_own[0].shape
     nz = zs * slabs
-    unrolled = ny * nz <= 256
     fill_second(field_ref, own, other, rim_own, rim_other, me)
-
-    def products(ref, start, depth, w_ref):
-        cols = jnp.concatenate(
-            [shifted(ref, 0, b, c, start, 1, depth) for _, b, c in OFFSETS[:9]], axis=1
-        )
-        return lax.dot_general(
-            cols, w_ref[...], (((1,), (1,)), ((), ())), preferred_element_type=F32
-        )
-
-    def conv(ref, start, planes, depth, w_ref, put):
-        def out(i, part):
-            total = sum(part(i - 1 - a)[:, (a + 1) * chans : (a + 2) * chans] for a in (-1, 0, 1))
-            put(i - 2, total.reshape(1, ny, depth, chans))
-
-        if unrolled:
-            parts = []
-            for i in range(planes + 2):
-                parts.append(products(ref, start - 1 + i, depth, w_ref))
-                if i >= 2:
-                    out(i, parts.__getitem__)
-            return
-
-        rows = pl.ds(0, ny * depth)
-
-        def step(i, carry):
-            parts_ref[i % 3, rows] = products(ref, start - 1 + i, depth, w_ref)
-            pl.when(i >= 2)(lambda: out(i, lambda j: parts_ref[(j + 3) % 3, rows]))
-            return carry
-
-        lax.fori_loop(0, planes + 2, step, 0)
 
     def pre_of(i):
         return pre_ref[pl.ds(i, 1)]
@@ -167,21 +190,12 @@
         sig = sigmoid(pre)
         put_planes(first_ref, i, grad_act * (sig * (1.0 + pre * (1.0 - sig))))
 
-    def put_grad_in(i, back):
-        grad_in_ref[pl.ds(i, 1)] = (grad_out_ref[pl.ds(i, 1)].astype(F32) + back).astype(BF16)
-
-    def widened(w_ref):
-        for k in range(27):
-            a, bc = divmod(k, 9)
-            wide_ref[pl.ds(a * chans, chans), pl.ds(bc * chans, chans)] = w_ref[k]
-        return wide_ref
-
-    conv(field_ref, 1, 2 * width + 2, nz, widened(w_second_ref), put_first)
-    conv(first_ref, 1 + width * me, width, zs, widened(w_first_ref), put_grad_in)
+    convolve(field_ref, 1, 2 * width + 2, nz, w_second_ref, parts_ref, put_first)
+    near_ref[...] = first_ref[1, pl.ds(width * me, width + 2)]
 
     for i in range(width):
-        for refs_of, who in ((own, me), (other, 1 - me)):
-            rows = joined(refs_of, 2 * width + i, 1).astype(BF16).reshape(ny * nz, chans)
+        for refs_of, who in ((in_own, me), (in_other, 1 - me)):
+            rows = joined(refs_of, i, 1).astype(BF16).reshape(ny * nz, chans)
             at = pl.multiple_of((who * width + i) * ny * nz, ny * nz)
             left_ref[pl.ds(at, ny * nz), :] = rows
     kernel_terms(left_ref, first_ref, 1, 2 * width, nz, scratch_ref, index_ref, per, scale)
@@ -220,7 +234,7 @@
     )(index, *operands)
 
 
-def combine(keep, sent, pairs, slabs):
+def combine(keep, sent, pairs, slabs, beside):
     total = keep + sum(partner(v, 2 * d).astype(F32) for d, v in enumerate(sent, 1))
     held = list(range(0, pairs, 4))
     middle = [1 << i for i in range(2, pairs.bit_length() - 2)]
@@ -231,6 +245,7 @@
         held = [r for r in held if not r & bit]
     mine = lax.reduce_precision(total, 8, 7).astype(BF16)
     got = partner(mine, pairs)
+    got, beside = lax.optimization_barrier((got, beside))
     array = (mine.astype(F32) + got[::-1].astype(F32)).astype(BF16)
     for bit in [*middle[::-1], 2]:
         array = jnp.concatenate([array, partner(array, 2 * bit)], axis=0)
@@ -244,7 +259,7 @@
                     lambda s, r=r: (s + r) % slabs,
                     lambda b, odd=odd: b ^ (2 * odd),
                 )
-    return pieces, held
+    return pieces, held, beside
 
 
 def place_kernel(slabs, pairs, held, index_ref, *refs):
@@ -312,7 +327,7 @@
     occ = occupancy[..., None] != 0
     masked = jnp.where(occ, grad_out, jnp.zeros_like(grad_out))
     pre = jnp.where(occ, pre_first, jnp.full_like(pre_first, EMPTY))
-    both = jnp.concatenate([masked, pre, inputs], axis=0)
+    both = jnp.concatenate([masked, pre], axis=0)
     odd = me == 1
     rim = jnp.concatenate(
         [
@@ -325,11 +340,18 @@
     def swap(b):
         return (b + 1) % bricks if b % 2 else (b - 1) % bricks
 
-    own = over_slabs(both)
+    own, in_own = over_slabs(both), over_slabs(inputs)
     rim_own = jnp.concatenate(over_slabs(rim, swap), axis=0)
 
-    rim_own, own[-1] = lax.optimization_barrier((rim_own, own[-1]))
+    wide = jax.ShapeDtypeStruct((9 * chans, 3 * chans), BF16)
+    wide_second, wide_first = call(
+        widen_kernel, index, [w_second, w_first], [wide, wide], [], 0, "kernels_side_by_side"
+    )
+    wide_second, rim_own, own[-1], in_own[-1] = lax.optimization_barrier(
+        (wide_second, rim_own, own[-1], in_own[-1])
+    )
     other = [partner(v, 1) for v in own]
+    in_other = [partner(v, 1) for v in in_own]
     rim_other = partner(rim_own, 1)
 
     shares = [
@@ -337,24 +359,34 @@
         for dtype in (F32, BF16, BF16, BF16)
     ]
     group = 2 * width * ny * nz
-    grad_in, keep, *sent = call(
+    parts = vmem((3, ny * nz, 3 * chans), F32)
+    near = jax.ShapeDtypeStruct((width + 2, ny + 2, nz, chans), BF16)
+    near, keep, *sent = call(
         functools.partial(group_kernel, slabs, per, scale),
         index,
-        [*own, *other, rim_own, rim_other, grad_out, w_second, w_first],
-        [jax.ShapeDtypeStruct(inputs.shape, BF16), *shares],
+        [*own, *other, *in_own, *in_other, rim_own, rim_other, wide_second],
+        [near, *shares],
         [
             vmem((3, 2 * width + 4, ny + 2, nz, chans), BF16),
             vmem((3, 2 * width + 2, ny + 2, nz, chans), BF16),
             vmem((2 * width + 2, ny, nz, chans), F32),
             vmem((group, chans), BF16),
-            vmem((3, ny * nz, 3 * chans), F32),
-            vmem((3 * chans, 9 * chans), BF16),
+            parts,
             vmem((per * chans, chans), F32),
         ],
-        2 * group * (28 + 2 * per) * chans * chans,
+        2 * group * (27 + 2 * per) * chans * chans,
         "group",
     )
-    pieces, held = combine(keep, sent, pairs, slabs)
+    (grad_in,) = call(
+        grad_in_kernel,
+        index,
+        [near, grad_out, wide_first],
+        [jax.ShapeDtypeStruct(inputs.shape, BF16)],
+        [vmem((3, *near.shape), BF16), parts],
+        2 * group * 9 * chans * chans,
+        "grad_in",
+    )
+    pieces, held, grad_in = combine(keep, sent, pairs, slabs, grad_in)
     pieces = [pieces[r, odd] for r in range(slabs) for odd in range(2)]
     pieces += [partner(v, 1) for v in pieces]
     outs = place(slabs, pairs, held, index, pieces, 27 * chans)

time: 63.6 us -> 62.1 us (0.976)
  waiting for transfers between devices: 31.4 us -> 24.3 us
  starting transfers between devices: 18.2 us -> 21.1 us
  Pallas kernels: 10.8 us -> 12.3 us
  local copies, waits for them, and re-layouts: 0.02 us -> 1.18 us
    ppermute x18 -> x21, waiting for transfers between devices: 31.4 us -> 24.3 us  [send(): return lax.ppermute(value, AXES, pairs)]
    ppermute x18 -> x21, starting transfers between devices: 18.2 us -> 21.1 us  [send(): return lax.ppermute(value, AXES, pairs)]
    pallas_call x1 -> x3, Pallas kernels: 9 us -> 10.4 us  [call(): pl.pallas_call(body, out_shape=out_shape, in_specs=[space(v) for v in (in...]
    unnamed x8, local copies, waits for them, and re-layouts: 0.02 us -> 1.18 us
  transfers between devices with their start and end apart: 18 -> 21, of which waited for: 15 -> 13; matrix products, arithmetic and copies ran while one was open for 0% -> 0% of each run, Pallas kernels for 0% -> 5%
where the time goes in v4:
time: 62.1 us; the launch traced here: 61.8 us
  waiting for transfers between devices  24.3 us (39%)
  starting transfers between devices  21.1 us (34%)
  Pallas kernels  12.3 us (20%)
  other arithmetic  2.17 us (3%)
  local copies, waits for them, and re-layouts  1.18 us (2%)
  between operations  0.73 us (1%)
    ppermute x21, waiting for transfers between devices, send(): return lax.ppermute(value, AXES, pairs)  24.3 us
    ppermute x21, starting transfers between devices, send(): return lax.ppermute(value, AXES, pairs)  21.1 us
    pallas_call x3, Pallas kernels, call(): pl.pallas_call(body, out_shape=out_shape, in_specs=[space(v) for v in (in...  10.4 us
    pallas_call x1, Pallas kernels, place(): pl.pallas_call(functools.partial(place_kernel, slabs, pairs, held), out_s...  1.82 us
  transfers between devices with their start and end apart: 21, of which 13 were waited for; matrix products, arithmetic and copies ran while one was open for 0% of the time, Pallas kernels for 5%

profile of v4, /device:TPU:0, one launch (start us, length us, event | category | flops | bytes accessed | tf_op | source)
XLA Modules:
  0.0 61.8 jit_solution(3040702249449557855)
XLA Ops:
  0.6 0.8 %broadcast_compare_fusion = pred[4,8,16]{2,1,0:T(8,128)(4,1)S(1)} fusion(s32[4,8,16]{2,1,0:T(8,128)} %param.8), kind=kLoop, calls=%fused_computation.10 | loop fusion | flops 512 | bytes 2560 | tf_op jit(solution)/shard_map/ne | solution.py:327
  1.4 1.1 %broadcast_select_fusion.1 = (bf16[4,8,16,128]{3,2,1,0:T(8,128)(2,1)S(1)}, bf16[4,8,16,128]{3,2,1,0:T(8,128)(2,1)S(1)}) fusion(bf16[4,8,16,128]{3,2,1,0:T(8,128)(2,1)} %grad_out_ref.1, pred[4,8,16]{2,1,0:T(8,128)(4,1)S(1)} %broadcast_compare_fusion, bf16[4,8,16,128]{3,2,1,0:T(8,128)(2,1)} %param.7), kind=kLoop, calls=%fused_computation.6 | loop fusion | flops 131072 | bytes 524800 | tf_op jit(solution)/shard_map/jit(_where)/select_n | solution.py:328
  2.6 3.0 %collective-permute-start.2 = (bf16[8,8,16,128]{3,2,1,0:T(8,128)(2,1)S(1)}, bf16[8,8,16,128]{3,2,1,0:T(8,128)(2,1)S(1)}, u32[]{:S(2)}, u32[]{:S(2)}) collective-permute-start(bf16[8,8,16,128]{3,2,1,0:T(8,128)(2,1)S(1)} %pad_maximum_fusion.refs_0_), channel_id=1, source_target_pairs={{16,0},{17,1},{18,2},{19,3},{20,4},{21,5},{22,6},{23,7},{24,8},{25... | collective-permute-start | bytes 786440 | tf_op jit(solution)/shard_map/ppermute | solution.py:25
  5.7 3.7 %collective-permute-start.1 = (bf16[3,8,16,128]{3,2,1,0:T(8,128)(2,1)S(1)}, bf16[3,8,16,128]{3,2,1,0:T(8,128)(2,1)S(1)}, u32[]{:S(2)}, u32[]{:S(2)}) collective-permute-start(bf16[3,8,16,128]{3,2,1,0:T(8,128)(2,1)S(1)} %pad_maximum_fusion.3), channel_id=1, source_target_pairs={{31,0},{18,1},{17,2},{20,3},{19,4},{22,5},{21,6},{24,7},{23,8},{26... | collective-permute-start | bytes 294920 | tf_op jit(solution)/shard_map/ppermute | solution.py:25
  9.7 2.0 %collective-permute-start.3 = (bf16[4,8,16,128]{3,2,1,0:T(8,128)(2,1)S(1)}, bf16[4,8,16,128]{3,2,1,0:T(8,128)(2,1)S(1)}, u32[]{:S(2)}, u32[]{:S(2)}) collective-permute-start(bf16[4,8,16,128]{3,2,1,0:T(8,128)(2,1)S(1)} %copy-done.3), channel_id=1, source_target_pairs={{16,0},{17,1},{18,2},{19,3},{20,4},{21,5},{22,6},{23,7},{24,8},{25... | collective-permute-start | bytes 393224 | tf_op jit(solution)/shard_map/ppermute | solution.py:25
  11.7 1.2 %copy-done.1 = bf16[27,128,128]{2,1,0:T(8,128)(2,1)S(1)} copy-done((bf16[27,128,128]{2,1,0:T(8,128)(2,1)S(1)}, bf16[27,128,128]{2,1,0:T(8,128)(2,1)}, u32[]{:S(2)}) %copy-start.1) | copy-done | bytes 884760
  12.9 1.1 %kernels_side_by_side.1 = (bf16[1152,384]{1,0:T(8,128)(2,1)S(1)}, bf16[1152,384]{1,0:T(8,128)(2,1)S(1)}) custom-call(s32[4]{0:T(128)S(1)} %pad_add_fusion.refs_0_.index_ref, bf16[27,128,128]{2,1,0:T(8,128)(2,1)S(1)} %copy-done, bf16[27,128,128]{2,1,0:T(8,128)(2,1)S(1)} %copy-done.1), custom_call_target="tpu_custom_call" | custom-call | bytes 4194304 | tf_op jit(solution)/shard_map/kernels_side_by_side/pallas_call | solution.py:225
  14.0 2.1 %collective-permute-done = bf16[3,8,16,128]{3,2,1,0:T(8,128)(2,1)S(1)} collective-permute-done((bf16[3,8,16,128]{3,2,1,0:T(8,128)(2,1)S(1)}, bf16[3,8,16,128]{3,2,1,0:T(8,128)(2,1)S(1)}, u32[]{:S(2)}, u32[]{:S(2)}) %collective-permute-start) | collective-permute-done | bytes 98336 | tf_op jit(solution)/shard_map/ppermute | solution.py:25
  17.9 1.0 %collective-permute-done.6.refs_6_ = bf16[4,8,16,128]{3,2,1,0:T(8,128)(2,1)S(1)} collective-permute-done((bf16[4,8,16,128]{3,2,1,0:T(8,128)(2,1)S(1)}, bf16[4,8,16,128]{3,2,1,0:T(8,128)(2,1)S(1)}, u32[]{:S(2)}, u32[]{:S(2)}) %collective-permute-start.6) | collective-permute-done | bytes 131104 | tf_op jit(solution)/shard_map/ppermute | solution.py:25
  19.0 7.2 %group.1 = (bf16[6,10,32,128]{3,2,1,0:T(8,128)(2,1)S(1)}, f32[2,224,128]{2,1,0:T(8,128)S(1)}, bf16[2,224,128]{2,1,0:T(8,128)(2,1)S(1)}, bf16[2,224,128]{2,1,0:T(8,128)(2,1)S(1)}, bf16[2,224,128]{2,1,0:T(8,128)(2,1)S(1)}) custom-call(s32[4]{0:T(128)S(1)} %pad_add_fusion.refs_0_.index_ref, bf16[8,8,16,128]{3,2,1,0:T(8,128)(2,1)S(1)} %pad_maximum_fusion.refs_0_, ...), custom_call_target="tpu_custom_call" | custom-call | flops 2751463424 | bytes 4194304 | tf_op jit(solution)/shard_map/group/pallas_call | solution.py:225
  26.2 1.8 %collective-permute-start.9 = (bf16[2,224,128]{2,1,0:T(8,128)(2,1)S(1)}, bf16[2,224,128]{2,1,0:T(8,128)(2,1)S(1)}, u32[]{:S(2)}, u32[]{:S(2)}) collective-permute-start(bf16[2,224,128]{2,1,0:T(8,128)(2,1)S(1)} %get-tuple-element.24), channel_id=1, source_target_pairs={{2,0},{3,1},{0,2},{1,3},{6,4},{7,5},{4,6},{5,7},{10,8},{11,9},{8,1... | collective-permute-start | bytes 344072 | tf_op jit(solution)/shard_map/ppermute | solution.py:25
  28.0 1.6 %collective-permute-start.10 = (bf16[2,224,128]{2,1,0:T(8,128)(2,1)S(1)}, bf16[2,224,128]{2,1,0:T(8,128)(2,1)S(1)}, u32[]{:S(2)}, u32[]{:S(2)}) collective-permute-start(bf16[2,224,128]{2,1,0:T(8,128)(2,1)S(1)} %get-tuple-element.25), channel_id=1, source_target_pairs={{4,0},{5,1},{6,2},{7,3},{0,4},{1,5},{2,6},{3,7},{12,8},{13,9},{14,... | collective-permute-start | bytes 344072 | tf_op jit(solution)/shard_map/ppermute | solution.py:25
  29.8 1.7 %collective-permute-done.9 = bf16[2,224,128]{2,1,0:T(8,128)(2,1)S(1)} collective-permute-done((bf16[2,224,128]{2,1,0:T(8,128)(2,1)S(1)}, bf16[2,224,128]{2,1,0:T(8,128)(2,1)S(1)}, u32[]{:S(2)}, u32[]{:S(2)}) %collective-permute-start.9) | collective-permute-done | bytes 114720 | tf_op jit(solution)/shard_map/ppermute | solution.py:25
  31.5 2.5 %collective-permute-done.10 = bf16[2,224,128]{2,1,0:T(8,128)(2,1)S(1)} collective-permute-done((bf16[2,224,128]{2,1,0:T(8,128)(2,1)S(1)}, bf16[2,224,128]{2,1,0:T(8,128)(2,1)S(1)}, u32[]{:S(2)}, u32[]{:S(2)}) %collective-permute-start.10) | collective-permute-done | bytes 114720 | tf_op jit(solution)/shard_map/ppermute | solution.py:25
  34.0 1.2 %collective-permute-done.11 = bf16[2,224,128]{2,1,0:T(8,128)(2,1)S(1)} collective-permute-done((bf16[2,224,128]{2,1,0:T(8,128)(2,1)S(1)}, bf16[2,224,128]{2,1,0:T(8,128)(2,1)S(1)}, u32[]{:S(2)}, u32[]{:S(2)}) %collective-permute-start.11) | collective-permute-done | bytes 114720 | tf_op jit(solution)/shard_map/ppermute | solution.py:25
  35.4 2.7 %collective-permute-start.12 = (bf16[2,224,128]{2,1,0:T(8,128)(2,1)S(1)}, bf16[2,224,128]{2,1,0:T(8,128)(2,1)S(1)}, u32[]{:S(2)}, u32[]{:S(2)}) collective-permute-start(bf16[2,224,128]{2,1,0:T(8,128)(2,1)S(1)} %reduce-precision_convert_fusion), channel_id=1, source_target_pairs={{8,0},{9,1},{10,2},{11,3},{12,4},{13,5},{14,6},{15,7},{0,8},{1,9},... | collective-permute-start | bytes 344072 | tf_op jit(solution)/shard_map/ppermute | solution.py:25
  38.1 2.2 %grad_in.1 = bf16[4,8,16,128]{3,2,1,0:T(8,128)(2,1)} custom-call(s32[4]{0:T(128)S(1)} %pad_add_fusion.refs_0_.index_ref, bf16[6,10,32,128]{3,2,1,0:T(8,128)(2,1)S(1)} %get-tuple-element.27.near_ref, bf16[4,8,16,128]{3,2,1,0:T(8,128)(2,1)S(1)} %copy-done.2, bf16[1152,384]{1,0:T(8,128)(2,1)S(1)} %get-tuple-element.28.w_ref), custom_call_target="tpu_custom_call" | custom-call | flops 603979776 | bytes 4194304 | tf_op jit(solution)/shard_map/grad_in/pallas_call | solution.py:225
  40.3 2.5 %collective-permute-done.12 = bf16[2,224,128]{2,1,0:T(8,128)(2,1)S(1)} collective-permute-done((bf16[2,224,128]{2,1,0:T(8,128)(2,1)S(1)}, bf16[2,224,128]{2,1,0:T(8,128)(2,1)S(1)}, u32[]{:S(2)}, u32[]{:S(2)}) %collective-permute-start.12) | collective-permute-done | bytes 114720 | tf_op jit(solution)/shard_map/ppermute | solution.py:25
  43.6 4.1 %collective-permute-done.13 = bf16[2,224,128]{2,1,0:T(8,128)(2,1)S(1)} collective-permute-done((bf16[2,224,128]{2,1,0:T(8,128)(2,1)S(1)}, bf16[2,224,128]{2,1,0:T(8,128)(2,1)S(1)}, u32[]{:S(2)}, u32[]{:S(2)}) %collective-permute-start.13) | collective-permute-done | bytes 114720 | tf_op jit(solution)/shard_map/ppermute | solution.py:25
  47.7 2.7 %collective-permute-start.16 = (bf16[4,224,128]{2,1,0:T(8,128)(2,1)S(1)}, bf16[4,224,128]{2,1,0:T(8,128)(2,1)S(1)}, u32[]{:S(2)}, u32[]{:S(2)}) collective-permute-start(bf16[4,224,128]{2,1,0:T(8,128)(2,1)S(1)} %pad_maximum_fusion.1.refs_0_), channel_id=1, source_target_pairs={{18,0},{19,1},{16,2},{17,3},{22,4},{23,5},{20,6},{21,7},{26,8},{27... | collective-permute-start | bytes 688136 | tf_op jit(solution)/shard_map/ppermute | solution.py:25
  51.3 4.8 %collective-permute-done.16.refs_3_ = bf16[4,224,128]{2,1,0:T(8,128)(2,1)S(1)} collective-permute-done((bf16[4,224,128]{2,1,0:T(8,128)(2,1)S(1)}, bf16[4,224,128]{2,1,0:T(8,128)(2,1)S(1)}, u32[]{:S(2)}, u32[]{:S(2)}) %collective-permute-start.16) | collective-permute-done | bytes 229408 | tf_op jit(solution)/shard_map/ppermute | solution.py:25
  56.0 2.2 %collective-permute-done.15.refs_2_ = bf16[4,224,128]{2,1,0:T(8,128)(2,1)S(1)} collective-permute-done((bf16[4,224,128]{2,1,0:T(8,128)(2,1)S(1)}, bf16[4,224,128]{2,1,0:T(8,128)(2,1)S(1)}, u32[]{:S(2)}, u32[]{:S(2)}) %collective-permute-start.15) | collective-permute-done | bytes 229408 | tf_op jit(solution)/shard_map/ppermute | solution.py:25
  58.7 1.0 %collective-permute-done.19.refs_6_ = bf16[4,224,128]{2,1,0:T(8,128)(2,1)S(1)} collective-permute-done((bf16[4,224,128]{2,1,0:T(8,128)(2,1)S(1)}, bf16[4,224,128]{2,1,0:T(8,128)(2,1)S(1)}, u32[]{:S(2)}, u32[]{:S(2)}) %collective-permute-start.19) | collective-permute-done | bytes 229408 | tf_op jit(solution)/shard_map/ppermute | solution.py:25
  60.0 1.8 %place.1 = (bf16[3456,128]{1,0:T(8,128)(2,1)}, bf16[3456,128]{1,0:T(8,128)(2,1)}) custom-call(s32[4]{0:T(128)S(1)} %pad_add_fusion.refs_0_.index_ref, bf16[4,224,128]{2,1,0:T(8,128)(2,1)S(1)} %pad_maximum_fusion.1.refs_0_, bf16[4,224,128]{2,1,0:T(8,128)(2,1)S(1)} %collective-permute-done.14.refs_1_, ...), custom_call_target="tpu_custom_call" | custom-call | tf_op jit(solution)/shard_map/place/pallas_call | solution.py:301
  (41 shorter events, 5.1 us)
Async XLA Ops:
  0.6 11.1 %copy-start = (bf16[27,128,128]{2,1,0:T(8,128)(2,1)S(1)}, bf16[27,128,128]{2,1,0:T(8,128)(2,1)}, u32[]{:S(2)}) copy-start(bf16[27,128,128]{2,1,0:T(8,128)(2,1)} %refs_1_.1) | copy-start | bytes 2654212
  2.6 14.3 %collective-permute-start.2 = (bf16[8,8,16,128]{3,2,1,0:T(8,128)(2,1)S(1)}, bf16[8,8,16,128]{3,2,1,0:T(8,128)(2,1)S(1)}, u32[]{:S(2)}, u32[]{:S(2)}) collective-permute-start(bf16[8,8,16,128]{3,2,1,0:T(8,128)(2,1)S(1)} %pad_maximum_fusion.refs_0_), channel_id=1, source_target_pairs={{16,0},{17,1},{18,2},{19,3},{20,4},{21,5},{22,6},{23,7},{24,8},{25... | collective-permute-start | bytes 786440 | tf_op jit(solution)/shard_map/ppermute | solution.py:25
  5.6 4.0 %copy-start.3 = (bf16[4,8,16,128]{3,2,1,0:T(8,128)(2,1)S(1)}, bf16[4,8,16,128]{3,2,1,0:T(8,128)(2,1)}, u32[]{:S(2)}) copy-start(bf16[4,8,16,128]{3,2,1,0:T(8,128)(2,1)} %refs_4_.1) | copy-start | bytes 393220
  5.7 8.3 %collective-permute-start.1 = (bf16[3,8,16,128]{3,2,1,0:T(8,128)(2,1)S(1)}, bf16[3,8,16,128]{3,2,1,0:T(8,128)(2,1)S(1)}, u32[]{:S(2)}, u32[]{:S(2)}) collective-permute-start(bf16[3,8,16,128]{3,2,1,0:T(8,128)(2,1)S(1)} %pad_maximum_fusion.3), channel_id=1, source_target_pairs={{31,0},{18,1},{17,2},{20,3},{19,4},{22,5},{21,6},{24,7},{23,8},{26... | collective-permute-start | bytes 294920 | tf_op jit(solution)/shard_map/ppermute | solution.py:25
  9.4 6.7 %collective-permute-start = (bf16[3,8,16,128]{3,2,1,0:T(8,128)(2,1)S(1)}, bf16[3,8,16,128]{3,2,1,0:T(8,128)(2,1)S(1)}, u32[]{:S(2)}, u32[]{:S(2)}) collective-permute-start(bf16[3,8,16,128]{3,2,1,0:T(8,128)(2,1)S(1)} %pad_maximum_fusion.3), channel_id=1, source_target_pairs={{15,0},{2,1},{1,2},{4,3},{3,4},{6,5},{5,6},{8,7},{7,8},{10,9},{9,1... | collective-permute-start | bytes 294920 | tf_op jit(solution)/shard_map/ppermute | solution.py:25
  9.6 9.2 %collective-permute-start.4 = (bf16[8,8,16,128]{3,2,1,0:T(8,128)(2,1)S(1)}, bf16[8,8,16,128]{3,2,1,0:T(8,128)(2,1)S(1)}, u32[]{:S(2)}, u32[]{:S(2)}) collective-permute-start(bf16[8,8,16,128]{3,2,1,0:T(8,128)(2,1)S(1)} %pad_maximum_fusion.refs_0_), channel_id=1, source_target_pairs={{1,0},{0,1},{3,2},{2,3},{5,4},{4,5},{7,6},{6,7},{9,8},{8,9},{11,10... | collective-permute-start | bytes 786440 | tf_op jit(solution)/shard_map/ppermute | solution.py:25
  9.7 7.2 %collective-permute-start.3 = (bf16[4,8,16,128]{3,2,1,0:T(8,128)(2,1)S(1)}, bf16[4,8,16,128]{3,2,1,0:T(8,128)(2,1)S(1)}, u32[]{:S(2)}, u32[]{:S(2)}) collective-permute-start(bf16[4,8,16,128]{3,2,1,0:T(8,128)(2,1)S(1)} %copy-done.3), channel_id=1, source_target_pairs={{16,0},{17,1},{18,2},{19,3},{20,4},{21,5},{22,6},{23,7},{24,8},{25... | collective-permute-start | bytes 393224 | tf_op jit(solution)/shard_map/ppermute | solution.py:25
  16.8 2.2 %collective-permute-start.5 = (bf16[8,8,16,128]{3,2,1,0:T(8,128)(2,1)S(1)}, bf16[8,8,16,128]{3,2,1,0:T(8,128)(2,1)S(1)}, u32[]{:S(2)}, u32[]{:S(2)}) collective-permute-start(bf16[8,8,16,128]{3,2,1,0:T(8,128)(2,1)S(1)} %collective-permute-done.2.refs_1_), channel_id=1, source_target_pairs={{1,0},{0,1},{3,2},{2,3},{5,4},{4,5},{7,6},{6,7},{9,8},{8,9},{11,10... | collective-permute-start | bytes 786440 | tf_op jit(solution)/shard_map/ppermute | solution.py:25
  16.8 2.2 %collective-permute-start.8 = (bf16[6,8,16,128]{3,2,1,0:T(8,128)(2,1)S(1)}, bf16[6,8,16,128]{3,2,1,0:T(8,128)(2,1)S(1)}, u32[]{:S(2)}, u32[]{:S(2)}) collective-permute-start(bf16[6,8,16,128]{3,2,1,0:T(8,128)(2,1)S(1)} %pad_maximum_fusion.2.refs_8_), channel_id=1, source_target_pairs={{1,0},{0,1},{3,2},{2,3},{5,4},{4,5},{7,6},{6,7},{9,8},{8,9},{11,10... | collective-permute-start | bytes 589832 | tf_op jit(solution)/shard_map/ppermute | solution.py:25
  17.4 1.5 %collective-permute-start.6 = (bf16[4,8,16,128]{3,2,1,0:T(8,128)(2,1)S(1)}, bf16[4,8,16,128]{3,2,1,0:T(8,128)(2,1)S(1)}, u32[]{:S(2)}, u32[]{:S(2)}) collective-permute-start(bf16[4,8,16,128]{3,2,1,0:T(8,128)(2,1)S(1)} %copy-done.3), channel_id=1, source_target_pairs={{1,0},{0,1},{3,2},{2,3},{5,4},{4,5},{7,6},{6,7},{9,8},{8,9},{11,10... | collective-permute-start | bytes 393224 | tf_op jit(solution)/shard_map/ppermute | solution.py:25
  17.4 1.7 %collective-permute-start.7 = (bf16[4,8,16,128]{3,2,1,0:T(8,128)(2,1)S(1)}, bf16[4,8,16,128]{3,2,1,0:T(8,128)(2,1)S(1)}, u32[]{:S(2)}, u32[]{:S(2)}) collective-permute-start(bf16[4,8,16,128]{3,2,1,0:T(8,128)(2,1)S(1)} %collective-permute-done.3.refs_5_), channel_id=1, source_target_pairs={{1,0},{0,1},{3,2},{2,3},{5,4},{4,5},{7,6},{6,7},{9,8},{8,9},{11,10... | collective-permute-start | bytes 393224 | tf_op jit(solution)/shard_map/ppermute | solution.py:25
  26.2 5.3 %collective-permute-start.9 = (bf16[2,224,128]{2,1,0:T(8,128)(2,1)S(1)}, bf16[2,224,128]{2,1,0:T(8,128)(2,1)S(1)}, u32[]{:S(2)}, u32[]{:S(2)}) collective-permute-start(bf16[2,224,128]{2,1,0:T(8,128)(2,1)S(1)} %get-tuple-element.24), channel_id=1, source_target_pairs={{2,0},{3,1},{0,2},{1,3},{6,4},{7,5},{4,6},{5,7},{10,8},{11,9},{8,1... | collective-permute-start | bytes 344072 | tf_op jit(solution)/shard_map/ppermute | solution.py:25
  28.0 6.0 %collective-permute-start.10 = (bf16[2,224,128]{2,1,0:T(8,128)(2,1)S(1)}, bf16[2,224,128]{2,1,0:T(8,128)(2,1)S(1)}, u32[]{:S(2)}, u32[]{:S(2)}) collective-permute-start(bf16[2,224,128]{2,1,0:T(8,128)(2,1)S(1)} %get-tuple-element.25), channel_id=1, source_target_pairs={{4,0},{5,1},{6,2},{7,3},{0,4},{1,5},{2,6},{3,7},{12,8},{13,9},{14,... | collective-permute-start | bytes 344072 | tf_op jit(solution)/shard_map/ppermute | solution.py:25
  29.6 5.7 %collective-permute-start.11 = (bf16[2,224,128]{2,1,0:T(8,128)(2,1)S(1)}, bf16[2,224,128]{2,1,0:T(8,128)(2,1)S(1)}, u32[]{:S(2)}, u32[]{:S(2)}) collective-permute-start(bf16[2,224,128]{2,1,0:T(8,128)(2,1)S(1)} %get-tuple-element.26), channel_id=1, source_target_pairs={{6,0},{7,1},{4,2},{5,3},{2,4},{3,5},{0,6},{1,7},{14,8},{15,9},{12,... | collective-permute-start | bytes 344072 | tf_op jit(solution)/shard_map/ppermute | solution.py:25
  35.3 2.8 %copy-start.2 = (bf16[4,8,16,128]{3,2,1,0:T(8,128)(2,1)S(1)}, bf16[4,8,16,128]{3,2,1,0:T(8,128)(2,1)}, u32[]{:S(2)}) copy-start(bf16[4,8,16,128]{3,2,1,0:T(8,128)(2,1)} %grad_out_ref.1) | copy-start | bytes 393220
  35.4 7.4 %collective-permute-start.12 = (bf16[2,224,128]{2,1,0:T(8,128)(2,1)S(1)}, bf16[2,224,128]{2,1,0:T(8,128)(2,1)S(1)}, u32[]{:S(2)}, u32[]{:S(2)}) collective-permute-start(bf16[2,224,128]{2,1,0:T(8,128)(2,1)S(1)} %reduce-precision_convert_fusion), channel_id=1, source_target_pairs={{8,0},{9,1},{10,2},{11,3},{12,4},{13,5},{14,6},{15,7},{0,8},{1,9},... | collective-permute-start | bytes 344072 | tf_op jit(solution)/shard_map/ppermute | solution.py:25
  42.8 4.9 %collective-permute-start.13 = (bf16[2,224,128]{2,1,0:T(8,128)(2,1)S(1)}, bf16[2,224,128]{2,1,0:T(8,128)(2,1)S(1)}, u32[]{:S(2)}, u32[]{:S(2)}) collective-permute-start(bf16[2,224,128]{2,1,0:T(8,128)(2,1)S(1)} %add_convert_fusion), channel_id=1, source_target_pairs={{4,0},{5,1},{6,2},{7,3},{0,4},{1,5},{2,6},{3,7},{12,8},{13,9},{14,... | collective-permute-start | bytes 344072 | tf_op jit(solution)/shard_map/ppermute | solution.py:25
  47.7 8.3 %collective-permute-start.16 = (bf16[4,224,128]{2,1,0:T(8,128)(2,1)S(1)}, bf16[4,224,128]{2,1,0:T(8,128)(2,1)S(1)}, u32[]{:S(2)}, u32[]{:S(2)}) collective-permute-start(bf16[4,224,128]{2,1,0:T(8,128)(2,1)S(1)} %pad_maximum_fusion.1.refs_0_), channel_id=1, source_target_pairs={{18,0},{19,1},{16,2},{17,3},{22,4},{23,5},{20,6},{21,7},{26,8},{27... | collective-permute-start | bytes 688136 | tf_op jit(solution)/shard_map/ppermute | solution.py:25
  50.4 7.7 %collective-permute-start.15 = (bf16[4,224,128]{2,1,0:T(8,128)(2,1)S(1)}, bf16[4,224,128]{2,1,0:T(8,128)(2,1)S(1)}, u32[]{:S(2)}, u32[]{:S(2)}) collective-permute-start(bf16[4,224,128]{2,1,0:T(8,128)(2,1)S(1)} %pad_maximum_fusion.1.refs_0_), channel_id=1, source_target_pairs={{16,0},{17,1},{18,2},{19,3},{20,4},{21,5},{22,6},{23,7},{24,8},{25... | collective-permute-start | bytes 688136 | tf_op jit(solution)/shard_map/ppermute | solution.py:25
  50.9 7.4 %collective-permute-start.14 = (bf16[4,224,128]{2,1,0:T(8,128)(2,1)S(1)}, bf16[4,224,128]{2,1,0:T(8,128)(2,1)S(1)}, u32[]{:S(2)}, u32[]{:S(2)}) collective-permute-start(bf16[4,224,128]{2,1,0:T(8,128)(2,1)S(1)} %pad_maximum_fusion.1.refs_0_), channel_id=1, source_target_pairs={{2,0},{3,1},{0,2},{1,3},{6,4},{7,5},{4,6},{5,7},{10,8},{11,9},{8,1... | collective-permute-start | bytes 688136 | tf_op jit(solution)/shard_map/ppermute | solution.py:25
  51.2 7.5 %collective-permute-start.17 = (bf16[4,224,128]{2,1,0:T(8,128)(2,1)S(1)}, bf16[4,224,128]{2,1,0:T(8,128)(2,1)S(1)}, u32[]{:S(2)}, u32[]{:S(2)}) collective-permute-start(bf16[4,224,128]{2,1,0:T(8,128)(2,1)S(1)} %pad_maximum_fusion.1.refs_0_), channel_id=1, source_target_pairs={{1,0},{0,1},{3,2},{2,3},{5,4},{4,5},{7,6},{6,7},{9,8},{8,9},{11,10... | collective-permute-start | bytes 688136 | tf_op jit(solution)/shard_map/ppermute | solution.py:25
  56.0 2.7 %collective-permute-start.20 = (bf16[4,224,128]{2,1,0:T(8,128)(2,1)S(1)}, bf16[4,224,128]{2,1,0:T(8,128)(2,1)S(1)}, u32[]{:S(2)}, u32[]{:S(2)}) collective-permute-start(bf16[4,224,128]{2,1,0:T(8,128)(2,1)S(1)} %collective-permute-done.16.refs_3_), channel_id=1, source_target_pairs={{1,0},{0,1},{3,2},{2,3},{5,4},{4,5},{7,6},{6,7},{9,8},{8,9},{11,10... | collective-permute-start | bytes 688136 | tf_op jit(solution)/shard_map/ppermute | solution.py:25
  58.2 1.5 %collective-permute-start.19 = (bf16[4,224,128]{2,1,0:T(8,128)(2,1)S(1)}, bf16[4,224,128]{2,1,0:T(8,128)(2,1)S(1)}, u32[]{:S(2)}, u32[]{:S(2)}) collective-permute-start(bf16[4,224,128]{2,1,0:T(8,128)(2,1)S(1)} %collective-permute-done.15.refs_2_), channel_id=1, source_target_pairs={{1,0},{0,1},{3,2},{2,3},{5,4},{4,5},{7,6},{6,7},{9,8},{8,9},{11,10... | collective-permute-start | bytes 688136 | tf_op jit(solution)/shard_map/ppermute | solution.py:25
  58.2 1.8 %collective-permute-start.18 = (bf16[4,224,128]{2,1,0:T(8,128)(2,1)S(1)}, bf16[4,224,128]{2,1,0:T(8,128)(2,1)S(1)}, u32[]{:S(2)}, u32[]{:S(2)}) collective-permute-start(bf16[4,224,128]{2,1,0:T(8,128)(2,1)S(1)} %collective-permute-done.14.refs_1_), channel_id=1, source_target_pairs={{1,0},{0,1},{3,2},{2,3},{5,4},{4,5},{7,6},{6,7},{9,8},{8,9},{11,10... | collective-permute-start | bytes 688136 | tf_op jit(solution)/shard_map/ppermute | solution.py:25
  (1 other events, 1.2 us)

commit v5 on v4

--- a/solution.py
+++ b/solution.py
@@ -167,7 +167,7 @@
         [ref.at[pl.ds(3 * r, 3)] for r in range(slabs)] for ref in refs[2 * slabs : 2 * slabs + 2]
     )
     w_second_ref, near_ref, keep_ref, *refs = refs[2 * slabs + 2 :]
-    *sent_refs, field_ref, first_ref, pre_ref, left_ref, parts_ref, scratch_ref = refs
+    *sent_refs, field_ref, first_ref, pre_ref, left_ref, act_ref, parts_ref, scratch_ref = refs
     me, pair = index_ref[0], index_ref[2]
     width, ny, zs, chans = in_own[0].shape
     nz = zs * slabs
@@ -188,6 +188,8 @@
     def put_first(i, grad_act):
         pre = pre_of(i)
         sig = sigmoid(pre)
+        at = pl.multiple_of(i * ny * nz, ny * nz)
+        act_ref[pl.ds(at, ny * nz), :] = (pre * sig).astype(BF16).reshape(ny * nz, chans)
         put_planes(first_ref, i, grad_act * (sig * (1.0 + pre * (1.0 - sig))))
 
     convolve(field_ref, 1, 2 * width + 2, nz, w_second_ref, parts_ref, put_first)
@@ -201,11 +203,8 @@
     kernel_terms(left_ref, first_ref, 1, 2 * width, nz, scratch_ref, index_ref, per, scale)
     put_chunks(scratch_ref, keep_ref, sent_refs, pair, 0)
 
-    for i in range(2 * width):
-        pre = pre_of(1 + i)
-        act = (pre * sigmoid(pre)).astype(BF16)
-        left_ref[pl.ds(i * ny * nz, ny * nz), :] = act.reshape(ny * nz, chans)
-    kernel_terms(left_ref, field_ref, 2, 2 * width, nz, scratch_ref, index_ref, per, scale)
+    act_group = act_ref.at[pl.ds(ny * nz, 2 * width * ny * nz)]
+    kernel_terms(act_group, field_ref, 2, 2 * width, nz, scratch_ref, index_ref, per, scale)
     put_chunks(scratch_ref, keep_ref, sent_refs, pair, 1)
 
 
@@ -215,7 +214,7 @@
 
 def vmem_bytes(scratch):
     held = sum(math.prod(v.shape) * v.dtype.itemsize for v in scratch)
-    return (12 << 20) + held * 3 // 2
+    return min((12 << 20) + held * 3 // 2, 62 << 20)
 
 
 def call(body, index, operands, out_shape, scratch, flops, name):
@@ -371,6 +370,7 @@
             vmem((3, 2 * width + 2, ny + 2, nz, chans), BF16),
             vmem((2 * width + 2, ny, nz, chans), F32),
             vmem((group, chans), BF16),
+            vmem((group + 2 * ny * nz, chans), BF16),
             parts,
             vmem((per * chans, chans), F32),
         ],

time: 62.1 us -> 61.9 us (level)
  no operation moved by 1% of the time
where the time goes in v5:
time: 61.9 us; the launch traced here: 61.6 us
  waiting for transfers between devices  24.4 us (39%)
  starting transfers between devices  21.1 us (34%)
  Pallas kernels  12 us (19%)
  other arithmetic  2.17 us (4%)
  local copies, waits for them, and re-layouts  1.18 us (2%)
  between operations  0.73 us (1%)
    ppermute x21, waiting for transfers between devices, send(): return lax.ppermute(value, AXES, pairs)  24.4 us
    ppermute x21, starting transfers between devices, send(): return lax.ppermute(value, AXES, pairs)  21.1 us
    pallas_call x3, Pallas kernels, call(): pl.pallas_call(body, out_shape=out_shape, in_specs=[space(v) for v in (in...  10.1 us
    pallas_call x1, Pallas kernels, place(): pl.pallas_call(functools.partial(place_kernel, slabs, pairs, held), out_s...  1.82 us
  transfers between devices with their start and end apart: 21, of which 13 were waited for; matrix products, arithmetic and copies ran while one was open for 0% of the time, Pallas kernels for 5%

profile of v5, /device:TPU:0, one launch (start us, length us, event | category | flops | bytes accessed | tf_op | source)
XLA Modules:
  0.0 61.6 jit_solution(18086847884133594347)
XLA Ops:
  0.6 0.8 %broadcast_compare_fusion = pred[4,8,16]{2,1,0:T(8,128)(4,1)S(1)} fusion(s32[4,8,16]{2,1,0:T(8,128)} %param.8), kind=kLoop, calls=%fused_computation.10 | loop fusion | flops 512 | bytes 2560 | tf_op jit(solution)/shard_map/ne | solution.py:326
  1.4 1.1 %broadcast_select_fusion.1 = (bf16[4,8,16,128]{3,2,1,0:T(8,128)(2,1)S(1)}, bf16[4,8,16,128]{3,2,1,0:T(8,128)(2,1)S(1)}) fusion(bf16[4,8,16,128]{3,2,1,0:T(8,128)(2,1)} %grad_out_ref.1, pred[4,8,16]{2,1,0:T(8,128)(4,1)S(1)} %broadcast_compare_fusion, bf16[4,8,16,128]{3,2,1,0:T(8,128)(2,1)} %param.7), kind=kLoop, calls=%fused_computation.6 | loop fusion | flops 131072 | bytes 524800 | tf_op jit(solution)/shard_map/jit(_where)/select_n | solution.py:327
  2.6 3.0 %collective-permute-start.2 = (bf16[8,8,16,128]{3,2,1,0:T(8,128)(2,1)S(1)}, bf16[8,8,16,128]{3,2,1,0:T(8,128)(2,1)S(1)}, u32[]{:S(2)}, u32[]{:S(2)}) collective-permute-start(bf16[8,8,16,128]{3,2,1,0:T(8,128)(2,1)S(1)} %pad_maximum_fusion.refs_0_), channel_id=1, source_target_pairs={{16,0},{17,1},{18,2},{19,3},{20,4},{21,5},{22,6},{23,7},{24,8},{25... | collective-permute-start | bytes 786440 | tf_op jit(solution)/shard_map/ppermute | solution.py:25
  5.7 3.7 %collective-permute-start.1 = (bf16[3,8,16,128]{3,2,1,0:T(8,128)(2,1)S(1)}, bf16[3,8,16,128]{3,2,1,0:T(8,128)(2,1)S(1)}, u32[]{:S(2)}, u32[]{:S(2)}) collective-permute-start(bf16[3,8,16,128]{3,2,1,0:T(8,128)(2,1)S(1)} %pad_maximum_fusion.3), channel_id=1, source_target_pairs={{31,0},{18,1},{17,2},{20,3},{19,4},{22,5},{21,6},{24,7},{23,8},{26... | collective-permute-start | bytes 294920 | tf_op jit(solution)/shard_map/ppermute | solution.py:25
  9.7 2.0 %collective-permute-start.3 = (bf16[4,8,16,128]{3,2,1,0:T(8,128)(2,1)S(1)}, bf16[4,8,16,128]{3,2,1,0:T(8,128)(2,1)S(1)}, u32[]{:S(2)}, u32[]{:S(2)}) collective-permute-start(bf16[4,8,16,128]{3,2,1,0:T(8,128)(2,1)S(1)} %copy-done.3), channel_id=1, source_target_pairs={{16,0},{17,1},{18,2},{19,3},{20,4},{21,5},{22,6},{23,7},{24,8},{25... | collective-permute-start | bytes 393224 | tf_op jit(solution)/shard_map/ppermute | solution.py:25
  11.7 1.2 %copy-done.1 = bf16[27,128,128]{2,1,0:T(8,128)(2,1)S(1)} copy-done((bf16[27,128,128]{2,1,0:T(8,128)(2,1)S(1)}, bf16[27,128,128]{2,1,0:T(8,128)(2,1)}, u32[]{:S(2)}) %copy-start.1) | copy-done | bytes 884760
  12.9 1.1 %kernels_side_by_side.1 = (bf16[1152,384]{1,0:T(8,128)(2,1)S(1)}, bf16[1152,384]{1,0:T(8,128)(2,1)S(1)}) custom-call(s32[4]{0:T(128)S(1)} %pad_add_fusion.refs_0_.index_ref, bf16[27,128,128]{2,1,0:T(8,128)(2,1)S(1)} %copy-done, bf16[27,128,128]{2,1,0:T(8,128)(2,1)S(1)} %copy-done.1), custom_call_target="tpu_custom_call" | custom-call | bytes 4194304 | tf_op jit(solution)/shard_map/kernels_side_by_side/pallas_call | solution.py:224
  14.0 2.1 %collective-permute-done = bf16[3,8,16,128]{3,2,1,0:T(8,128)(2,1)S(1)} collective-permute-done((bf16[3,8,16,128]{3,2,1,0:T(8,128)(2,1)S(1)}, bf16[3,8,16,128]{3,2,1,0:T(8,128)(2,1)S(1)}, u32[]{:S(2)}, u32[]{:S(2)}) %collective-permute-start) | collective-permute-done | bytes 98336 | tf_op jit(solution)/shard_map/ppermute | solution.py:25
  17.9 1.0 %collective-permute-done.6.refs_6_ = bf16[4,8,16,128]{3,2,1,0:T(8,128)(2,1)S(1)} collective-permute-done((bf16[4,8,16,128]{3,2,1,0:T(8,128)(2,1)S(1)}, bf16[4,8,16,128]{3,2,1,0:T(8,128)(2,1)S(1)}, u32[]{:S(2)}, u32[]{:S(2)}) %collective-permute-start.6) | collective-permute-done | bytes 131104 | tf_op jit(solution)/shard_map/ppermute | solution.py:25
  19.0 6.9 %group.1 = (bf16[6,10,32,128]{3,2,1,0:T(8,128)(2,1)S(1)}, f32[2,224,128]{2,1,0:T(8,128)S(1)}, bf16[2,224,128]{2,1,0:T(8,128)(2,1)S(1)}, bf16[2,224,128]{2,1,0:T(8,128)(2,1)S(1)}, bf16[2,224,128]{2,1,0:T(8,128)(2,1)S(1)}) custom-call(s32[4]{0:T(128)S(1)} %pad_add_fusion.refs_0_.index_ref, bf16[8,8,16,128]{3,2,1,0:T(8,128)(2,1)S(1)} %pad_maximum_fusion.refs_0_, ...), custom_call_target="tpu_custom_call" | custom-call | flops 2751463424 | bytes 4194304 | tf_op jit(solution)/shard_map/group/pallas_call | solution.py:224
  26.0 1.8 %collective-permute-start.9 = (bf16[2,224,128]{2,1,0:T(8,128)(2,1)S(1)}, bf16[2,224,128]{2,1,0:T(8,128)(2,1)S(1)}, u32[]{:S(2)}, u32[]{:S(2)}) collective-permute-start(bf16[2,224,128]{2,1,0:T(8,128)(2,1)S(1)} %get-tuple-element.24), channel_id=1, source_target_pairs={{2,0},{3,1},{0,2},{1,3},{6,4},{7,5},{4,6},{5,7},{10,8},{11,9},{8,1... | collective-permute-start | bytes 344072 | tf_op jit(solution)/shard_map/ppermute | solution.py:25
  27.7 1.6 %collective-permute-start.10 = (bf16[2,224,128]{2,1,0:T(8,128)(2,1)S(1)}, bf16[2,224,128]{2,1,0:T(8,128)(2,1)S(1)}, u32[]{:S(2)}, u32[]{:S(2)}) collective-permute-start(bf16[2,224,128]{2,1,0:T(8,128)(2,1)S(1)} %get-tuple-element.25), channel_id=1, source_target_pairs={{4,0},{5,1},{6,2},{7,3},{0,4},{1,5},{2,6},{3,7},{12,8},{13,9},{14,... | collective-permute-start | bytes 344072 | tf_op jit(solution)/shard_map/ppermute | solution.py:25
  29.5 1.7 %collective-permute-done.9 = bf16[2,224,128]{2,1,0:T(8,128)(2,1)S(1)} collective-permute-done((bf16[2,224,128]{2,1,0:T(8,128)(2,1)S(1)}, bf16[2,224,128]{2,1,0:T(8,128)(2,1)S(1)}, u32[]{:S(2)}, u32[]{:S(2)}) %collective-permute-start.9) | collective-permute-done | bytes 114720 | tf_op jit(solution)/shard_map/ppermute | solution.py:25
  31.2 2.5 %collective-permute-done.10 = bf16[2,224,128]{2,1,0:T(8,128)(2,1)S(1)} collective-permute-done((bf16[2,224,128]{2,1,0:T(8,128)(2,1)S(1)}, bf16[2,224,128]{2,1,0:T(8,128)(2,1)S(1)}, u32[]{:S(2)}, u32[]{:S(2)}) %collective-permute-start.10) | collective-permute-done | bytes 114720 | tf_op jit(solution)/shard_map/ppermute | solution.py:25
  33.8 1.2 %collective-permute-done.11 = bf16[2,224,128]{2,1,0:T(8,128)(2,1)S(1)} collective-permute-done((bf16[2,224,128]{2,1,0:T(8,128)(2,1)S(1)}, bf16[2,224,128]{2,1,0:T(8,128)(2,1)S(1)}, u32[]{:S(2)}, u32[]{:S(2)}) %collective-permute-start.11) | collective-permute-done | bytes 114720 | tf_op jit(solution)/shard_map/ppermute | solution.py:25
  35.1 2.7 %collective-permute-start.12 = (bf16[2,224,128]{2,1,0:T(8,128)(2,1)S(1)}, bf16[2,224,128]{2,1,0:T(8,128)(2,1)S(1)}, u32[]{:S(2)}, u32[]{:S(2)}) collective-permute-start(bf16[2,224,128]{2,1,0:T(8,128)(2,1)S(1)} %reduce-precision_convert_fusion), channel_id=1, source_target_pairs={{8,0},{9,1},{10,2},{11,3},{12,4},{13,5},{14,6},{15,7},{0,8},{1,9},... | collective-permute-start | bytes 344072 | tf_op jit(solution)/shard_map/ppermute | solution.py:25
  37.8 2.2 %grad_in.1 = bf16[4,8,16,128]{3,2,1,0:T(8,128)(2,1)} custom-call(s32[4]{0:T(128)S(1)} %pad_add_fusion.refs_0_.index_ref, bf16[6,10,32,128]{3,2,1,0:T(8,128)(2,1)S(1)} %get-tuple-element.27.near_ref, bf16[4,8,16,128]{3,2,1,0:T(8,128)(2,1)S(1)} %copy-done.2, bf16[1152,384]{1,0:T(8,128)(2,1)S(1)} %get-tuple-element.28.w_ref), custom_call_target="tpu_custom_call" | custom-call | flops 603979776 | bytes 4194304 | tf_op jit(solution)/shard_map/grad_in/pallas_call | solution.py:224
  40.0 2.5 %collective-permute-done.12 = bf16[2,224,128]{2,1,0:T(8,128)(2,1)S(1)} collective-permute-done((bf16[2,224,128]{2,1,0:T(8,128)(2,1)S(1)}, bf16[2,224,128]{2,1,0:T(8,128)(2,1)S(1)}, u32[]{:S(2)}, u32[]{:S(2)}) %collective-permute-start.12) | collective-permute-done | bytes 114720 | tf_op jit(solution)/shard_map/ppermute | solution.py:25
  43.3 4.1 %collective-permute-done.13 = bf16[2,224,128]{2,1,0:T(8,128)(2,1)S(1)} collective-permute-done((bf16[2,224,128]{2,1,0:T(8,128)(2,1)S(1)}, bf16[2,224,128]{2,1,0:T(8,128)(2,1)S(1)}, u32[]{:S(2)}, u32[]{:S(2)}) %collective-permute-start.13) | collective-permute-done | bytes 114720 | tf_op jit(solution)/shard_map/ppermute | solution.py:25
  47.4 2.8 %collective-permute-start.16 = (bf16[4,224,128]{2,1,0:T(8,128)(2,1)S(1)}, bf16[4,224,128]{2,1,0:T(8,128)(2,1)S(1)}, u32[]{:S(2)}, u32[]{:S(2)}) collective-permute-start(bf16[4,224,128]{2,1,0:T(8,128)(2,1)S(1)} %pad_maximum_fusion.1.refs_0_), channel_id=1, source_target_pairs={{18,0},{19,1},{16,2},{17,3},{22,4},{23,5},{20,6},{21,7},{26,8},{27... | collective-permute-start | bytes 688136 | tf_op jit(solution)/shard_map/ppermute | solution.py:25
  51.0 4.8 %collective-permute-done.16.refs_3_ = bf16[4,224,128]{2,1,0:T(8,128)(2,1)S(1)} collective-permute-done((bf16[4,224,128]{2,1,0:T(8,128)(2,1)S(1)}, bf16[4,224,128]{2,1,0:T(8,128)(2,1)S(1)}, u32[]{:S(2)}, u32[]{:S(2)}) %collective-permute-start.16) | collective-permute-done | bytes 229408 | tf_op jit(solution)/shard_map/ppermute | solution.py:25
  55.8 2.2 %collective-permute-done.15.refs_2_ = bf16[4,224,128]{2,1,0:T(8,128)(2,1)S(1)} collective-permute-done((bf16[4,224,128]{2,1,0:T(8,128)(2,1)S(1)}, bf16[4,224,128]{2,1,0:T(8,128)(2,1)S(1)}, u32[]{:S(2)}, u32[]{:S(2)}) %collective-permute-start.15) | collective-permute-done | bytes 229408 | tf_op jit(solution)/shard_map/ppermute | solution.py:25
  58.5 1.0 %collective-permute-done.19.refs_6_ = bf16[4,224,128]{2,1,0:T(8,128)(2,1)S(1)} collective-permute-done((bf16[4,224,128]{2,1,0:T(8,128)(2,1)S(1)}, bf16[4,224,128]{2,1,0:T(8,128)(2,1)S(1)}, u32[]{:S(2)}, u32[]{:S(2)}) %collective-permute-start.19) | collective-permute-done | bytes 229408 | tf_op jit(solution)/shard_map/ppermute | solution.py:25
  59.8 1.8 %place.1 = (bf16[3456,128]{1,0:T(8,128)(2,1)}, bf16[3456,128]{1,0:T(8,128)(2,1)}) custom-call(s32[4]{0:T(128)S(1)} %pad_add_fusion.refs_0_.index_ref, bf16[4,224,128]{2,1,0:T(8,128)(2,1)S(1)} %pad_maximum_fusion.1.refs_0_, bf16[4,224,128]{2,1,0:T(8,128)(2,1)S(1)} %collective-permute-done.14.refs_1_, ...), custom_call_target="tpu_custom_call" | custom-call | tf_op jit(solution)/shard_map/place/pallas_call | solution.py:300
  (41 shorter events, 5.1 us)
Async XLA Ops:
  0.6 11.1 %copy-start = (bf16[27,128,128]{2,1,0:T(8,128)(2,1)S(1)}, bf16[27,128,128]{2,1,0:T(8,128)(2,1)}, u32[]{:S(2)}) copy-start(bf16[27,128,128]{2,1,0:T(8,128)(2,1)} %refs_1_.1) | copy-start | bytes 2654212
  2.6 14.3 %collective-permute-start.2 = (bf16[8,8,16,128]{3,2,1,0:T(8,128)(2,1)S(1)}, bf16[8,8,16,128]{3,2,1,0:T(8,128)(2,1)S(1)}, u32[]{:S(2)}, u32[]{:S(2)}) collective-permute-start(bf16[8,8,16,128]{3,2,1,0:T(8,128)(2,1)S(1)} %pad_maximum_fusion.refs_0_), channel_id=1, source_target_pairs={{16,0},{17,1},{18,2},{19,3},{20,4},{21,5},{22,6},{23,7},{24,8},{25... | collective-permute-start | bytes 786440 | tf_op jit(solution)/shard_map/ppermute | solution.py:25
  5.6 4.0 %copy-start.3 = (bf16[4,8,16,128]{3,2,1,0:T(8,128)(2,1)S(1)}, bf16[4,8,16,128]{3,2,1,0:T(8,128)(2,1)}, u32[]{:S(2)}) copy-start(bf16[4,8,16,128]{3,2,1,0:T(8,128)(2,1)} %refs_4_.1) | copy-start | bytes 393220
  5.7 8.3 %collective-permute-start.1 = (bf16[3,8,16,128]{3,2,1,0:T(8,128)(2,1)S(1)}, bf16[3,8,16,128]{3,2,1,0:T(8,128)(2,1)S(1)}, u32[]{:S(2)}, u32[]{:S(2)}) collective-permute-start(bf16[3,8,16,128]{3,2,1,0:T(8,128)(2,1)S(1)} %pad_maximum_fusion.3), channel_id=1, source_target_pairs={{31,0},{18,1},{17,2},{20,3},{19,4},{22,5},{21,6},{24,7},{23,8},{26... | collective-permute-start | bytes 294920 | tf_op jit(solution)/shard_map/ppermute | solution.py:25
  9.4 6.7 %collective-permute-start = (bf16[3,8,16,128]{3,2,1,0:T(8,128)(2,1)S(1)}, bf16[3,8,16,128]{3,2,1,0:T(8,128)(2,1)S(1)}, u32[]{:S(2)}, u32[]{:S(2)}) collective-permute-start(bf16[3,8,16,128]{3,2,1,0:T(8,128)(2,1)S(1)} %pad_maximum_fusion.3), channel_id=1, source_target_pairs={{15,0},{2,1},{1,2},{4,3},{3,4},{6,5},{5,6},{8,7},{7,8},{10,9},{9,1... | collective-permute-start | bytes 294920 | tf_op jit(solution)/shard_map/ppermute | solution.py:25
  9.6 9.2 %collective-permute-start.4 = (bf16[8,8,16,128]{3,2,1,0:T(8,128)(2,1)S(1)}, bf16[8,8,16,128]{3,2,1,0:T(8,128)(2,1)S(1)}, u32[]{:S(2)}, u32[]{:S(2)}) collective-permute-start(bf16[8,8,16,128]{3,2,1,0:T(8,128)(2,1)S(1)} %pad_maximum_fusion.refs_0_), channel_id=1, source_target_pairs={{1,0},{0,1},{3,2},{2,3},{5,4},{4,5},{7,6},{6,7},{9,8},{8,9},{11,10... | collective-permute-start | bytes 786440 | tf_op jit(solution)/shard_map/ppermute | solution.py:25
  9.7 7.2 %collective-permute-start.3 = (bf16[4,8,16,128]{3,2,1,0:T(8,128)(2,1)S(1)}, bf16[4,8,16,128]{3,2,1,0:T(8,128)(2,1)S(1)}, u32[]{:S(2)}, u32[]{:S(2)}) collective-permute-start(bf16[4,8,16,128]{3,2,1,0:T(8,128)(2,1)S(1)} %copy-done.3), channel_id=1, source_target_pairs={{16,0},{17,1},{18,2},{19,3},{20,4},{21,5},{22,6},{23,7},{24,8},{25... | collective-permute-start | bytes 393224 | tf_op jit(solution)/shard_map/ppermute | solution.py:25
  16.8 2.2 %collective-permute-start.5 = (bf16[8,8,16,128]{3,2,1,0:T(8,128)(2,1)S(1)}, bf16[8,8,16,128]{3,2,1,0:T(8,128)(2,1)S(1)}, u32[]{:S(2)}, u32[]{:S(2)}) collective-permute-start(bf16[8,8,16,128]{3,2,1,0:T(8,128)(2,1)S(1)} %collective-permute-done.2.refs_1_), channel_id=1, source_target_pairs={{1,0},{0,1},{3,2},{2,3},{5,4},{4,5},{7,6},{6,7},{9,8},{8,9},{11,10... | collective-permute-start | bytes 786440 | tf_op jit(solution)/shard_map/ppermute | solution.py:25
  16.8 2.2 %collective-permute-start.8 = (bf16[6,8,16,128]{3,2,1,0:T(8,128)(2,1)S(1)}, bf16[6,8,16,128]{3,2,1,0:T(8,128)(2,1)S(1)}, u32[]{:S(2)}, u32[]{:S(2)}) collective-permute-start(bf16[6,8,16,128]{3,2,1,0:T(8,128)(2,1)S(1)} %pad_maximum_fusion.2.refs_8_), channel_id=1, source_target_pairs={{1,0},{0,1},{3,2},{2,3},{5,4},{4,5},{7,6},{6,7},{9,8},{8,9},{11,10... | collective-permute-start | bytes 589832 | tf_op jit(solution)/shard_map/ppermute | solution.py:25
  17.4 1.5 %collective-permute-start.6 = (bf16[4,8,16,128]{3,2,1,0:T(8,128)(2,1)S(1)}, bf16[4,8,16,128]{3,2,1,0:T(8,128)(2,1)S(1)}, u32[]{:S(2)}, u32[]{:S(2)}) collective-permute-start(bf16[4,8,16,128]{3,2,1,0:T(8,128)(2,1)S(1)} %copy-done.3), channel_id=1, source_target_pairs={{1,0},{0,1},{3,2},{2,3},{5,4},{4,5},{7,6},{6,7},{9,8},{8,9},{11,10... | collective-permute-start | bytes 393224 | tf_op jit(solution)/shard_map/ppermute | solution.py:25
  17.4 1.7 %collective-permute-start.7 = (bf16[4,8,16,128]{3,2,1,0:T(8,128)(2,1)S(1)}, bf16[4,8,16,128]{3,2,1,0:T(8,128)(2,1)S(1)}, u32[]{:S(2)}, u32[]{:S(2)}) collective-permute-start(bf16[4,8,16,128]{3,2,1,0:T(8,128)(2,1)S(1)} %collective-permute-done.3.refs_5_), channel_id=1, source_target_pairs={{1,0},{0,1},{3,2},{2,3},{5,4},{4,5},{7,6},{6,7},{9,8},{8,9},{11,10... | collective-permute-start | bytes 393224 | tf_op jit(solution)/shard_map/ppermute | solution.py:25
  26.0 5.3 %collective-permute-start.9 = (bf16[2,224,128]{2,1,0:T(8,128)(2,1)S(1)}, bf16[2,224,128]{2,1,0:T(8,128)(2,1)S(1)}, u32[]{:S(2)}, u32[]{:S(2)}) collective-permute-start(bf16[2,224,128]{2,1,0:T(8,128)(2,1)S(1)} %get-tuple-element.24), channel_id=1, source_target_pairs={{2,0},{3,1},{0,2},{1,3},{6,4},{7,5},{4,6},{5,7},{10,8},{11,9},{8,1... | collective-permute-start | bytes 344072 | tf_op jit(solution)/shard_map/ppermute | solution.py:25
  27.7 6.0 %collective-permute-start.10 = (bf16[2,224,128]{2,1,0:T(8,128)(2,1)S(1)}, bf16[2,224,128]{2,1,0:T(8,128)(2,1)S(1)}, u32[]{:S(2)}, u32[]{:S(2)}) collective-permute-start(bf16[2,224,128]{2,1,0:T(8,128)(2,1)S(1)} %get-tuple-element.25), channel_id=1, source_target_pairs={{4,0},{5,1},{6,2},{7,3},{0,4},{1,5},{2,6},{3,7},{12,8},{13,9},{14,... | collective-permute-start | bytes 344072 | tf_op jit(solution)/shard_map/ppermute | solution.py:25
  29.3 5.7 %collective-permute-start.11 = (bf16[2,224,128]{2,1,0:T(8,128)(2,1)S(1)}, bf16[2,224,128]{2,1,0:T(8,128)(2,1)S(1)}, u32[]{:S(2)}, u32[]{:S(2)}) collective-permute-start(bf16[2,224,128]{2,1,0:T(8,128)(2,1)S(1)} %get-tuple-element.26), channel_id=1, source_target_pairs={{6,0},{7,1},{4,2},{5,3},{2,4},{3,5},{0,6},{1,7},{14,8},{15,9},{12,... | collective-permute-start | bytes 344072 | tf_op jit(solution)/shard_map/ppermute | solution.py:25
  35.0 2.8 %copy-start.2 = (bf16[4,8,16,128]{3,2,1,0:T(8,128)(2,1)S(1)}, bf16[4,8,16,128]{3,2,1,0:T(8,128)(2,1)}, u32[]{:S(2)}) copy-start(bf16[4,8,16,128]{3,2,1,0:T(8,128)(2,1)} %grad_out_ref.1) | copy-start | bytes 393220
  35.1 7.4 %collective-permute-start.12 = (bf16[2,224,128]{2,1,0:T(8,128)(2,1)S(1)}, bf16[2,224,128]{2,1,0:T(8,128)(2,1)S(1)}, u32[]{:S(2)}, u32[]{:S(2)}) collective-permute-start(bf16[2,224,128]{2,1,0:T(8,128)(2,1)S(1)} %reduce-precision_convert_fusion), channel_id=1, source_target_pairs={{8,0},{9,1},{10,2},{11,3},{12,4},{13,5},{14,6},{15,7},{0,8},{1,9},... | collective-permute-start | bytes 344072 | tf_op jit(solution)/shard_map/ppermute | solution.py:25
  42.5 4.9 %collective-permute-start.13 = (bf16[2,224,128]{2,1,0:T(8,128)(2,1)S(1)}, bf16[2,224,128]{2,1,0:T(8,128)(2,1)S(1)}, u32[]{:S(2)}, u32[]{:S(2)}) collective-permute-start(bf16[2,224,128]{2,1,0:T(8,128)(2,1)S(1)} %add_convert_fusion), channel_id=1, source_target_pairs={{4,0},{5,1},{6,2},{7,3},{0,4},{1,5},{2,6},{3,7},{12,8},{13,9},{14,... | collective-permute-start | bytes 344072 | tf_op jit(solution)/shard_map/ppermute | solution.py:25
  47.4 8.4 %collective-permute-start.16 = (bf16[4,224,128]{2,1,0:T(8,128)(2,1)S(1)}, bf16[4,224,128]{2,1,0:T(8,128)(2,1)S(1)}, u32[]{:S(2)}, u32[]{:S(2)}) collective-permute-start(bf16[4,224,128]{2,1,0:T(8,128)(2,1)S(1)} %pad_maximum_fusion.1.refs_0_), channel_id=1, source_target_pairs={{18,0},{19,1},{16,2},{17,3},{22,4},{23,5},{20,6},{21,7},{26,8},{27... | collective-permute-start | bytes 688136 | tf_op jit(solution)/shard_map/ppermute | solution.py:25
  50.2 7.8 %collective-permute-start.15 = (bf16[4,224,128]{2,1,0:T(8,128)(2,1)S(1)}, bf16[4,224,128]{2,1,0:T(8,128)(2,1)S(1)}, u32[]{:S(2)}, u32[]{:S(2)}) collective-permute-start(bf16[4,224,128]{2,1,0:T(8,128)(2,1)S(1)} %pad_maximum_fusion.1.refs_0_), channel_id=1, source_target_pairs={{16,0},{17,1},{18,2},{19,3},{20,4},{21,5},{22,6},{23,7},{24,8},{25... | collective-permute-start | bytes 688136 | tf_op jit(solution)/shard_map/ppermute | solution.py:25
  50.6 7.4 %collective-permute-start.14 = (bf16[4,224,128]{2,1,0:T(8,128)(2,1)S(1)}, bf16[4,224,128]{2,1,0:T(8,128)(2,1)S(1)}, u32[]{:S(2)}, u32[]{:S(2)}) collective-permute-start(bf16[4,224,128]{2,1,0:T(8,128)(2,1)S(1)} %pad_maximum_fusion.1.refs_0_), channel_id=1, source_target_pairs={{2,0},{3,1},{0,2},{1,3},{6,4},{7,5},{4,6},{5,7},{10,8},{11,9},{8,1... | collective-permute-start | bytes 688136 | tf_op jit(solution)/shard_map/ppermute | solution.py:25
  51.0 7.5 %collective-permute-start.17 = (bf16[4,224,128]{2,1,0:T(8,128)(2,1)S(1)}, bf16[4,224,128]{2,1,0:T(8,128)(2,1)S(1)}, u32[]{:S(2)}, u32[]{:S(2)}) collective-permute-start(bf16[4,224,128]{2,1,0:T(8,128)(2,1)S(1)} %pad_maximum_fusion.1.refs_0_), channel_id=1, source_target_pairs={{1,0},{0,1},{3,2},{2,3},{5,4},{4,5},{7,6},{6,7},{9,8},{8,9},{11,10... | collective-permute-start | bytes 688136 | tf_op jit(solution)/shard_map/ppermute | solution.py:25
  55.8 2.7 %collective-permute-start.20 = (bf16[4,224,128]{2,1,0:T(8,128)(2,1)S(1)}, bf16[4,224,128]{2,1,0:T(8,128)(2,1)S(1)}, u32[]{:S(2)}, u32[]{:S(2)}) collective-permute-start(bf16[4,224,128]{2,1,0:T(8,128)(2,1)S(1)} %collective-permute-done.16.refs_3_), channel_id=1, source_target_pairs={{1,0},{0,1},{3,2},{2,3},{5,4},{4,5},{7,6},{6,7},{9,8},{8,9},{11,10... | collective-permute-start | bytes 688136 | tf_op jit(solution)/shard_map/ppermute | solution.py:25
  58.0 1.5 %collective-permute-start.19 = (bf16[4,224,128]{2,1,0:T(8,128)(2,1)S(1)}, bf16[4,224,128]{2,1,0:T(8,128)(2,1)S(1)}, u32[]{:S(2)}, u32[]{:S(2)}) collective-permute-start(bf16[4,224,128]{2,1,0:T(8,128)(2,1)S(1)} %collective-permute-done.15.refs_2_), channel_id=1, source_target_pairs={{1,0},{0,1},{3,2},{2,3},{5,4},{4,5},{7,6},{6,7},{9,8},{8,9},{11,10... | collective-permute-start | bytes 688136 | tf_op jit(solution)/shard_map/ppermute | solution.py:25
  58.0 1.8 %collective-permute-start.18 = (bf16[4,224,128]{2,1,0:T(8,128)(2,1)S(1)}, bf16[4,224,128]{2,1,0:T(8,128)(2,1)S(1)}, u32[]{:S(2)}, u32[]{:S(2)}) collective-permute-start(bf16[4,224,128]{2,1,0:T(8,128)(2,1)S(1)} %collective-permute-done.14.refs_1_), channel_id=1, source_target_pairs={{1,0},{0,1},{3,2},{2,3},{5,4},{4,5},{7,6},{6,7},{9,8},{8,9},{11,10... | collective-permute-start | bytes 688136 | tf_op jit(solution)/shard_map/ppermute | solution.py:25
  (1 other events, 1.2 us)
